TPU v7x, 32 devices: a whole 2x2x4 slice. The times are simulated.
32 devices in a mesh: dp: 2 (over y), seq: 16 (over z, x, core).
Axes of the slice: x: 2, y: 2, z: 4, core: 2. Of those that a mesh axis runs over, the one named last changes fastest.
Arguments:
- tokens: bfloat16 [2, 256, 128, 512], P('dp', None, 'seq'), may hold values from -6 to 6
- patch_mask: int32 [2, 256, 128], P('dp', None, 'seq'), may hold values 0 or 1
- mask_token: float32 [512], replicated, may hold values from -6 to 6
- gain: float32 [512], replicated, may hold values from 0.1 to 1.9
- w_qkv: bfloat16 [512, 1536], replicated, may hold values from -0.25 to 0.25
- w_out: bfloat16 [512, 512], replicated, may hold values from -0.25 to 0.25
- block_ids: int32 [256], replicated, may hold values from 0 to 3, as said below
- temporal_mask: int32 [8, 8], replicated, may hold values from 0 to 1, as said below
- cotangent: bfloat16 [2, 256, 128, 512], P('dp', None, 'seq'), may hold values from -6 to 6
Outputs:
- layer_out: bfloat16 [2, 256, 128, 512], P('dp', None, 'seq')
- qkv_grad: float32 [1536, 512], P('seq')
- out_grad: float32 [512, 512], P('seq')
Inputs may be any that keep to these rules, and one draw needn't show every extreme that they name: `block_ids`: each block id is held by exactly 64 electrodes. `temporal_mask`: every diagonal entry is 1.
All inputs are finite; a program needn't handle non-finite values. No bound on the sum of `patch_mask` on one device may be relied on, other than what follows from the above.
Results may differ from a plain program's by a relative error of at most 0.0092.
Values may be sent and summed in bfloat16 or wider, within the bound.
A program may use at most 128 MiB of HBM per device.

v0:
```python
import math

import jax
import jax.numpy as jnp
from jax import lax
from jax.sharding import PartitionSpec as P

P_SIZE = 128
HEADS = 8
HEAD_DIM = 64
EB = 64
TB = 16


NORM_EPS = 1e-05


def normed_input(tokens, patch_mask, mask_token, gain):
    masked = jnp.where(patch_mask[..., None] == 1, mask_token, tokens.astype(jnp.float32))
    row_mean = jnp.mean(masked, axis=-1, keepdims=True)
    centred = masked - row_mean
    spread = jnp.mean(centred * centred, axis=-1, keepdims=True)
    normed = (centred * lax.rsqrt(spread + NORM_EPS) * gain).astype(jnp.bfloat16)
    return (masked, normed)


def forward_attend(queries, key_rows, values, allowed, factor):
    scores = (
        jnp.einsum("anhd,amhd->ahnm", queries, key_rows, preferred_element_type=jnp.float32)
        * factor
    )
    exponent = jnp.exp(scores) * allowed
    weights = exponent / jnp.sum(exponent, axis=-1, keepdims=True)
    rounded = weights.astype(jnp.bfloat16)
    output = jnp.einsum(
        "ahnm,amhd->anhd", rounded, values, preferred_element_type=jnp.float32
    ).astype(jnp.bfloat16)
    return (output, weights, rounded)


def backward_attend(queries, key_rows, values, weights, rounded, grad_out, factor):
    grad_values = jnp.einsum(
        "ahnm,anhd->amhd", rounded, grad_out, preferred_element_type=jnp.float32
    ).astype(jnp.bfloat16)
    grad_weights = jnp.einsum(
        "anhd,amhd->ahnm", grad_out, values, preferred_element_type=jnp.float32
    )
    inner_sum = jnp.sum(grad_weights * weights, axis=-1, keepdims=True)
    grad_scores = (weights * (grad_weights - inner_sum)).astype(jnp.bfloat16)
    grad_queries = (
        jnp.einsum("ahnm,amhd->anhd", grad_scores, key_rows, preferred_element_type=jnp.float32)
        * factor
    ).astype(jnp.bfloat16)
    grad_keys = (
        jnp.einsum("ahnm,anhd->amhd", grad_scores, queries, preferred_element_type=jnp.float32)
        * factor
    ).astype(jnp.bfloat16)
    return (grad_queries, grad_keys, grad_values)


def to_blocks(tensor, block_order, block_size):
    record_count, electrodes, local_patches = tensor.shape[:3]
    trailing = tensor.shape[3:]
    picked = jnp.take(tensor, block_order, axis=1)
    picked = picked.reshape(
        (record_count, electrodes // block_size, block_size, local_patches) + trailing
    )
    picked = jnp.moveaxis(picked, 3, 2)
    return picked.reshape(
        (record_count * (electrodes // block_size) * local_patches, block_size) + trailing
    )


def from_blocks(tensor, inverse, record_count, electrodes, local_patches):
    block_size = tensor.shape[1]
    trailing = tensor.shape[2:]
    restored = tensor.reshape(
        (record_count, electrodes // block_size, local_patches, block_size) + trailing
    )
    restored = jnp.moveaxis(restored, 2, 3).reshape(
        (record_count, electrodes, local_patches) + trailing
    )
    return jnp.take(restored, inverse, axis=1)


def shards(tokens, patch_mask, mask_token, gain, w_qkv, w_out, block_ids, temporal_mask, cotangent):
    record_count, electrodes, local_patches, model_width = tokens.shape
    half_width = model_width // 2
    heads_half = HEADS // 2
    factor = HEAD_DIM ** (-0.5)
    block_order = jnp.argsort(block_ids, stable=True)
    inverse = jnp.argsort(block_order, stable=True)
    onehot = (jnp.arange(P_SIZE)[:, None] // TB == jnp.arange(P_SIZE // TB)[None, :]).astype(
        jnp.float32
    )
    time_allowed = jnp.dot(jnp.dot(onehot, temporal_mask.astype(jnp.float32)), onehot.T)
    same_block = jnp.ones((EB, EB), jnp.float32)
    masked, normed = normed_input(tokens, patch_mask, mask_token, gain)
    normed_flat = normed.reshape(-1, model_width)
    local_columns = 3 * model_width
    projected = jnp.dot(normed_flat, w_qkv, preferred_element_type=jnp.float32).astype(jnp.bfloat16)
    projected = projected.reshape(
        record_count, electrodes, local_patches, local_columns // half_width, heads_half, HEAD_DIM
    )
    spatial = to_blocks(projected[:, :, :, :3], block_order, EB)
    space_out, space_weights, space_rounded = forward_attend(
        spatial[:, :, 0], spatial[:, :, 1], spatial[:, :, 2], same_block, factor
    )
    time_part = projected[:, :, :, 3:].reshape(
        record_count, electrodes, local_patches, 3 * half_width
    )
    regrouped = lax.all_to_all(time_part, "seq", split_axis=1, concat_axis=2, tiled=True)
    items = regrouped.shape[0]
    owned = regrouped.shape[1]
    split_heads = regrouped.reshape(items * owned, P_SIZE, 3, heads_half, HEAD_DIM)
    time_out, time_weights, time_rounded = forward_attend(
        split_heads[:, :, 0], split_heads[:, :, 1], split_heads[:, :, 2], time_allowed, factor
    )
    time_out = time_out.reshape(items, owned, P_SIZE, half_width)
    time_back = lax.all_to_all(time_out, "seq", split_axis=2, concat_axis=1, tiled=True)
    space_back = from_blocks(space_out, inverse, record_count, electrodes, local_patches).reshape(
        record_count, electrodes, local_patches, half_width
    )
    attended = jnp.concatenate([space_back, time_back], axis=-1)
    attended_flat = attended.reshape(-1, model_width)
    layer_out = (
        masked.reshape(-1, model_width)
        + jnp.dot(attended_flat, w_out, preferred_element_type=jnp.float32)
    ).astype(jnp.bfloat16)
    layer_out = layer_out.reshape(tokens.shape)
    cot_flat = cotangent.reshape(-1, model_width)
    out_grad = jnp.einsum("tc,td->cd", cot_flat, attended_flat, preferred_element_type=jnp.float32)
    attended_grad = jnp.einsum(
        "td,cd->tc", cot_flat, w_out, preferred_element_type=jnp.float32
    ).astype(jnp.bfloat16)
    attended_grad = attended_grad.reshape(record_count, electrodes, local_patches, model_width)
    space_grad = to_blocks(
        attended_grad[..., :half_width].reshape(
            record_count, electrodes, local_patches, heads_half, HEAD_DIM
        ),
        block_order,
        EB,
    )
    space_grads = backward_attend(
        spatial[:, :, 0],
        spatial[:, :, 1],
        spatial[:, :, 2],
        space_weights,
        space_rounded,
        space_grad,
        factor,
    )
    spatial_grad = from_blocks(
        jnp.stack(space_grads, axis=2), inverse, record_count, electrodes, local_patches
    )
    spatial_grad = spatial_grad.reshape(-1, 3 * half_width)
    time_grad = lax.all_to_all(
        attended_grad[..., half_width:], "seq", split_axis=1, concat_axis=2, tiled=True
    )
    owned = time_grad.shape[1]
    split_heads = regrouped.reshape(record_count * owned, P_SIZE, 3, heads_half, HEAD_DIM)
    unused_out, time_weights, time_rounded = forward_attend(
        split_heads[:, :, 0], split_heads[:, :, 1], split_heads[:, :, 2], time_allowed, factor
    )
    time_grads = backward_attend(
        split_heads[:, :, 0],
        split_heads[:, :, 1],
        split_heads[:, :, 2],
        time_weights,
        time_rounded,
        time_grad.reshape(record_count * owned, P_SIZE, heads_half, HEAD_DIM),
        factor,
    )
    temporal_grad = jnp.stack(time_grads, axis=2).reshape(
        record_count, owned, P_SIZE, 3 * half_width
    )
    temporal_back = lax.all_to_all(
        temporal_grad, "seq", split_axis=2, concat_axis=1, tiled=True
    ).reshape(-1, 3 * half_width)
    projected_grad = jnp.concatenate([spatial_grad, temporal_back], axis=1)
    qkv_grad = jnp.einsum(
        "tc,td->cd", projected_grad, normed_flat, preferred_element_type=jnp.float32
    )
    groups = lax.axis_size("seq")
    grad_scale = 1.0 / math.sqrt(
        record_count * lax.axis_size("dp") * electrodes * local_patches * groups
    )
    rows_qkv = qkv_grad.shape[0] // groups
    rows_out = model_width // groups
    total_qkv, total_out = lax.psum((qkv_grad, out_grad), ("dp", "seq"))
    position = lax.axis_index("seq")
    share_qkv = lax.dynamic_slice_in_dim(total_qkv, position * rows_qkv, rows_qkv, 0)
    share_out = lax.dynamic_slice_in_dim(total_out, position * rows_out, rows_out, 0)
    return (layer_out, share_qkv * grad_scale, share_out * grad_scale)


def solution(mesh):
    return jax.shard_map(
        shards,
        mesh=mesh,
        in_specs=(
            P("dp", None, "seq", None),
            P("dp", None, "seq"),
            P(),
            P(),
            P(),
            P(),
            P(),
            P(),
            P("dp", None, "seq", None),
        ),
        out_specs=(P("dp", None, "seq", None), P("seq", None), P("seq", None)),
        check_vma=False,
    )
```

profile of v0, /device:TPU:0, one launch (start us, length us, event | category | flops | bytes accessed | tf_op | source)
XLA Modules:
  0.0 516.5 jit_solution(13414291428565303997)
XLA Ops:
  13.5 7.4 %all-to-all-start.2 = ((bf16[1,256,8,256]{3,2,0,1:T(8,128)(2,1)}), bf16[1,256,8,256]{3,2,0,1:T(8,128)(2,1)S(1)}, u32[]{:S(2)}, u32[]{:S(2)}) async-start(bf16[1,256,8,256]{3,2,0,1:T(8,128)(2,1)} %slice.65), calls=%async_computation.2 | async-start | bytes 2097152 | tf_op jit(solution)/shard_map/all_to_all | solution.py:157
  26.8 5.7 %convolution_convert_fusion = bf16[2048,1536]{1,0:T(8,128)(2,1)} fusion(bf16[512,1536]{1,0:T(8,128)(2,1)S(1)} %copy-done.20, bf16[1,256,8,512]{3,2,1,0:T(8,128)(2,1)S(1)} %copy-done.7, f32[512]{0:T(512)S(1)} %copy-done.22, f32[256,8]{1,0:T(8,128)S(1)} %add_rsqrt_fusion, f32[256,8]{1,0:T(8,128)S(1)} %broadcast_multiply_fusion, f32[512]{0:T(512)S(1)} %copy-done.18, ...), kind=kOutput, calls=%fused_computation.4 | convolution fusion | flops 3230662656 | bytes 9984000 | tf_op jit(solution)/shard_map/dot_general | solution.py:101
  32.5 19.5 %reshape.200 = bf16[1,256,8,6,4,64]{5,4,3,2,1,0:T(4,128)(2,1)} reshape(bf16[2048,1536]{1,0:T(8,128)(2,1)} %convolution_convert_fusion) | data formatting | bytes 12582912 | tf_op jit(solution)/shard_map/reshape | solution.py:102
  52.0 11.9 %slice_bitcast_fusion = (bf16[256,8,3,4,64]{4,3,2,1,0:T(4,128)(2,1)}, bf16[1,256,8,3,4,64]{5,4,3,2,1,0:T(4,128)(2,1)}) fusion(bf16[1,256,8,6,4,64]{5,4,3,2,1,0:T(4,128)(2,1)} %reshape.200), kind=kLoop, calls=%fused_computation.5 | loop fusion | bytes 12582912 | tf_op jit(solution)/shard_map/jit(_take)/Arg_0.11 | solution.py:64
  64.0 10.1 %copy.131 = bf16[1,256,8,3,4,64]{1,5,4,3,2,0:T(8,128)(2,1)} copy(bf16[1,256,8,3,4,64]{5,4,3,2,1,0:T(4,128)(2,1)} %get-tuple-element.24) | data formatting | bytes 6291456 | tf_op jit(solution)/shard_map/slice | solution.py:109
  74.1 5.1 copy.132
  79.2 6.2 %all-to-all-start = ((bf16[1,256,8,768]{3,2,0,1:T(8,128)(2,1)}), bf16[1,256,8,768]{3,2,0,1:T(8,128)(2,1)}, u32[]{:S(2)}, u32[]{:S(2)}) async-start(bf16[1,256,8,768]{3,2,0,1:T(8,128)(2,1)} %copy.132), calls=%async_computation | async-start | bytes 6291456 | tf_op jit(solution)/shard_map/all_to_all | solution.py:112
  103.3 4.7 copy.191
  112.2 15.2 %gather_fusion = bf16[256,8,3,4,64]{4,3,2,1,0:T(4,128)(2,1)} fusion(bf16[256,8,3,4,64]{4,3,2,1,0:T(4,128)(2,1)} %get-tuple-element.23, s32[1024]{0:T(1024)S(1)} %pad_clamp_fusion.1), kind=kCustom, calls=%fused_computation.clone | custom fusion | bytes 6292480 | tf_op jit(solution)/shard_map/jit(_take)/gather | solution.py:64
  127.5 8.5 %bitcast_select_fusion.1 = bf16[1,256,8,3,4,64]{5,4,3,2,1,0:T(4,128)(2,1)} fusion(bf16[256,8,3,4,64]{4,3,2,1,0:T(4,128)(2,1)} %gather_fusion, pred[256]{0:T(512)(128)(4,1)S(1)} %compare_and_fusion.1), kind=kLoop, calls=%fused_computation.12 | loop fusion | flops 1572864 | bytes 6291712 | tf_op jit(solution)/shard_map/jit(_take)/select_n | solution.py:64
  135.9 9.5 %copy.125 = bf16[1,4,64,8,3,4,64]{6,2,5,3,1,4,0:T(8,128)(2,1)} copy(bf16[1,4,64,8,3,4,64]{6,5,4,3,2,1,0:T(4,128)(2,1)} %bitcast.171) | data formatting | bytes 6291456 | tf_op jit(solution)/shard_map/reshape | solution.py:65
  145.8 5.5 %fusion.8 = (f32[32,4,64]{2,1,0:T(4,128)S(1)}, f32[32,4,64,64]{2,3,1,0:T(8,128)}) fusion(bf16[32,64,3,4,64]{4,1,3,0,2:T(8,128)(2,1)} %bitcast.166), kind=kOutput, calls=%fused_computation.29 | convolution fusion | flops 68149248 | bytes 6324224 | tf_op jit(solution)/shard_map/anhd,amhd->ahnm/dot_general | solution.py:29
  161.1 10.1 %reshape.206 = bf16[16,128,3,4,64]{4,3,2,1,0:T(4,128)(2,1)} reshape(bf16[1,16,16,8,768]{4,3,2,1,0:T(8,128)(2,1)} %copy.133) | data formatting | bytes 6291456 | tf_op jit(solution)/shard_map/reshape | solution.py:115
  171.2 5.8 %fusion.59 = (bf16[16,128,1,4,64]{4,3,2,1,0:T(4,128)(2,1)}, bf16[16,128,1,4,64]{4,3,2,1,0:T(4,128)(2,1)}, bf16[16,128,1,4,64]{4,3,2,1,0:T(4,128)(2,1)}) fusion(bf16[16,128,3,4,64]{4,3,2,1,0:T(4,128)(2,1)} %reshape.206), kind=kLoop, calls=%fused_computation.100 | loop fusion | bytes 6291456 | tf_op jit(solution)/shard_map/slice | solution.py:117
  195.3 6.2 %all-to-all-start.1 = ((bf16[1,16,128,256]{3,1,0,2:T(8,128)(2,1)}), bf16[1,16,128,256]{3,1,0,2:T(8,128)(2,1)}, u32[]{:S(2)}, u32[]{:S(2)}) async-start(bf16[1,16,128,256]{3,1,0,2:T(8,128)(2,1)} %copy.139), calls=%async_computation.1 | async-start | bytes 2097152 | tf_op jit(solution)/shard_map/all_to_all | solution.py:120
  214.4 5.1 copy.167
  219.5 5.0 all-to-all-done.1
  224.5 6.9 %all-to-all-start.3 = ((bf16[1,16,128,768]{3,1,0,2:T(8,128)(2,1)}), bf16[1,16,128,768]{3,1,0,2:T(8,128)(2,1)}, u32[]{:S(2)}, u32[]{:S(2)}) async-start(bf16[1,16,128,768]{3,1,0,2:T(8,128)(2,1)} %copy.167), calls=%async_computation.3 | async-start | bytes 6291456 | tf_op jit(solution)/shard_map/all_to_all | solution.py:177
  231.6 5.4 %convolution_convert_fusion.2 = bf16[32,4,64,64]{3,2,1,0:T(8,128)(2,1)} fusion(bf16[32,64,4,64]{3,1,2,0:T(8,128)(2,1)} %bitcast.189, f32[32,4,64,64]{2,3,1,0:T(8,128)} %get-tuple-element.31, f32[32,4,64]{2,1,0:T(4,128)S(1)} %get-tuple-element.30), kind=kOutput, calls=%fused_computation.53 | convolution fusion | flops 69206016 | bytes 4227072 | tf_op jit(solution)/shard_map/ahnm,anhd->amhd/dot_general | solution.py:42
  240.2 5.0 copy.156
  251.4 4.8 copy.190
  266.7 4.9 multiply_reduce_fusion.1
  290.8 9.7 %maximum_bitcast_fusion = bf16[1,4,64,8,3,4,64]{2,1,6,5,4,3,0:T(4,128)(2,1)} fusion(bf16[1,4,8,64,1,4,64]{3,1,6,5,4,2,0:T(4,128)(2,1)} %copy.156, bf16[1,4,8,64,1,4,64]{3,1,6,5,4,2,0:T(4,128)(2,1)} %copy.155, bf16[1,4,8,64,1,4,64]{3,1,6,5,4,2,0:T(4,128)(2,1)} %copy.154), kind=kLoop, calls=%fused_computation.6 | loop fusion | flops 3145728 | bytes 6291456 | tf_op jit(solution)/shard_map/transpose | solution.py:80
  300.5 11.7 %copy.194 = bf16[1,4,64,8,3,4,64]{6,3,5,4,2,1,0:T(8,128)(2,1)} copy(bf16[1,4,64,8,3,4,64]{2,1,6,5,4,3,0:T(4,128)(2,1)} %maximum_bitcast_fusion) | data formatting | bytes 6291456 | tf_op jit(solution)/shard_map/reshape | solution.py:80
  312.2 6.8 %gather_fusion.3 = bf16[256,8,3,4,64]{4,1,3,2,0:T(8,128)(2,1)} fusion(bf16[256,8,3,4,64]{4,1,3,2,0:T(8,128)(2,1)} %bitcast.172, s32[1024]{0:T(1024)S(1)} %pad_clamp_fusion), kind=kCustom, calls=%fused_computation.2.clone | custom fusion | bytes 6292480 | tf_op jit(solution)/shard_map/jit(_take)/gather | solution.py:83
  319.0 6.1 %bitcast_select_fusion = bf16[1,256,8,3,4,64]{5,2,4,3,1,0:T(8,128)(2,1)} fusion(bf16[256,8,3,4,64]{4,1,3,2,0:T(8,128)(2,1)} %gather_fusion.3, pred[256]{0:T(512)(128)(4,1)S(1)} %compare_and_fusion), kind=kLoop, calls=%fused_computation.11 | loop fusion | flops 1572864 | bytes 6291712 | tf_op jit(solution)/shard_map/jit(_take)/select_n | solution.py:83
  325.1 8.7 %copy.158 = bf16[1,256,8,3,4,64]{5,4,3,2,1,0:T(4,128)(2,1)} copy(bf16[1,256,8,3,4,64]{5,2,4,3,1,0:T(8,128)(2,1)} %bitcast_select_fusion) | data formatting | bytes 6291456 | tf_op jit(solution)/shard_map/jit(_take)/select_n | solution.py:83
  333.7 10.0 %reshape.215 = bf16[2048,768]{1,0:T(8,128)(2,1)} reshape(bf16[1,256,8,3,4,64]{5,4,3,2,1,0:T(4,128)(2,1)} %copy.158) | data formatting | bytes 6291456 | tf_op jit(solution)/shard_map/reshape | solution.py:156
  356.6 5.4 %fusion = f32[1536,512]{1,0:T(8,128)} fusion(bf16[2048,768]{1,0:T(8,128)(2,1)S(1)} %bitcast.188, bf16[2048,768]{1,0:T(8,128)(2,1)S(1)} %copy-done.11, bf16[1,256,8,512]{3,2,1,0:T(8,128)(2,1)S(1)} %copy-done.8, f32[512]{0:T(512)S(1)} %copy-done.22, f32[256,8]{1,0:T(8,128)S(1)} %copy-done.16, f32[256,8]{1,0:T(8,128)S(1)} %broadcast_multiply_fusion, ...), kind=kOutput, calls=%fused_computation.7 | convolution fusion | flops 3240099840 | bytes 11556864 | tf_op jit(solution)/shard_map/tc,td->cd/dot_general | solution.py:181
  366.1 4.4 concatenate.14
  370.5 4.7 fusion.22
  375.2 130.5 %all-reduce.3.cloned.1.call-done = (f32[1536,512]{1,0:T(8,128)}, f32[512,512]{0,1:T(8,128)}) async-done(((f32[1536,512]{1,0:T(8,128)}, f32[512,512]{0,1:T(8,128)}), (f32[1536,512]{1,0:T(8,128)}, f32[512,512]{0,1:T(8,128)})) %all-reduce.3.cloned.1.call-update) | async-done | bytes 4194320 | tf_op jit(solution)/shard_map/psum | solution.py:190
  (114 shorter events, 135.1 us)
Async XLA Ops:
  7.2 1.6 copy-start
  11.1 1.3 copy-start.12
  11.1 9.7 %copy-start.17 = (s32[1,256,8]{1,2,0:T(8,128)S(1)}, s32[1,256,8]{1,2,0:T(8,128)}, u32[]{:S(2)}) copy-start(s32[1,256,8]{1,2,0:T(8,128)} %param.14) | copy-start | bytes 24580
  11.1 9.9 %copy-start.18 = (f32[512]{0:T(512)S(1)}, f32[512]{0:T(512)}, u32[]{:S(2)}) copy-start(f32[512]{0:T(512)} %param.15) | copy-start | bytes 6148
  12.4 14.4 %copy-start.22 = (f32[512]{0:T(512)S(1)}, f32[512]{0:T(512)}, u32[]{:S(2)}) copy-start(f32[512]{0:T(512)} %param.16) | copy-start | bytes 6148
  13.5 65.7 %all-to-all-start.2 = ((bf16[1,256,8,256]{3,2,0,1:T(8,128)(2,1)}), bf16[1,256,8,256]{3,2,0,1:T(8,128)(2,1)S(1)}, u32[]{:S(2)}, u32[]{:S(2)}) async-start(bf16[1,256,8,256]{3,2,0,1:T(8,128)(2,1)} %slice.65), calls=%async_computation.2 | async-start | bytes 2097152 | tf_op jit(solution)/shard_map/all_to_all | solution.py:157
  21.0 5.8 %copy-start.7 = (bf16[1,256,8,512]{3,2,1,0:T(8,128)(2,1)S(1)}, bf16[1,256,8,512]{3,2,1,0:T(8,128)(2,1)}, u32[]{:S(2)}) copy-start(bf16[1,256,8,512]{3,2,1,0:T(8,128)(2,1)} %param.13) | copy-start | bytes 6291460
  21.1 5.8 %copy-start.20 = (bf16[512,1536]{1,0:T(8,128)(2,1)S(1)}, bf16[512,1536]{1,0:T(8,128)(2,1)}, u32[]{:S(2)}) copy-start(bf16[512,1536]{1,0:T(8,128)(2,1)} %param.17) | copy-start | bytes 4718596
  26.1 0.7 copy-start.15
  79.2 6.3 %copy-start.9 = (bf16[1,256,8,256]{3,2,0,1:T(8,128)(2,1)}, bf16[1,256,8,256]{3,2,0,1:T(8,128)(2,1)S(1)}, u32[]{:S(2)}) copy-start(bf16[1,256,8,256]{3,2,0,1:T(8,128)(2,1)S(1)} %all-to-all-done.2) | copy-start | bytes 3145732
  79.2 78.0 %all-to-all-start = ((bf16[1,256,8,768]{3,2,0,1:T(8,128)(2,1)}), bf16[1,256,8,768]{3,2,0,1:T(8,128)(2,1)}, u32[]{:S(2)}, u32[]{:S(2)}) async-start(bf16[1,256,8,768]{3,2,0,1:T(8,128)(2,1)} %copy.132), calls=%async_computation | async-start | bytes 6291456 | tf_op jit(solution)/shard_map/all_to_all | solution.py:112
  85.5 7.8 %copy-start.19 = (s32[256]{0:T(256)S(1)}, s32[256]{0:T(256)}, u32[]{:S(2)}) copy-start(s32[256]{0:T(256)} %param.19) | copy-start | bytes 3076
  135.9 9.5 %copy-start.21 = (s32[8,8]{1,0:T(8,128)S(1)}, s32[8,8]{1,0:T(8,128)}, u32[]{:S(2)}) copy-start(s32[8,8]{1,0:T(8,128)} %param.20) | copy-start | bytes 772
  145.8 5.5 %copy-start.10 = (bf16[1,256,8,256]{3,2,0,1:T(8,128)(2,1)S(1)}, bf16[1,256,8,256]{3,2,0,1:T(8,128)(2,1)}, u32[]{:S(2)}) copy-start(bf16[1,256,8,256]{3,2,0,1:T(8,128)(2,1)} %copy-done.9) | copy-start | bytes 3145732
  187.6 2.5 copy-start.14
  190.2 2.4 copy-start.4
  195.3 29.2 %all-to-all-start.1 = ((bf16[1,16,128,256]{3,1,0,2:T(8,128)(2,1)}), bf16[1,16,128,256]{3,1,0,2:T(8,128)(2,1)}, u32[]{:S(2)}, u32[]{:S(2)}) async-start(bf16[1,16,128,256]{3,1,0,2:T(8,128)(2,1)} %copy.139), calls=%async_computation.1 | async-start | bytes 2097152 | tf_op jit(solution)/shard_map/all_to_all | solution.py:120
  201.5 4.5 copy-start.5
  207.3 1.6 copy-start.6
  207.3 2.3 copy-start.13
  224.5 126.7 %all-to-all-start.3 = ((bf16[1,16,128,768]{3,1,0,2:T(8,128)(2,1)}), bf16[1,16,128,768]{3,1,0,2:T(8,128)(2,1)}, u32[]{:S(2)}, u32[]{:S(2)}) async-start(bf16[1,16,128,768]{3,1,0,2:T(8,128)(2,1)} %copy.167), calls=%async_computation.3 | async-start | bytes 6291456 | tf_op jit(solution)/shard_map/all_to_all | solution.py:177
  231.4 274.3 %all-reduce.3.cloned.1.call-start = ((), (), s32[]{:S(2)}) async-start(), calls=%async_computation.4 | async-start | bytes 8388608 | tf_op jit(solution)/shard_map/psum | solution.py:190
  240.2 5.0 copy-start.2
  266.7 4.9 copy-start.3
  272.9 1.3 copy-start.1
  354.1 1.6 copy-start.8
  354.1 2.5 copy-start.11
  354.1 2.5 copy-start.16
Sparse Core Ops, SparseCore 0:
  362.1 143.5 all-reduce.2
where the time goes:
time: 525 us; the launch traced here: 517 us
  local copies, waits for them, and re-layouts  229 us (44%)
  waiting for transfers between devices  136 us (26%)
  matrix products  62.3 us (12%)
  other arithmetic  47.6 us (9%)
  starting transfers between devices  26.9 us (5%)
  between operations  15 us (3%)
    psum x1, waiting for transfers between devices, shards(): total_qkv, total_out = lax.psum((qkv_grad, out_grad), ('dp', 'seq'))  131 us
    unnamed x51, local copies, waits for them, and re-layouts  20.1 us
    reshape x1, local copies, waits for them, and re-layouts, shards(): projected.reshape(record_count, electrodes, local_patches, local_columns...  19.5 us
    gather x2, local copies, waits for them, and re-layouts, to_blocks(): picked = jnp.take(tensor, block_order, axis=1)  19 us
    reshape x2, local copies, waits for them, and re-layouts, from_blocks(): jnp.moveaxis(restored, 2, 3)  16.5 us
    select_n x3, local copies, waits for them, and re-layouts, from_blocks(): return jnp.take(restored, inverse, axis=1)  16.3 us
    reshape x2, local copies, waits for them, and re-layouts, to_blocks(): picked.reshape((record_count, electrodes // block_size, block_size, local...  14.2 us
    another operation x3, local copies, waits for them, and re-layouts, shards(): jnp.stack(space_grads, axis=2)  13.6 us
  transfers between devices with their start and end apart: 5, of which 2 were waited for; matrix products, arithmetic and copies ran while one was open for 54% of the time, Pallas kernels for 0%

commit v1 on v0

v1 whole, which is shorter than its diff:
```python
import functools
import math

import jax
import jax.numpy as jnp
from jax import lax
from jax.experimental import pallas as pl
from jax.experimental.pallas import tpu as pltpu
from jax.sharding import PartitionSpec as P

HEADS = 8
HEAD_DIM = 64
NORM_EPS = 1e-05
LANES = 128
F32 = jnp.float32
BF16 = jnp.bfloat16
VMEM_BYTES = 48 * 1024 * 1024


def dot(a, b, ca=1, cb=0):
    return lax.dot_general(a, b, (((ca,), (cb,)), ((), ())), preferred_element_type=F32)


def params():
    return pltpu.CompilerParams(vmem_limit_bytes=VMEM_BYTES)


def full(shape):
    return pl.BlockSpec(shape, lambda i: (0,) * len(shape))


def rows_of(rows, columns):
    return pl.BlockSpec((rows, columns), lambda i: (i, 0))


def scatter_rows(scratch, value, rows=slice(None)):
    for c in range(scratch.shape[0]):
        scratch[c, rows, :] = value[:, c * LANES : (c + 1) * LANES].astype(F32)


def gather_rows(scratch, rows):
    return jnp.concatenate(
        [scratch[c, rows, :] for c in range(scratch.shape[0])], axis=1
    )


def masked_rows(tokens, mask, mask_token):
    return jnp.where(mask == 1.0, mask_token, tokens.astype(F32))


def attention_weights(q, k, allowed):
    scores = dot(q, k, 1, 1) * (HEAD_DIM**-0.5)
    exponent = jnp.where(allowed, jnp.exp(scores), 0.0)
    return exponent / jnp.sum(exponent, axis=-1, keepdims=True)


def attention_grads(q, k, v, g, weights, rounded):
    factor = HEAD_DIM**-0.5
    grad_v = dot(rounded, g, 0, 0).astype(BF16)
    grad_w = dot(g, v, 1, 1)
    inner = jnp.sum(grad_w * weights, axis=-1, keepdims=True)
    grad_s = (weights * (grad_w - inner)).astype(BF16)
    grad_q = (dot(grad_s, k) * factor).astype(BF16)
    grad_k = (dot(grad_s, q, 0, 0) * factor).astype(BF16)
    return grad_q, grad_k, grad_v


def head_columns(qkv, h, half):
    at = h * HEAD_DIM
    return [qkv[:, part * half + at : part * half + at + HEAD_DIM] for part in range(3)]


def prepare_kernel(tokens, mask, mask_token, gain, w_out, cot, send, grad_space):
    width = tokens.shape[1]
    half = width // 2
    masked = masked_rows(tokens[...], mask[...], mask_token[...])
    centred = masked - jnp.mean(masked, axis=-1, keepdims=True)
    spread = jnp.mean(centred * centred, axis=-1, keepdims=True)
    send[:, :width] = (centred * lax.rsqrt(spread + NORM_EPS) * gain[...]).astype(BF16)
    grad = dot(cot[...], w_out[...], 1, 1).astype(BF16)
    send[:, width:] = grad[:, half:]
    grad_space[...] = grad[:, :half]


def space_kernel(
    patches, normed, grad, cot, w, id_col, id_row, out, qkv_grad, out_grad,
    n_scr, g_scr, c_scr, o_scr, q_acc, o_acc,
):
    p = pl.program_id(0)
    rows = normed.shape[0]
    half = grad.shape[1]
    electrodes = id_col.shape[0]

    @pl.when(p == 0)
    def _():
        scatter_rows(n_scr, normed[...])
        scatter_rows(g_scr, grad[...])
        scatter_rows(c_scr, cot[...])
        q_acc[...] = jnp.zeros_like(q_acc)
        o_acc[...] = jnp.zeros_like(o_acc)

    mine = pl.ds(p, electrodes, stride=patches)
    n = gather_rows(n_scr, mine).astype(BF16)
    g = gather_rows(g_scr, mine).astype(BF16)
    c = gather_rows(c_scr, mine).astype(BF16)
    allowed = id_col[...] == id_row[...]
    qkv = dot(n, w[...]).astype(BF16)
    outs, grads = [], [[], [], []]
    for h in range(half // HEAD_DIM):
        q, k, v = head_columns(qkv, h, half)
        gh = g[:, h * HEAD_DIM : (h + 1) * HEAD_DIM]
        weights = attention_weights(q, k, allowed)
        rounded = weights.astype(BF16)
        outs.append(dot(rounded, v).astype(BF16))
        for part, value in zip(grads, attention_grads(q, k, v, gh, weights, rounded)):
            part.append(value)
    o = jnp.concatenate(outs, axis=1)
    scatter_rows(o_scr, o, mine)
    projected_grad = jnp.concatenate(grads[0] + grads[1] + grads[2], axis=1)
    q_acc[...] += dot(projected_grad, n, 0, 0)
    o_acc[...] += dot(c, o, 0, 0)

    @pl.when(p == patches - 1)
    def _():
        out[...] = gather_rows(o_scr, slice(None)).astype(BF16)
        qkv_grad[...] = q_acc[...].astype(BF16)
        out_grad[...] = o_acc[...].astype(BF16)


def time_forward_kernel(owned, local, direct, recv, w, allowed, out, normed, grad, qkv, scr, o_scr):
    width = normed.shape[1]
    half = grad.shape[1]
    steps = owned * local
    groups = recv.shape[0] // steps
    length = groups * local
    if direct:
        for s in range(groups):
            block = recv[s * steps : (s + 1) * steps, :].astype(F32)
            scr[:, s * local : (s + 1) * local, :] = block.reshape(owned, local, width + half)
    may = allowed[...] > 0.0

    @pl.loop(0, owned)
    def _(e):
        at = pl.ds(pl.multiple_of(e * length, length), length)
        if direct:
            block = scr[e].astype(BF16)
        else:
            block = recv[at, :]
        n = block[:, :width]
        normed[at, :] = n
        grad[at, :] = block[:, width:]
        mine = dot(n, w[...]).astype(BF16)
        qkv[at, :] = mine
        outs = []
        for h in range(half // HEAD_DIM):
            q, k, v = head_columns(mine, h, half)
            rounded = attention_weights(q, k, may).astype(BF16)
            outs.append(dot(rounded, v).astype(BF16))
        o = jnp.concatenate(outs, axis=1)
        if direct:
            o_scr[e] = o.astype(F32)
        else:
            out[at, :] = o

    if direct:
        for s in range(groups):
            block = o_scr[:, s * local : (s + 1) * local, :]
            out[s * steps : (s + 1) * steps, :] = block.reshape(steps, half).astype(BF16)


def time_backward_kernel(length, normed, grad, qkv, allowed, qkv_grad, acc):
    i = pl.program_id(0)
    half = grad.shape[1]
    may = allowed[...] > 0.0

    @pl.when(i == 0)
    def _():
        acc[...] = jnp.zeros_like(acc)

    both = []
    for e in range(normed.shape[0] // length):
        at = slice(e * length, (e + 1) * length)
        mine, g = qkv[at, :], grad[at, :]
        grads = [[], [], []]
        for h in range(half // HEAD_DIM):
            q, k, v = head_columns(mine, h, half)
            gh = g[:, h * HEAD_DIM : (h + 1) * HEAD_DIM]
            weights = attention_weights(q, k, may)
            found = attention_grads(q, k, v, gh, weights, weights.astype(BF16))
            for part, value in zip(grads, found):
                part.append(value)
        both.append(jnp.concatenate(grads[0] + grads[1] + grads[2], axis=1))
    acc[...] += dot(jnp.concatenate(both, axis=0), normed[...], 0, 0)

    @pl.when(i == pl.num_programs(0) - 1)
    def _():
        qkv_grad[...] = acc[...].astype(BF16)


def finish_kernel(tokens, mask, mask_token, space, time, w_out, cot, layer_out, out_grad, acc):
    i = pl.program_id(0)

    @pl.when(i == 0)
    def _():
        acc[...] = jnp.zeros_like(acc)

    t = time[...]
    attended = jnp.concatenate([space[...], t], axis=1)
    masked = masked_rows(tokens[...], mask[...], mask_token[...])
    layer_out[...] = (masked + dot(attended, w_out[...])).astype(BF16)
    acc[...] += dot(cot[...], t, 0, 0)

    @pl.when(i == pl.num_programs(0) - 1)
    def _():
        out_grad[...] = acc[...].astype(BF16)


def shape(rows, columns, kind=BF16):
    return jax.ShapeDtypeStruct((rows, columns), kind)


def sum_shares(terms):
    total = terms[0].astype(F32)
    for s in range(1, terms.shape[0]):
        total = total + terms[s].astype(F32)
    return total


def reduce_parts(parts, parts_out, scale):
    def exchange(value, groups):
        value = value.reshape(groups, value.shape[0] // groups, value.shape[1])
        return sum_shares(lax.all_to_all(value, "seq", split_axis=0, concat_axis=0))

    groups = lax.axis_size("seq")
    totals = [exchange(value, groups) for value in (parts, parts_out)]
    cut = totals[0].shape[0]
    total = jnp.concatenate(totals, axis=0).astype(BF16)
    copies = lax.axis_size("dp")
    if copies == 2:
        other = lax.ppermute(total, "dp", [(0, 1), (1, 0)])
        whole = total.astype(F32) + other.astype(F32)
    else:
        whole = sum_shares(lax.all_gather(total, "dp"))
    whole = whole * scale
    return whole[:cut], whole[cut:]


def shards(tokens, patch_mask, mask_token, gain, w_qkv, w_out, block_ids, temporal_mask, cotangent):
    record_count, electrodes, local, width = tokens.shape
    half = width // 2
    groups = lax.axis_size("seq")
    owned = electrodes // groups
    length = groups * local
    count = electrodes * local
    tile = min(256, count)
    steps = count // tile
    tokens_flat = tokens.reshape(count, width)
    cot = cotangent.reshape(count, width)
    mask = patch_mask.reshape(count, 1).astype(F32)
    mask_token = mask_token.reshape(1, width)
    gain = gain.reshape(1, width)
    ids = block_ids.astype(F32)
    blocks = temporal_mask.shape[0]
    onehot = (
        jnp.arange(length)[:, None] // (length // blocks) == jnp.arange(blocks)[None, :]
    ).astype(F32)
    allowed = jnp.dot(jnp.dot(onehot, temporal_mask.astype(F32)), onehot.T)

    send, grad_space = pl.pallas_call(
        prepare_kernel,
        grid=(steps,),
        in_specs=[
            rows_of(tile, width), rows_of(tile, 1), full((1, width)), full((1, width)),
            full((width, width)), rows_of(tile, width),
        ],
        out_specs=[rows_of(tile, width + half), rows_of(tile, half)],
        out_shape=[shape(count, width + half), shape(count, half)],
        compiler_params=params(),
        cost_estimate=pl.CostEstimate(
            flops=2 * count * width * width, bytes_accessed=9 * count * width, transcendentals=0
        ),
    )(tokens_flat, mask, mask_token, gain, w_out, cot)

    direct = local % 8 == 0
    recv = lax.all_to_all(
        send.reshape(groups, owned, local, width + half), "seq", split_axis=0, concat_axis=0
    )
    if not direct:
        recv = jnp.swapaxes(recv, 0, 1)
    recv = recv.reshape(count, width + half)

    space_out, grad_qkv_space, grad_out_space = pl.pallas_call(
        functools.partial(space_kernel, local),
        grid=(local,),
        in_specs=[
            full((count, width)), full((count, half)), full((count, width)),
            full((width, 3 * half)), full((electrodes, 1)), full((1, electrodes)),
        ],
        out_specs=[full((count, half)), full((3 * half, width)), full((width, half))],
        out_shape=[shape(count, half), shape(3 * half, width), shape(width, half)],
        scratch_shapes=[
            pltpu.VMEM((width // LANES, count, LANES), F32),
            pltpu.VMEM((half // LANES, count, LANES), F32),
            pltpu.VMEM((width // LANES, count, LANES), F32),
            pltpu.VMEM((half // LANES, count, LANES), F32),
            pltpu.VMEM((3 * half, width), F32),
            pltpu.VMEM((width, half), F32),
        ],
        compiler_params=params(),
        cost_estimate=pl.CostEstimate(
            flops=32 * count * width * width, bytes_accessed=8 * count * width, transcendentals=0
        ),
    )(send, grad_space, cot, w_qkv, ids.reshape(electrodes, 1), ids.reshape(1, electrodes))

    time_out, normed_time, grad_time, qkv_time = pl.pallas_call(
        functools.partial(time_forward_kernel, owned, local, direct),
        grid=(1,),
        in_specs=[
            full((count, width + half)),
            pl.BlockSpec((width, 3 * half), lambda i: (0, 1)),
            full((length, length)),
        ],
        out_specs=[
            full((count, half)), full((count, width)), full((count, half)), full((count, 3 * half)),
        ],
        out_shape=[
            shape(count, half), shape(count, width), shape(count, half), shape(count, 3 * half),
        ],
        scratch_shapes=[
            pltpu.VMEM((owned, length, width + half), F32),
            pltpu.VMEM((owned, length, half), F32),
        ],
        compiler_params=params(),
        cost_estimate=pl.CostEstimate(
            flops=6 * count * width * width, bytes_accessed=8 * count * width, transcendentals=0
        ),
    )(recv, w_qkv, allowed)

    if direct:
        back = time_out.reshape(groups, owned, local, half)
    else:
        back = jnp.swapaxes(time_out.reshape(owned, groups, local, half), 0, 1)
    time_back = lax.all_to_all(back, "seq", split_axis=0, concat_axis=0).reshape(count, half)

    pair = 2 * length if owned % 2 == 0 else length
    grad_qkv_time = pl.pallas_call(
        functools.partial(time_backward_kernel, length),
        grid=(count // pair,),
        in_specs=[
            rows_of(pair, width), rows_of(pair, half), rows_of(pair, 3 * half),
            full((length, length)),
        ],
        out_specs=full((3 * half, width)),
        out_shape=shape(3 * half, width),
        scratch_shapes=[pltpu.VMEM((3 * half, width), F32)],
        compiler_params=params(),
        cost_estimate=pl.CostEstimate(
            flops=16 * count * width * width, bytes_accessed=8 * count * width, transcendentals=0
        ),
    )(normed_time, grad_time, qkv_time, allowed)

    layer_out, grad_out_time = pl.pallas_call(
        finish_kernel,
        grid=(steps,),
        in_specs=[
            rows_of(tile, width), rows_of(tile, 1), full((1, width)), rows_of(tile, half),
            rows_of(tile, half), full((width, width)), rows_of(tile, width),
        ],
        out_specs=[rows_of(tile, width), full((width, half))],
        out_shape=[shape(count, width), shape(width, half)],
        scratch_shapes=[pltpu.VMEM((width, half), F32)],
        compiler_params=params(),
        cost_estimate=pl.CostEstimate(
            flops=4 * count * width * width, bytes_accessed=8 * count * width, transcendentals=0
        ),
    )(tokens_flat, mask, mask_token, space_out, time_back, w_out, cot)

    grad_qkv = jnp.concatenate([grad_qkv_space, grad_qkv_time], axis=0)
    grad_out = jnp.concatenate([grad_out_space, grad_out_time], axis=1)
    scale = 1.0 / math.sqrt(record_count * lax.axis_size("dp") * electrodes * length)
    share_qkv, share_out = reduce_parts(grad_qkv, grad_out, scale)
    return layer_out.reshape(tokens.shape), share_qkv, share_out


def solution(mesh):
    return jax.shard_map(
        shards,
        mesh=mesh,
        in_specs=(
            P("dp", None, "seq", None),
            P("dp", None, "seq"),
            P(),
            P(),
            P(),
            P(),
            P(),
            P(),
            P("dp", None, "seq", None),
        ),
        out_specs=(P("dp", None, "seq", None), P("seq", None), P("seq", None)),
        check_vma=False,
    )
```

time: 525 us -> 258 us (0.49)
  local copies, waits for them, and re-layouts: 229 us -> 17.6 us
  Pallas kernels: 0 us -> 100 us
  matrix products: 62.3 us -> 0.31 us
  other arithmetic: 47.6 us -> 3.15 us
  waiting for transfers between devices: 136 us -> 95.6 us
  between operations: 15 us -> 0.85 us
  starting transfers between devices: 26.9 us -> 36.7 us
    psum x1 -> x0, waiting for transfers between devices: 131 us -> none  [shards(): total_qkv, total_out = lax.psum((qkv_grad, out_grad), ('dp', 'seq'))]
    pallas_call x0 -> x5, Pallas kernels: none -> 100 us  [the longest x1 33.4 us: shards(): pl.pallas_call(functools.partial(space_kernel, local), grid=(local,), in_...]
    reshape x14 -> x1, local copies, waits for them, and re-layouts: 96 us -> 0.13 us  [shards(): ids.reshape(electrodes, 1)]
    all_to_all x4, waiting for transfers between devices: 5.01 us -> 91 us  [the longest x1 59.1 us: shards(): lax.all_to_all(send.reshape(groups, owned, local, width + half), 'seq', s...]
    dot_general x18 -> x1, matrix products: 62.3 us -> 0.31 us  [shards(): allowed = jnp.dot(jnp.dot(onehot, temporal_mask.astype(F32)), onehot.T)]
    gather x4 -> x0, local copies, waits for them, and re-layouts: 29.6 us -> none  [the longest x2 19 us: to_blocks(): picked = jnp.take(tensor, block_order, axis=1)]
    another operation x5 -> x0, local copies, waits for them, and re-layouts: 28.4 us -> none  [the longest x3 13.6 us: shards(): jnp.stack(space_grads, axis=2)]
    select_n x7 -> x1, other arithmetic: 20.8 us -> 0.01 us  [shards(): jnp.arange(length)[:, None] // (length // blocks)]
  transfers between devices with their start and end apart: 5 -> 5, of which waited for: 2 -> 3; matrix products, arithmetic and copies ran while one was open for 54% -> 1% of each run, Pallas kernels for 0% -> 25%
where the time goes in v1:
time: 258 us; the launch traced here: 254 us
  Pallas kernels  100 us (39%)
  waiting for transfers between devices  95.6 us (37%)
  starting transfers between devices  36.7 us (14%)
  local copies, waits for them, and re-layouts  17.6 us (7%)
  other arithmetic  3.15 us (1%)
    all_to_all x1, waiting for transfers between devices, shards(): lax.all_to_all(send.reshape(groups, owned, local, width + half), 'seq', s...  59.1 us
    pallas_call x1, Pallas kernels, shards(): pl.pallas_call(functools.partial(space_kernel, local), grid=(local,), in_...  33.4 us
    all_to_all x2, waiting for transfers between devices, exchange(): return sum_shares(lax.all_to_all(value, 'seq', split_axis=0, concat_axis=0))  31.9 us
    pallas_call x1, Pallas kernels, shards(): pl.pallas_call(functools.partial(time_backward_kernel, length), grid=(cou...  29.2 us
    pallas_call x1, Pallas kernels, shards(): pl.pallas_call(functools.partial(time_forward_kernel, owned, local, direc...  23 us
    unnamed x46, local copies, waits for them, and re-layouts  15.7 us
    all_to_all x1, starting transfers between devices, shards(): lax.all_to_all(back, 'seq', split_axis=0, concat_axis=0)  15.6 us
    all_to_all x2, starting transfers between devices, exchange(): return sum_shares(lax.all_to_all(value, 'seq', split_axis=0, concat_axis=0))  12 us
  transfers between devices with their start and end apart: 5, of which 3 were waited for; matrix products, arithmetic and copies ran while one was open for 1% of the time, Pallas kernels for 25%

profile of v1, /device:TPU:0, one launch (start us, length us, event | category | flops | bytes accessed | tf_op | source)
XLA Modules:
  0.0 254.4 jit_solution(11954405173679637101)
XLA Ops:
  0.6 0.7 convert_element_type.195
  1.8 1.6 copy-done
  3.4 1.0 copy-done.4
  4.4 0.7 copy-done.6
  5.1 0.7 copy-done.7
  5.8 7.2 %shard_map.112 = (bf16[2048,768]{1,0:T(8,128)(2,1)}, bf16[2048,256]{1,0:T(8,128)(2,1)S(1)}) custom-call(bf16[2048,512]{1,0:T(8,128)(2,1)S(1)} %bitcast.27, f32[2048,1]{1,0:T(8,128)S(1)} %convert_element_type.281.mask, f32[1,512]{1,0:T(1,128)S(1)} %bitcast.32, f32[1,512]{1,0:T(1,128)S(1)} %bitcast.31, bf16[512,512]{1,0:T(8,128)(2,1)S(1)} %copy-done.4, ...), custom_call_target="tpu_custom_call" | custom-call | flops 1073741824 | bytes 9437184 | tf_op jit(solution)/shard_map/pallas_call | solution.py:269
  13.0 1.0 copy-done.11
  13.9 7.5 %all-to-all-start = ((bf16[16,16,8,768]{3,2,1,0:T(8,128)(2,1)}), bf16[16,16,8,768]{3,2,1,0:T(8,128)(2,1)}, u32[]{:S(2)}, u32[]{:S(2)}) async-start(bf16[16,16,8,768]{3,2,1,0:T(8,128)(2,1)} %bitcast.34), calls=%async_computation | async-start | bytes 6291456 | tf_op jit(solution)/shard_map/all_to_all | solution.py:285
  21.8 59.1 %all-to-all-done = bf16[16,16,8,768]{3,2,1,0:T(8,128)(2,1)} async-done(((bf16[16,16,8,768]{3,2,1,0:T(8,128)(2,1)}), bf16[16,16,8,768]{3,2,1,0:T(8,128)(2,1)}, u32[]{:S(2)}, u32[]{:S(2)}) %all-to-all-start) | async-done | bytes 3145760 | tf_op jit(solution)/shard_map/all_to_all | solution.py:285
  80.9 23.0 %shard_map.114 = (bf16[2048,256]{1,0:T(8,128)(2,1)}, bf16[2048,512]{1,0:T(8,128)(2,1)S(1)}, bf16[2048,256]{1,0:T(8,128)(2,1)S(1)}, bf16[2048,768]{1,0:T(8,128)(2,1)}) custom-call(bf16[2048,768]{1,0:T(8,128)(2,1)} %bitcast.7.recv, bf16[512,1536]{1,0:T(8,128)(2,1)S(1)} %copy-done.9, f32[128,128]{1,0:T(8,128)S(1)} %fusion.allowed), custom_call_target="tpu_custom_call" | custom-call | flops 3221225472 | bytes 8388608 | tf_op jit(solution)/shard_map/pallas_call | solution.py:315
  104.0 1.4 copy-done.17
  105.3 1.0 copy-done.19
  106.4 15.6 %all-to-all-start.1 = ((bf16[16,16,8,256]{3,2,1,0:T(8,128)(2,1)}), bf16[16,16,8,256]{3,2,1,0:T(8,128)(2,1)}, u32[]{:S(2)}, u32[]{:S(2)}) async-start(bf16[16,16,8,256]{3,2,1,0:T(8,128)(2,1)} %bitcast.8), calls=%async_computation.1 | async-start | bytes 2097152 | tf_op jit(solution)/shard_map/all_to_all | solution.py:343
  122.2 1.4 copy-done.10
  123.6 1.2 copy-done.12
  124.8 33.4 %shard_map.113 = (bf16[2048,256]{1,0:T(8,128)(2,1)S(1)}, bf16[768,512]{1,0:T(8,128)(2,1)S(1)}, bf16[512,256]{1,0:T(8,128)(2,1)S(1)}) custom-call(bf16[2048,768]{1,0:T(8,128)(2,1)} %get-tuple-element.14.normed, bf16[2048,256]{1,0:T(8,128)(2,1)S(1)} %copy-done.12, bf16[2048,512]{1,0:T(8,128)(2,1)} %bitcast.36, bf16[512,1536]{1,0:T(8,128)(2,1)S(1)} %copy-done.10, ...), custom_call_target="tpu_custom_call" | custom-call | flops 17179869184 | bytes 8388608 | tf_op jit(solution)/shard_map/pallas_call | solution.py:292
  158.2 0.9 copy-done.2
  159.1 1.0 copy-done.13
  160.1 1.0 copy-done.5
  161.1 1.2 copy-done.14
  162.3 7.4 %shard_map.115 = (bf16[2048,512]{1,0:T(8,128)(2,1)}, bf16[512,256]{1,0:T(8,128)(2,1)S(1)}) custom-call(bf16[2048,512]{1,0:T(8,128)(2,1)S(1)} %bitcast.28, f32[2048,1]{1,0:T(8,128)S(1)} %convert_element_type.281.mask, f32[1,512]{1,0:T(1,128)S(1)} %bitcast.33, bf16[2048,256]{1,0:T(8,128)(2,1)S(1)} %copy-done.14, bf16[2048,256]{1,0:T(8,128)(2,1)} %bitcast.9.time, ...), custom_call_target="tpu_custom_call" | custom-call | flops 2147483648 | bytes 8388608 | tf_op jit(solution)/shard_map/pallas_call | solution.py:362
  169.7 0.8 pad_maximum_fusion.1
  170.5 6.0 %all-to-all-start.3 = ((bf16[16,32,512]{2,1,0:T(8,128)(2,1)}), bf16[16,32,512]{2,1,0:T(8,128)(2,1)S(1)}, u32[]{:S(2)}, u32[]{:S(2)}) async-start(bf16[16,32,512]{2,1,0:T(8,128)(2,1)} %bitcast.14), calls=%async_computation.3 | async-start | bytes 1048576 | tf_op jit(solution)/shard_map/all_to_all | solution.py:232
  176.5 1.6 copy-done.18
  178.1 29.2 %shard_map.116 = bf16[768,512]{1,0:T(8,128)(2,1)S(1)} custom-call(bf16[2048,512]{1,0:T(8,128)(2,1)S(1)} %copy-done.18, bf16[2048,256]{1,0:T(8,128)(2,1)S(1)} %copy-done.20, bf16[2048,768]{1,0:T(8,128)(2,1)} %get-tuple-element.22.qkv, f32[128,128]{1,0:T(8,128)S(1)} %copy-done.16), custom_call_target="tpu_custom_call" | custom-call | flops 8589934592 | bytes 8388608 | tf_op jit(solution)/shard_map/pallas_call | solution.py:346
  207.3 1.3 pad_maximum_fusion
  208.6 6.0 %all-to-all-start.2 = ((bf16[16,96,512]{2,1,0:T(8,128)(2,1)}), bf16[16,96,512]{2,1,0:T(8,128)(2,1)S(1)}, u32[]{:S(2)}, u32[]{:S(2)}) async-start(bf16[16,96,512]{2,1,0:T(8,128)(2,1)} %bitcast.11), calls=%async_computation.2 | async-start | bytes 3145728 | tf_op jit(solution)/shard_map/all_to_all | solution.py:232
  214.7 31.9 %all-to-all-done.2 = bf16[16,96,512]{2,1,0:T(8,128)(2,1)S(1)} async-done(((bf16[16,96,512]{2,1,0:T(8,128)(2,1)}), bf16[16,96,512]{2,1,0:T(8,128)(2,1)S(1)}, u32[]{:S(2)}, u32[]{:S(2)}) %all-to-all-start.2) | async-done | bytes 1572896 | tf_op jit(solution)/shard_map/all_to_all | solution.py:232
  246.8 1.6 collective-permute-start
  248.4 4.7 %collective-permute-done = bf16[128,512]{1,0:T(8,128)(2,1)S(1)} collective-permute-done((bf16[128,512]{1,0:T(8,128)(2,1)S(1)}, bf16[128,512]{1,0:T(8,128)(2,1)S(1)}, u32[]{:S(2)}, u32[]{:S(2)}) %collective-permute-start) | collective-permute-done | bytes 131104 | tf_op jit(solution)/shard_map/ppermute | solution.py:240
  253.1 0.6 slice.169
  253.8 0.7 slice.168
  (44 shorter events, 1.3 us)
Async XLA Ops:
  1.8 1.6 copy-start
  3.4 1.0 copy-start.4
  4.4 0.7 copy-start.6
  5.1 0.7 copy-start.7
  13.0 1.0 copy-start.11
  13.9 7.6 %copy-start.22 = (s32[8,8]{1,0:T(8,128)S(1)}, s32[8,8]{1,0:T(8,128)}, u32[]{:S(2)}) copy-start(s32[8,8]{1,0:T(8,128)} %param.16) | copy-start | bytes 772
  13.9 67.0 %copy-start.9 = (bf16[512,1536]{1,0:T(8,128)(2,1)S(1)}, bf16[512,1536]{1,0:T(8,128)(2,1)}, u32[]{:S(2)}) copy-start(bf16[512,1536]{1,0:T(8,128)(2,1)} %w.3) | copy-start | bytes 4718596
  13.9 67.0 %all-to-all-start = ((bf16[16,16,8,768]{3,2,1,0:T(8,128)(2,1)}), bf16[16,16,8,768]{3,2,1,0:T(8,128)(2,1)}, u32[]{:S(2)}, u32[]{:S(2)}) async-start(bf16[16,16,8,768]{3,2,1,0:T(8,128)(2,1)} %bitcast.34), calls=%async_computation | async-start | bytes 6291456 | tf_op jit(solution)/shard_map/all_to_all | solution.py:285
  21.8 82.1 %copy-start.15 = (f32[128,128]{1,0:T(8,128)}, f32[128,128]{1,0:T(8,128)S(1)}, u32[]{:S(2)}) copy-start(f32[128,128]{1,0:T(8,128)S(1)} %fusion.allowed) | copy-start | bytes 196612
  104.0 1.4 copy-start.17
  105.3 1.0 copy-start.19
  106.4 15.6 %copy-start.21 = (s32[256]{0:T(256)S(1)}, s32[256]{0:T(256)}, u32[]{:S(2)}) copy-start(s32[256]{0:T(256)} %param.15) | copy-start | bytes 3076
  106.4 53.7 %all-to-all-start.1 = ((bf16[16,16,8,256]{3,2,1,0:T(8,128)(2,1)}), bf16[16,16,8,256]{3,2,1,0:T(8,128)(2,1)}, u32[]{:S(2)}, u32[]{:S(2)}) async-start(bf16[16,16,8,256]{3,2,1,0:T(8,128)(2,1)} %bitcast.8), calls=%async_computation.1 | async-start | bytes 2097152 | tf_op jit(solution)/shard_map/all_to_all | solution.py:343
  122.2 1.4 copy-start.10
  123.6 1.2 copy-start.12
  124.8 35.2 %copy-start.1 = (bf16[1,256,8,512]{3,2,1,0:T(8,128)(2,1)S(1)}, bf16[1,256,8,512]{3,2,1,0:T(8,128)(2,1)}, u32[]{:S(2)}) copy-start(bf16[1,256,8,512]{3,2,1,0:T(8,128)(2,1)} %param.9) | copy-start | bytes 6291460
  124.8 35.2 %copy-start.8 = (f32[512]{0:T(512)S(1)}, f32[512]{0:T(512)}, u32[]{:S(2)}) copy-start(f32[512]{0:T(512)} %param.11) | copy-start | bytes 6148
  158.2 0.9 copy-start.2
  159.1 1.0 copy-start.13
  160.0 1.0 copy-start.5
  161.1 1.2 copy-start.14
  169.7 6.8 %copy-start.16 = (f32[128,128]{1,0:T(8,128)S(1)}, f32[128,128]{1,0:T(8,128)}, u32[]{:S(2)}) copy-start(f32[128,128]{1,0:T(8,128)} %copy-done.15) | copy-start | bytes 196612
  169.7 6.8 %copy-start.20 = (bf16[2048,256]{1,0:T(8,128)(2,1)S(1)}, bf16[2048,256]{1,0:T(8,128)(2,1)}, u32[]{:S(2)}) copy-start(bf16[2048,256]{1,0:T(8,128)(2,1)} %copy-done.19) | copy-start | bytes 3145732
  170.5 38.1 %all-to-all-start.3 = ((bf16[16,32,512]{2,1,0:T(8,128)(2,1)}), bf16[16,32,512]{2,1,0:T(8,128)(2,1)S(1)}, u32[]{:S(2)}, u32[]{:S(2)}) async-start(bf16[16,32,512]{2,1,0:T(8,128)(2,1)} %bitcast.14), calls=%async_computation.3 | async-start | bytes 1048576 | tf_op jit(solution)/shard_map/all_to_all | solution.py:232
  176.5 1.6 copy-start.18
  178.1 29.2 %copy-start.3 = (bf16[768,512]{1,0:T(8,128)(2,1)S(1)}, bf16[768,512]{1,0:T(8,128)(2,1)}, u32[]{:S(2)}) copy-start(bf16[768,512]{1,0:T(8,128)(2,1)} %copy-done.2) | copy-start | bytes 2359300
  208.6 38.0 %all-to-all-start.2 = ((bf16[16,96,512]{2,1,0:T(8,128)(2,1)}), bf16[16,96,512]{2,1,0:T(8,128)(2,1)S(1)}, u32[]{:S(2)}, u32[]{:S(2)}) async-start(bf16[16,96,512]{2,1,0:T(8,128)(2,1)} %bitcast.11), calls=%async_computation.2 | async-start | bytes 3145728 | tf_op jit(solution)/shard_map/all_to_all | solution.py:232
  246.8 6.2 %collective-permute-start = (bf16[128,512]{1,0:T(8,128)(2,1)S(1)}, bf16[128,512]{1,0:T(8,128)(2,1)S(1)}, u32[]{:S(2)}, u32[]{:S(2)}) collective-permute-start(bf16[128,512]{1,0:T(8,128)(2,1)S(1)} %pad_maximum_fusion.2), channel_id=1, source_target_pairs={{0,16},{16,0},{1,17},{17,1},{2,18},{18,2},{3,19},{19,3},{4,20},{20... | collective-permute-start | bytes 393224 | tf_op jit(solution)/shard_map/ppermute | solution.py:240

commit v2 on v1

--- a/solution.py
+++ b/solution.py
@@ -49,37 +49,44 @@
 
 
 def attention_weights(q, k, allowed):
-    scores = dot(q, k, 1, 1) * (HEAD_DIM**-0.5)
-    exponent = jnp.where(allowed, jnp.exp(scores), 0.0)
-    return exponent / jnp.sum(exponent, axis=-1, keepdims=True)
+    exponent = jnp.where(allowed, jnp.exp(dot(q, k, 1, 1)), 0.0)
+    return exponent * (1.0 / jnp.sum(exponent, axis=-1, keepdims=True))
 
 
 def attention_grads(q, k, v, g, weights, rounded):
-    factor = HEAD_DIM**-0.5
     grad_v = dot(rounded, g, 0, 0).astype(BF16)
     grad_w = dot(g, v, 1, 1)
     inner = jnp.sum(grad_w * weights, axis=-1, keepdims=True)
     grad_s = (weights * (grad_w - inner)).astype(BF16)
-    grad_q = (dot(grad_s, k) * factor).astype(BF16)
-    grad_k = (dot(grad_s, q, 0, 0) * factor).astype(BF16)
+    grad_q = (dot(grad_s, k) * (HEAD_DIM**-0.5)).astype(BF16)
+    grad_k = dot(grad_s, q, 0, 0).astype(BF16)
     return grad_q, grad_k, grad_v
 
 
 def head_columns(qkv, h, half):
     at = h * HEAD_DIM
-    return [qkv[:, part * half + at : part * half + at + HEAD_DIM] for part in range(3)]
-
-
-def prepare_kernel(tokens, mask, mask_token, gain, w_out, cot, send, grad_space):
+    q, k, v = [qkv[:, part * half + at : part * half + at + HEAD_DIM] for part in range(3)]
+    return (q.astype(F32) * (HEAD_DIM**-0.5)).astype(BF16), k, v
+
+
+def prepare_kernel(
+    share, tokens, mask, mask_token, gain, w_out, cot, normed, grad_space, first, second
+):
     width = tokens.shape[1]
     half = width // 2
     masked = masked_rows(tokens[...], mask[...], mask_token[...])
     centred = masked - jnp.mean(masked, axis=-1, keepdims=True)
     spread = jnp.mean(centred * centred, axis=-1, keepdims=True)
-    send[:, :width] = (centred * lax.rsqrt(spread + NORM_EPS) * gain[...]).astype(BF16)
+    n = (centred * lax.rsqrt(spread + NORM_EPS) * gain[...]).astype(BF16)
+    normed[...] = n
     grad = dot(cot[...], w_out[...], 1, 1).astype(BF16)
-    send[:, width:] = grad[:, half:]
     grad_space[...] = grad[:, :half]
+    for s in range(tokens.shape[0] // share // 2):
+        for which, send in enumerate((first, second)):
+            to = slice(s * share, (s + 1) * share)
+            at = slice((2 * s + which) * share, (2 * s + which + 1) * share)
+            send[to, :width] = n[at, :]
+            send[to, width:] = grad[at, half:]
 
 
 def space_kernel(
@@ -139,8 +146,7 @@
             scr[:, s * local : (s + 1) * local, :] = block.reshape(owned, local, width + half)
     may = allowed[...] > 0.0
 
-    @pl.loop(0, owned)
-    def _(e):
+    def one(e):
         at = pl.ds(pl.multiple_of(e * length, length), length)
         if direct:
             block = scr[e].astype(BF16)
@@ -162,6 +168,13 @@
         else:
             out[at, :] = o
 
+    together = 2 if owned % 2 == 0 else 1
+
+    @pl.loop(0, owned // together)
+    def _(i):
+        for e in range(together):
+            one(i * together + e)
+
     if direct:
         for s in range(groups):
             block = o_scr[:, s * local : (s + 1) * local, :]
@@ -226,23 +239,24 @@
     return total
 
 
-def reduce_parts(parts, parts_out, scale):
-    def exchange(value, groups):
-        value = value.reshape(groups, value.shape[0] // groups, value.shape[1])
-        return sum_shares(lax.all_to_all(value, "seq", split_axis=0, concat_axis=0))
-
+def reduce_part(value, scale):
     groups = lax.axis_size("seq")
-    totals = [exchange(value, groups) for value in (parts, parts_out)]
-    cut = totals[0].shape[0]
-    total = jnp.concatenate(totals, axis=0).astype(BF16)
-    copies = lax.axis_size("dp")
-    if copies == 2:
+    pairs = groups // 2
+    value = value.reshape(pairs, 2, value.shape[0] // groups, value.shape[1])
+    odd = lax.axis_index("seq") % 2 == 1
+    sent = jnp.where(odd, value[:, 0], value[:, 1])
+    kept = jnp.where(odd, value[:, 1], value[:, 0])
+    got = lax.ppermute(sent, "seq", [(i, i ^ 1) for i in range(groups)])
+    both = (kept.astype(F32) + got.astype(F32)).astype(BF16)
+    sides = [list(range(side, groups, 2)) for side in range(2)]
+    terms = lax.all_to_all(both, "seq", split_axis=0, concat_axis=0, axis_index_groups=sides)
+    total = sum_shares(terms).astype(BF16)
+    if lax.axis_size("dp") == 2:
         other = lax.ppermute(total, "dp", [(0, 1), (1, 0)])
         whole = total.astype(F32) + other.astype(F32)
     else:
         whole = sum_shares(lax.all_gather(total, "dp"))
-    whole = whole * scale
-    return whole[:cut], whole[cut:]
+    return total, whole * scale
 
 
 def shards(tokens, patch_mask, mask_token, gain, w_qkv, w_out, block_ids, temporal_mask, cotangent):
@@ -266,15 +280,24 @@
     ).astype(F32)
     allowed = jnp.dot(jnp.dot(onehot, temporal_mask.astype(F32)), onehot.T)
 
-    send, grad_space = pl.pallas_call(
-        prepare_kernel,
+    owned_half = owned // 2
+    share = owned_half * local
+    some = count // 2
+    normed, grad_space, send_first, send_second = pl.pallas_call(
+        functools.partial(prepare_kernel, share),
         grid=(steps,),
         in_specs=[
             rows_of(tile, width), rows_of(tile, 1), full((1, width)), full((1, width)),
             full((width, width)), rows_of(tile, width),
         ],
-        out_specs=[rows_of(tile, width + half), rows_of(tile, half)],
-        out_shape=[shape(count, width + half), shape(count, half)],
+        out_specs=[
+            rows_of(tile, width), rows_of(tile, half),
+            rows_of(tile // 2, width + half), rows_of(tile // 2, width + half),
+        ],
+        out_shape=[
+            shape(count, width), shape(count, half),
+            shape(some, width + half), shape(some, width + half),
+        ],
         compiler_params=params(),
         cost_estimate=pl.CostEstimate(
             flops=2 * count * width * width, bytes_accessed=9 * count * width, transcendentals=0
@@ -282,12 +305,17 @@
     )(tokens_flat, mask, mask_token, gain, w_out, cot)
 
     direct = local % 8 == 0
-    recv = lax.all_to_all(
-        send.reshape(groups, owned, local, width + half), "seq", split_axis=0, concat_axis=0
-    )
-    if not direct:
-        recv = jnp.swapaxes(recv, 0, 1)
-    recv = recv.reshape(count, width + half)
+
+    def to_electrodes(send):
+        recv = lax.all_to_all(
+            send.reshape(groups, owned_half, local, width + half), "seq",
+            split_axis=0, concat_axis=0,
+        )
+        if not direct:
+            recv = jnp.swapaxes(recv, 0, 1)
+        return recv.reshape(some, width + half)
+
+    recv_first = to_electrodes(send_first)
 
     space_out, grad_qkv_space, grad_out_space = pl.pallas_call(
         functools.partial(space_kernel, local),
@@ -310,54 +338,81 @@
         cost_estimate=pl.CostEstimate(
             flops=32 * count * width * width, bytes_accessed=8 * count * width, transcendentals=0
         ),
-    )(send, grad_space, cot, w_qkv, ids.reshape(electrodes, 1), ids.reshape(1, electrodes))
-
-    time_out, normed_time, grad_time, qkv_time = pl.pallas_call(
-        functools.partial(time_forward_kernel, owned, local, direct),
-        grid=(1,),
-        in_specs=[
-            full((count, width + half)),
-            pl.BlockSpec((width, 3 * half), lambda i: (0, 1)),
-            full((length, length)),
-        ],
-        out_specs=[
-            full((count, half)), full((count, width)), full((count, half)), full((count, 3 * half)),
-        ],
-        out_shape=[
-            shape(count, half), shape(count, width), shape(count, half), shape(count, 3 * half),
-        ],
-        scratch_shapes=[
-            pltpu.VMEM((owned, length, width + half), F32),
-            pltpu.VMEM((owned, length, half), F32),
-        ],
-        compiler_params=params(),
-        cost_estimate=pl.CostEstimate(
-            flops=6 * count * width * width, bytes_accessed=8 * count * width, transcendentals=0
-        ),
-    )(recv, w_qkv, allowed)
-
-    if direct:
-        back = time_out.reshape(groups, owned, local, half)
-    else:
-        back = jnp.swapaxes(time_out.reshape(owned, groups, local, half), 0, 1)
+    )(normed, grad_space, cot, w_qkv, ids.reshape(electrodes, 1), ids.reshape(1, electrodes))
+
+    recv_first, send_second, space_out = lax.optimization_barrier(
+        (recv_first, send_second, space_out)
+    )
+    recv_second = to_electrodes(send_second)
+
+    def time_forward(recv):
+        return pl.pallas_call(
+            functools.partial(time_forward_kernel, owned_half, local, direct),
+            grid=(1,),
+            in_specs=[
+                full((some, width + half)),
+                pl.BlockSpec((width, 3 * half), lambda i: (0, 1)),
+                full((length, length)),
+            ],
+            out_specs=[
+                full((some, half)), full((some, width)), full((some, half)),
+                full((some, 3 * half)),
+            ],
+            out_shape=[
+                shape(some, half), shape(some, width), shape(some, half), shape(some, 3 * half),
+            ],
+            scratch_shapes=[
+                pltpu.VMEM((owned_half, length, width + half), F32),
+                pltpu.VMEM((owned_half, length, half), F32),
+            ],
+            compiler_params=params(),
+            cost_estimate=pl.CostEstimate(
+                flops=16 * some * width * width, bytes_accessed=8 * some * width,
+                transcendentals=0,
+            ),
+        )(recv, w_qkv, allowed)
+
+    pair = 2 * length if owned_half % 2 == 0 else length
+
+    def time_backward(normed_time, grad_time, qkv_time):
+        return pl.pallas_call(
+            functools.partial(time_backward_kernel, length),
+            grid=(some // pair,),
+            in_specs=[
+                rows_of(pair, width), rows_of(pair, half), rows_of(pair, 3 * half),
+                full((length, length)),
+            ],
+            out_specs=full((3 * half, width)),
+            out_shape=shape(3 * half, width),
+            scratch_shapes=[pltpu.VMEM((3 * half, width), F32)],
+            compiler_params=params(),
+            cost_estimate=pl.CostEstimate(
+                flops=24 * some * width * width, bytes_accessed=8 * some * width,
+                transcendentals=0,
+            ),
+        )(normed_time, grad_time, qkv_time, allowed)
+
+    time_first, *kept_first = time_forward(recv_first)
+    grad_qkv_first = time_backward(*kept_first)
+    recv_second, time_first, grad_qkv_first = lax.optimization_barrier(
+        (recv_second, time_first, grad_qkv_first)
+    )
+    time_second, *kept_second = time_forward(recv_second)
+
+    def by_group(out):
+        if direct:
+            return out.reshape(groups, share, half)
+        back = jnp.swapaxes(out.reshape(owned_half, groups, local, half), 0, 1)
+        return back.reshape(groups, share, half)
+
+    back = jnp.concatenate([by_group(time_first), by_group(time_second)], axis=1)
     time_back = lax.all_to_all(back, "seq", split_axis=0, concat_axis=0).reshape(count, half)
-
-    pair = 2 * length if owned % 2 == 0 else length
-    grad_qkv_time = pl.pallas_call(
-        functools.partial(time_backward_kernel, length),
-        grid=(count // pair,),
-        in_specs=[
-            rows_of(pair, width), rows_of(pair, half), rows_of(pair, 3 * half),
-            full((length, length)),
-        ],
-        out_specs=full((3 * half, width)),
-        out_shape=shape(3 * half, width),
-        scratch_shapes=[pltpu.VMEM((3 * half, width), F32)],
-        compiler_params=params(),
-        cost_estimate=pl.CostEstimate(
-            flops=16 * count * width * width, bytes_accessed=8 * count * width, transcendentals=0
-        ),
-    )(normed_time, grad_time, qkv_time, allowed)
+    grad_qkv_second = time_backward(*kept_second)
+    grad_qkv_time = (grad_qkv_first.astype(F32) + grad_qkv_second.astype(F32)).astype(BF16)
+    grad_qkv = jnp.concatenate([grad_qkv_space, grad_qkv_time], axis=0)
+    time_back, grad_qkv = lax.optimization_barrier((time_back, grad_qkv))
+    scale = 1.0 / math.sqrt(record_count * lax.axis_size("dp") * electrodes * length)
+    total_qkv, share_qkv = reduce_part(grad_qkv, scale)
 
     layer_out, grad_out_time = pl.pallas_call(
         finish_kernel,
@@ -375,10 +430,9 @@
         ),
     )(tokens_flat, mask, mask_token, space_out, time_back, w_out, cot)
 
-    grad_qkv = jnp.concatenate([grad_qkv_space, grad_qkv_time], axis=0)
     grad_out = jnp.concatenate([grad_out_space, grad_out_time], axis=1)
-    scale = 1.0 / math.sqrt(record_count * lax.axis_size("dp") * electrodes * length)
-    share_qkv, share_out = reduce_parts(grad_qkv, grad_out, scale)
+    total_qkv, grad_out = lax.optimization_barrier((total_qkv, grad_out))
+    _, share_out = reduce_part(grad_out, scale)
     return layer_out.reshape(tokens.shape), share_qkv, share_out
 
 

time: 258 us -> 198 us (0.77)
  waiting for transfers between devices: 95.6 us -> 32.1 us
  other arithmetic: 3.15 us -> 11.3 us
  Pallas kernels: 100 us -> 96.8 us
    all_to_all x3 -> x4, waiting for transfers between devices: 91 us -> 23.6 us  [the longest x2 17.8 us: reduce_part(): lax.all_to_all(both, 'seq', split_axis=0, concat_axis=0, axis_index_group...]
    all_to_all x1, starting transfers between devices: 15.6 us -> 9.11 us  [shards(): lax.all_to_all(back, 'seq', split_axis=0, concat_axis=0)]
    all_to_all x1, waiting for transfers between devices: 0.01 us -> 4.68 us  [shards(): lax.all_to_all(back, 'seq', split_axis=0, concat_axis=0)]
    all_to_all x3 -> x4, starting transfers between devices: 19.5 us -> 24 us  [the longest x2 13.7 us: to_electrodes(): lax.all_to_all(send.reshape(groups, owned_half, local, width + half), 'se...]
    convert_element_type x0 -> x5, other arithmetic: none -> 3.61 us  [the longest x2 2.04 us: reduce_part(): both = (kept.astype(F32) + got.astype(F32)).astype(BF16)]
    pallas_call x3 -> x5, Pallas kernels: 59.4 us -> 56.5 us  [the longest x2 28.2 us: time_backward(): pl.pallas_call(functools.partial(time_backward_kernel, length), grid=(som...]
    mul x1 -> x2, other arithmetic: 0.04 us -> 2.68 us  [reduce_part(): return (total, whole * scale)]
    unnamed x46 -> x54, local copies, waits for them, and re-layouts: 15.7 us -> 17.8 us
  transfers between devices with their start and end apart: 5 -> 9, of which waited for: 3 -> 7; matrix products, arithmetic and copies ran while one was open for 1% -> 2% of each run, Pallas kernels for 25% -> 40%
where the time goes in v2:
time: 198 us; the launch traced here: 197 us
  Pallas kernels  96.8 us (49%)
  starting transfers between devices  36.9 us (19%)
  waiting for transfers between devices  32.1 us (16%)
  local copies, waits for them, and re-layouts  18.3 us (9%)
  other arithmetic  11.3 us (6%)
    pallas_call x1, Pallas kernels, shards(): pl.pallas_call(functools.partial(space_kernel, local), grid=(local,), in_...  33.2 us
    pallas_call x2, Pallas kernels, time_backward(): pl.pallas_call(functools.partial(time_backward_kernel, length), grid=(som...  28.2 us
    pallas_call x2, Pallas kernels, time_forward(): pl.pallas_call(functools.partial(time_forward_kernel, owned_half, local,...  20.7 us
    all_to_all x2, waiting for transfers between devices, reduce_part(): lax.all_to_all(both, 'seq', split_axis=0, concat_axis=0, axis_index_group...  17.8 us
    unnamed x54, local copies, waits for them, and re-layouts  17.8 us
    all_to_all x2, starting transfers between devices, to_electrodes(): lax.all_to_all(send.reshape(groups, owned_half, local, width + half), 'se...  13.7 us
    all_to_all x2, starting transfers between devices, reduce_part(): lax.all_to_all(both, 'seq', split_axis=0, concat_axis=0, axis_index_group...  10.3 us
    all_to_all x1, starting transfers between devices, shards(): lax.all_to_all(back, 'seq', split_axis=0, concat_axis=0)  9.11 us
  transfers between devices with their start and end apart: 9, of which 7 were waited for; matrix products, arithmetic and copies ran while one was open for 2% of the time, Pallas kernels for 40%

profile of v2, /device:TPU:0, one launch (start us, length us, event | category | flops | bytes accessed | tf_op | source)
XLA Modules:
  0.0 196.6 jit_solution(16325240644966011070)
XLA Ops:
  3.2 7.5 %shard_map.112 = (bf16[2048,512]{1,0:T(8,128)(2,1)}, bf16[2048,256]{1,0:T(8,128)(2,1)S(1)}, bf16[1024,768]{1,0:T(8,128)(2,1)S(1)}, bf16[1024,768]{1,0:T(8,128)(2,1)}) custom-call(bf16[2048,512]{1,0:T(8,128)(2,1)} %bitcast.58, f32[2048,1]{1,0:T(8,128)S(1)} %convert_element_type.200.mask, f32[1,512]{1,0:T(1,128)S(1)} %bitcast.68, f32[1,512]{1,0:T(1,128)S(1)} %bitcast.67, ...), custom_call_target="tpu_custom_call" | custom-call | flops 1073741824 | bytes 9437184 | tf_op jit(solution)/shard_map/pallas_call | solution.py:286
  10.8 1.2 copy-done.1
  12.9 7.5 %all-to-all-start = ((bf16[16,8,8,768]{3,2,1,0:T(8,128)(2,1)}), bf16[16,8,8,768]{3,2,1,0:T(8,128)(2,1)S(1)}, u32[]{:S(2)}, u32[]{:S(2)}) async-start(bf16[16,8,8,768]{3,2,1,0:T(8,128)(2,1)} %bitcast.61), calls=%async_computation | async-start | bytes 3145728 | tf_op jit(solution)/shard_map/all_to_all | solution.py:310
  20.6 1.4 copy-done.15
  22.0 1.2 copy-done.17
  23.2 33.2 %shard_map.113 = (bf16[2048,256]{1,0:T(8,128)(2,1)S(1)}, bf16[768,512]{1,0:T(8,128)(2,1)S(1)}, bf16[512,256]{1,0:T(8,128)(2,1)S(1)}) custom-call(bf16[2048,512]{1,0:T(8,128)(2,1)} %get-tuple-element.31.normed, bf16[2048,256]{1,0:T(8,128)(2,1)S(1)} %copy-done.17, bf16[2048,512]{1,0:T(8,128)(2,1)} %bitcast.75, bf16[512,1536]{1,0:T(8,128)(2,1)S(1)} %copy-done.15, ...), custom_call_target="tpu_custom_call" | custom-call | flops 17179869184 | bytes 8388608 | tf_op jit(solution)/shard_map/pallas_call | solution.py:320
  58.1 6.2 %all-to-all-start.1 = ((bf16[16,8,8,768]{3,2,1,0:T(8,128)(2,1)}), bf16[16,8,8,768]{3,2,1,0:T(8,128)(2,1)}, u32[]{:S(2)}, u32[]{:S(2)}) async-start(bf16[16,8,8,768]{3,2,1,0:T(8,128)(2,1)} %bitcast.8), calls=%async_computation.1 | async-start | bytes 3145728 | tf_op jit(solution)/shard_map/all_to_all | solution.py:310
  64.6 10.1 %shard_map.114 = (bf16[1024,256]{1,0:T(8,128)(2,1)S(1)}, bf16[1024,512]{1,0:T(8,128)(2,1)S(1)}, bf16[1024,256]{1,0:T(8,128)(2,1)S(1)}, bf16[1024,768]{1,0:T(8,128)(2,1)S(1)}) custom-call(bf16[1024,768]{1,0:T(8,128)(2,1)S(1)} %bitcast.60, bf16[512,1536]{1,0:T(8,128)(2,1)} %w.5, f32[128,128]{1,0:T(8,128)S(1)} %fusion.1.allowed), custom_call_target="tpu_custom_call" | custom-call | flops 4294967296 | bytes 4194304 | tf_op jit(solution)/shard_map/pallas_call | solution.py:349
  75.5 14.1 %shard_map.115 = bf16[768,512]{1,0:T(8,128)(2,1)S(1)} custom-call(bf16[1024,512]{1,0:T(8,128)(2,1)S(1)} %get-tuple-element.38.normed, bf16[1024,256]{1,0:T(8,128)(2,1)S(1)} %get-tuple-element.39.grad, bf16[1024,768]{1,0:T(8,128)(2,1)S(1)} %get-tuple-element.40.qkv, f32[128,128]{1,0:T(8,128)S(1)} %fusion.1.allowed), custom_call_target="tpu_custom_call" | custom-call | flops 6442450944 | bytes 4194304 | tf_op jit(solution)/shard_map/pallas_call | solution.py:378
  90.5 5.8 %all-to-all-done.1 = bf16[16,8,8,768]{3,2,1,0:T(8,128)(2,1)} async-done(((bf16[16,8,8,768]{3,2,1,0:T(8,128)(2,1)}), bf16[16,8,8,768]{3,2,1,0:T(8,128)(2,1)}, u32[]{:S(2)}, u32[]{:S(2)}) %all-to-all-start.1) | async-done | bytes 1572896 | tf_op jit(solution)/shard_map/all_to_all | solution.py:310
  96.3 10.6 %shard_map.116 = (bf16[1024,256]{1,0:T(8,128)(2,1)S(1)}, bf16[1024,512]{1,0:T(8,128)(2,1)S(1)}, bf16[1024,256]{1,0:T(8,128)(2,1)S(1)}, bf16[1024,768]{1,0:T(8,128)(2,1)S(1)}) custom-call(bf16[1024,768]{1,0:T(8,128)(2,1)} %bitcast.9.recv, bf16[512,1536]{1,0:T(8,128)(2,1)} %w.5, f32[128,128]{1,0:T(8,128)S(1)} %fusion.1.allowed), custom_call_target="tpu_custom_call" | custom-call | flops 4294967296 | bytes 4194304 | tf_op jit(solution)/shard_map/pallas_call | solution.py:349
  110.2 9.1 %all-to-all-start.2 = ((bf16[16,128,256]{2,1,0:T(8,128)(2,1)}), bf16[16,128,256]{2,1,0:T(8,128)(2,1)S(1)}, u32[]{:S(2)}, u32[]{:S(2)}) async-start(bf16[16,128,256]{2,1,0:T(8,128)(2,1)} %pad_maximum_fusion.1), calls=%async_computation.2 | async-start | bytes 2097152 | tf_op jit(solution)/shard_map/all_to_all | solution.py:409
  119.3 1.4 copy-done.21
  120.7 1.2 copy-done.23
  121.9 14.1 %shard_map.117 = bf16[768,512]{1,0:T(8,128)(2,1)S(1)} custom-call(bf16[1024,512]{1,0:T(8,128)(2,1)S(1)} %copy-done.23, bf16[1024,256]{1,0:T(8,128)(2,1)S(1)} %get-tuple-element.47.grad, bf16[1024,768]{1,0:T(8,128)(2,1)S(1)} %copy-done.21, f32[128,128]{1,0:T(8,128)S(1)} %fusion.1.allowed), custom_call_target="tpu_custom_call" | custom-call | flops 6442450944 | bytes 4194304 | tf_op jit(solution)/shard_map/pallas_call | solution.py:378
  136.3 1.2 pad_maximum_fusion
  137.5 4.7 %all-to-all-done.2 = bf16[16,128,256]{2,1,0:T(8,128)(2,1)S(1)} async-done(((bf16[16,128,256]{2,1,0:T(8,128)(2,1)}), bf16[16,128,256]{2,1,0:T(8,128)(2,1)S(1)}, u32[]{:S(2)}, u32[]{:S(2)}) %all-to-all-start.2) | async-done | bytes 1048608 | tf_op jit(solution)/shard_map/all_to_all | solution.py:409
  142.2 1.9 select_bitcast_fusion
  144.8 1.9 collective-permute-done
  146.7 1.2 fusion
  147.9 6.7 %all-to-all-start.3 = ((bf16[8,96,512]{2,1,0:T(8,128)(2,1)}), bf16[8,96,512]{2,1,0:T(8,128)(2,1)}, u32[]{:S(2)}, u32[]{:S(2)}) async-start(bf16[8,96,512]{2,1,0:T(8,128)(2,1)} %fusion), calls=%async_computation.3 | async-start | bytes 1572864 | tf_op jit(solution)/shard_map/all_to_all | solution.py:252
  154.6 1.2 copy-done.3
  156.9 1.2 copy-done.19
  158.1 7.1 %shard_map.118 = (bf16[2048,512]{1,0:T(8,128)(2,1)}, bf16[512,256]{1,0:T(8,128)(2,1)S(1)}) custom-call(bf16[2048,512]{1,0:T(8,128)(2,1)S(1)} %bitcast.59, f32[2048,1]{1,0:T(8,128)S(1)} %convert_element_type.200.mask, f32[1,512]{1,0:T(1,128)S(1)} %bitcast.69, bf16[2048,256]{1,0:T(8,128)(2,1)S(1)} %copy-done.19, bf16[2048,256]{1,0:T(8,128)(2,1)S(1)} %bitcast.62, ...), custom_call_target="tpu_custom_call" | custom-call | flops 2147483648 | bytes 8388608 | tf_op jit(solution)/shard_map/pallas_call | solution.py:417
  165.2 10.1 %all-to-all-done.3 = bf16[8,96,512]{2,1,0:T(8,128)(2,1)} async-done(((bf16[8,96,512]{2,1,0:T(8,128)(2,1)}), bf16[8,96,512]{2,1,0:T(8,128)(2,1)}, u32[]{:S(2)}, u32[]{:S(2)}) %all-to-all-start.3) | async-done | bytes 786464 | tf_op jit(solution)/shard_map/all_to_all | solution.py:252
  175.3 1.3 fusion.5
  176.7 1.5 collective-permute-done.2
  179.1 3.6 %all-to-all-start.4 = ((bf16[8,32,512]{2,1,0:T(8,128)(2,1)}), bf16[8,32,512]{2,1,0:T(8,128)(2,1)S(1)}, u32[]{:S(2)}, u32[]{:S(2)}) async-start(bf16[8,32,512]{2,1,0:T(8,128)(2,1)} %fusion.4), calls=%async_computation.4 | async-start | bytes 524288 | tf_op jit(solution)/shard_map/all_to_all | solution.py:252
  182.7 1.5 collective-permute-start.1
  184.2 7.7 %all-to-all-done.4 = bf16[8,32,512]{2,1,0:T(8,128)(2,1)S(1)} async-done(((bf16[8,32,512]{2,1,0:T(8,128)(2,1)}), bf16[8,32,512]{2,1,0:T(8,128)(2,1)S(1)}, u32[]{:S(2)}, u32[]{:S(2)}) %all-to-all-start.4) | async-done | bytes 262176 | tf_op jit(solution)/shard_map/all_to_all | solution.py:252
  192.0 1.6 collective-permute-start.3
  193.5 2.0 %add_multiply_fusion = f32[96,512]{1,0:T(8,128)} fusion(bf16[96,512]{1,0:T(8,128)(2,1)S(1)} %collective-permute-done.1, bf16[8,96,512]{2,1,0:T(8,128)(2,1)} %all-to-all-done.3), kind=kLoop, calls=%fused_computation.17 | loop fusion | flops 983040 | bytes 1081344 | tf_op jit(solution)/shard_map/mul | solution.py:259
  (66 shorter events, 14.6 us)
Async XLA Ops:
  0.6 1.2 copy-start.6
  10.8 1.2 copy-start.1
  11.9 1.0 copy-start.16
  12.9 7.5 %copy-start.25 = (s32[256]{0:T(256)S(1)}, s32[256]{0:T(256)}, u32[]{:S(2)}) copy-start(s32[256]{0:T(256)} %param.15) | copy-start | bytes 3076
  12.9 45.1 %all-to-all-start = ((bf16[16,8,8,768]{3,2,1,0:T(8,128)(2,1)}), bf16[16,8,8,768]{3,2,1,0:T(8,128)(2,1)S(1)}, u32[]{:S(2)}, u32[]{:S(2)}) async-start(bf16[16,8,8,768]{3,2,1,0:T(8,128)(2,1)} %bitcast.61), calls=%async_computation | async-start | bytes 3145728 | tf_op jit(solution)/shard_map/all_to_all | solution.py:310
  20.6 1.4 copy-start.15
  22.0 1.2 copy-start.17
  57.1 1.0 copy-start.18
  58.1 6.2 %copy-start.26 = (s32[8,8]{1,0:T(8,128)S(1)}, s32[8,8]{1,0:T(8,128)}, u32[]{:S(2)}) copy-start(s32[8,8]{1,0:T(8,128)} %param.16) | copy-start | bytes 772
  58.1 38.2 %all-to-all-start.1 = ((bf16[16,8,8,768]{3,2,1,0:T(8,128)(2,1)}), bf16[16,8,8,768]{3,2,1,0:T(8,128)(2,1)}, u32[]{:S(2)}, u32[]{:S(2)}) async-start(bf16[16,8,8,768]{3,2,1,0:T(8,128)(2,1)} %bitcast.8), calls=%async_computation.1 | async-start | bytes 3145728 | tf_op jit(solution)/shard_map/all_to_all | solution.py:310
  89.6 0.9 copy-start.4
  96.3 12.8 %copy-start.9 = (bf16[1024,256]{1,0:T(8,128)(2,1)S(1)}, bf16[1024,256]{1,0:T(8,128)(2,1)}, u32[]{:S(2)}) copy-start(bf16[1024,256]{1,0:T(8,128)(2,1)} %copy-done.8) | copy-start | bytes 1572868
  106.9 1.1 copy-start.20
  108.1 1.0 copy-start.22
  110.2 32.1 %all-to-all-start.2 = ((bf16[16,128,256]{2,1,0:T(8,128)(2,1)}), bf16[16,128,256]{2,1,0:T(8,128)(2,1)S(1)}, u32[]{:S(2)}, u32[]{:S(2)}) async-start(bf16[16,128,256]{2,1,0:T(8,128)(2,1)} %pad_maximum_fusion.1), calls=%async_computation.2 | async-start | bytes 2097152 | tf_op jit(solution)/shard_map/all_to_all | solution.py:409
  119.3 1.4 copy-start.21
  120.7 1.2 copy-start.23
  121.9 14.1 %copy-start.5 = (bf16[768,512]{1,0:T(8,128)(2,1)S(1)}, bf16[768,512]{1,0:T(8,128)(2,1)}, u32[]{:S(2)}) copy-start(bf16[768,512]{1,0:T(8,128)(2,1)} %copy-done.4) | copy-start | bytes 2359300
  142.2 2.6 %copy-start.2 = (bf16[16,128,256]{2,1,0:T(8,128)(2,1)}, bf16[16,128,256]{2,1,0:T(8,128)(2,1)S(1)}, u32[]{:S(2)}) copy-start(bf16[16,128,256]{2,1,0:T(8,128)(2,1)S(1)} %all-to-all-done.2) | copy-start | bytes 3145732
  142.2 4.5 %copy-start.24 = (bf16[1536,512]{1,0:T(8,128)(2,1)S(1)}, bf16[1536,512]{1,0:T(8,128)(2,1)}, u32[]{:S(2)}) copy-start(bf16[1536,512]{1,0:T(8,128)(2,1)} %pad_maximum_fusion) | copy-start | bytes 4718596
  144.1 2.6 %collective-permute-start = (bf16[8,96,512]{2,1,0:T(8,128)(2,1)S(1)}, bf16[8,96,512]{2,1,0:T(8,128)(2,1)S(1)}, u32[]{:S(2)}, u32[]{:S(2)}) collective-permute-start(bf16[8,96,512]{2,1,0:T(8,128)(2,1)S(1)} %select_bitcast_fusion), channel_id=1, source_target_pairs={{0,1},{1,0},{2,3},{3,2},{4,5},{5,4},{6,7},{7,6},{8,9},{9,8},{10,11... | collective-permute-start | bytes 2359304 | tf_op jit(solution)/shard_map/ppermute | solution.py:249
  146.7 7.9 %copy-start = (bf16[1,256,8,512]{3,2,1,0:T(8,128)(2,1)S(1)}, bf16[1,256,8,512]{3,2,1,0:T(8,128)(2,1)}, u32[]{:S(2)}) copy-start(bf16[1,256,8,512]{3,2,1,0:T(8,128)(2,1)} %param.9) | copy-start | bytes 6291460
  147.9 6.7 %copy-start.14 = (f32[512]{0:T(512)S(1)}, f32[512]{0:T(512)}, u32[]{:S(2)}) copy-start(f32[512]{0:T(512)} %param.11) | copy-start | bytes 6148
  147.9 27.4 %all-to-all-start.3 = ((bf16[8,96,512]{2,1,0:T(8,128)(2,1)}), bf16[8,96,512]{2,1,0:T(8,128)(2,1)}, u32[]{:S(2)}, u32[]{:S(2)}) async-start(bf16[8,96,512]{2,1,0:T(8,128)(2,1)} %fusion), calls=%async_computation.3 | async-start | bytes 1572864 | tf_op jit(solution)/shard_map/all_to_all | solution.py:252
  154.6 1.2 copy-start.3
  155.8 1.0 copy-start.7
  156.9 1.2 copy-start.19
  158.1 7.1 %copy-start.11 = (bf16[512,256]{1,0:T(8,128)(2,1)S(1)}, bf16[512,256]{1,0:T(8,128)(2,1)}, u32[]{:S(2)}) copy-start(bf16[512,256]{1,0:T(8,128)(2,1)} %copy-done.10) | copy-start | bytes 786436
  176.7 1.6 collective-permute-start.2
  179.1 12.9 %all-to-all-start.4 = ((bf16[8,32,512]{2,1,0:T(8,128)(2,1)}), bf16[8,32,512]{2,1,0:T(8,128)(2,1)S(1)}, u32[]{:S(2)}, u32[]{:S(2)}) async-start(bf16[8,32,512]{2,1,0:T(8,128)(2,1)} %fusion.4), calls=%async_computation.4 | async-start | bytes 524288 | tf_op jit(solution)/shard_map/all_to_all | solution.py:252
  182.7 10.8 %collective-permute-start.1 = (bf16[96,512]{1,0:T(8,128)(2,1)S(1)}, bf16[96,512]{1,0:T(8,128)(2,1)S(1)}, u32[]{:S(2)}, u32[]{:S(2)}) collective-permute-start(bf16[96,512]{1,0:T(8,128)(2,1)S(1)} %fusion.5), channel_id=1, source_target_pairs={{0,16},{16,0},{1,17},{17,1},{2,18},{18,2},{3,19},{19,3},{4,20},{20... | collective-permute-start | bytes 294920 | tf_op jit(solution)/shard_map/ppermute | solution.py:255
  192.0 4.0 %collective-permute-start.3 = (bf16[32,512]{1,0:T(8,128)(2,1)S(1)}, bf16[32,512]{1,0:T(8,128)(2,1)S(1)}, u32[]{:S(2)}, u32[]{:S(2)}) collective-permute-start(bf16[32,512]{1,0:T(8,128)(2,1)S(1)} %fusion.6), channel_id=1, source_target_pairs={{0,16},{16,0},{1,17},{17,1},{2,18},{18,2},{3,19},{19,3},{4,20},{20... | collective-permute-start | bytes 98312 | tf_op jit(solution)/shard_map/ppermute | solution.py:255
  (4 other events, 2.9 us)

commit v3 on v2

--- a/solution.py
+++ b/solution.py
@@ -33,6 +33,10 @@
     return pl.BlockSpec((rows, columns), lambda i: (i, 0))
 
 
+def columns_of(rows, columns):
+    return pl.BlockSpec((rows, columns), lambda i: (0, i))
+
+
 def scatter_rows(scratch, value, rows=slice(None)):
     for c in range(scratch.shape[0]):
         scratch[c, rows, :] = value[:, c * LANES : (c + 1) * LANES].astype(F32)
@@ -49,24 +53,28 @@
 
 
 def attention_weights(q, k, allowed):
-    exponent = jnp.where(allowed, jnp.exp(dot(q, k, 1, 1)), 0.0)
-    return exponent * (1.0 / jnp.sum(exponent, axis=-1, keepdims=True))
+    exponent = jnp.where(allowed, jnp.exp(dot(k, q, 0, 0)), 0.0)
+    return exponent * (1.0 / jnp.sum(exponent, axis=0, keepdims=True))
 
 
 def attention_grads(q, k, v, g, weights, rounded):
-    grad_v = dot(rounded, g, 0, 0).astype(BF16)
-    grad_w = dot(g, v, 1, 1)
-    inner = jnp.sum(grad_w * weights, axis=-1, keepdims=True)
+    grad_v = dot(g, rounded, 1, 1).astype(BF16)
+    grad_w = dot(v, g, 0, 0)
+    inner = jnp.sum(grad_w * weights, axis=0, keepdims=True)
     grad_s = (weights * (grad_w - inner)).astype(BF16)
-    grad_q = (dot(grad_s, k) * (HEAD_DIM**-0.5)).astype(BF16)
-    grad_k = dot(grad_s, q, 0, 0).astype(BF16)
+    grad_q = (dot(k, grad_s) * (HEAD_DIM**-0.5)).astype(BF16)
+    grad_k = dot(q, grad_s, 1, 1).astype(BF16)
     return grad_q, grad_k, grad_v
 
 
-def head_columns(qkv, h, half):
+def head_rows(qkv, h, half):
     at = h * HEAD_DIM
-    q, k, v = [qkv[:, part * half + at : part * half + at + HEAD_DIM] for part in range(3)]
+    q, k, v = [qkv[part * half + at : part * half + at + HEAD_DIM, :] for part in range(3)]
     return (q.astype(F32) * (HEAD_DIM**-0.5)).astype(BF16), k, v
+
+
+def transposed(value):
+    return value.astype(F32).T.astype(BF16)
 
 
 def prepare_kernel(
@@ -108,35 +116,35 @@
 
     mine = pl.ds(p, electrodes, stride=patches)
     n = gather_rows(n_scr, mine).astype(BF16)
-    g = gather_rows(g_scr, mine).astype(BF16)
+    g = gather_rows(g_scr, mine).T.astype(BF16)
     c = gather_rows(c_scr, mine).astype(BF16)
     allowed = id_col[...] == id_row[...]
-    qkv = dot(n, w[...]).astype(BF16)
+    qkv = dot(w[...], n, 1, 1).astype(BF16)
     outs, grads = [], [[], [], []]
     for h in range(half // HEAD_DIM):
-        q, k, v = head_columns(qkv, h, half)
-        gh = g[:, h * HEAD_DIM : (h + 1) * HEAD_DIM]
+        q, k, v = head_rows(qkv, h, half)
+        gh = g[h * HEAD_DIM : (h + 1) * HEAD_DIM, :]
         weights = attention_weights(q, k, allowed)
         rounded = weights.astype(BF16)
-        outs.append(dot(rounded, v).astype(BF16))
+        outs.append(dot(v, rounded).astype(BF16))
         for part, value in zip(grads, attention_grads(q, k, v, gh, weights, rounded)):
             part.append(value)
-    o = jnp.concatenate(outs, axis=1)
-    scatter_rows(o_scr, o, mine)
-    projected_grad = jnp.concatenate(grads[0] + grads[1] + grads[2], axis=1)
-    q_acc[...] += dot(projected_grad, n, 0, 0)
-    o_acc[...] += dot(c, o, 0, 0)
+    o = jnp.concatenate(outs, axis=0)
+    scatter_rows(o_scr, o.astype(F32).T, mine)
+    projected_grad = jnp.concatenate(grads[0] + grads[1] + grads[2], axis=0)
+    q_acc[...] += dot(projected_grad, n)
+    o_acc[...] += dot(o, c)
 
     @pl.when(p == patches - 1)
     def _():
         out[...] = gather_rows(o_scr, slice(None)).astype(BF16)
         qkv_grad[...] = q_acc[...].astype(BF16)
-        out_grad[...] = o_acc[...].astype(BF16)
+        out_grad[...] = o_acc[...].T.astype(BF16)
 
 
 def time_forward_kernel(owned, local, direct, recv, w, allowed, out, normed, grad, qkv, scr, o_scr):
     width = normed.shape[1]
-    half = grad.shape[1]
+    half = grad.shape[0]
     steps = owned * local
     groups = recv.shape[0] // steps
     length = groups * local
@@ -154,19 +162,19 @@
             block = recv[at, :]
         n = block[:, :width]
         normed[at, :] = n
-        grad[at, :] = block[:, width:]
-        mine = dot(n, w[...]).astype(BF16)
-        qkv[at, :] = mine
+        grad[:, at] = transposed(block[:, width:])
+        mine = dot(w[...], n, 1, 1).astype(BF16)
+        qkv[:, at] = mine
         outs = []
         for h in range(half // HEAD_DIM):
-            q, k, v = head_columns(mine, h, half)
+            q, k, v = head_rows(mine, h, half)
             rounded = attention_weights(q, k, may).astype(BF16)
-            outs.append(dot(rounded, v).astype(BF16))
-        o = jnp.concatenate(outs, axis=1)
+            outs.append(dot(v, rounded).astype(BF16))
+        o = jnp.concatenate(outs, axis=0).astype(F32).T
         if direct:
-            o_scr[e] = o.astype(F32)
+            o_scr[e] = o
         else:
-            out[at, :] = o
+            out[at, :] = o.astype(BF16)
 
     together = 2 if owned % 2 == 0 else 1
 
@@ -183,7 +191,7 @@
 
 def time_backward_kernel(length, normed, grad, qkv, allowed, qkv_grad, acc):
     i = pl.program_id(0)
-    half = grad.shape[1]
+    half = grad.shape[0]
     may = allowed[...] > 0.0
 
     @pl.when(i == 0)
@@ -193,17 +201,17 @@
     both = []
     for e in range(normed.shape[0] // length):
         at = slice(e * length, (e + 1) * length)
-        mine, g = qkv[at, :], grad[at, :]
+        mine, g = qkv[:, at], grad[:, at]
         grads = [[], [], []]
         for h in range(half // HEAD_DIM):
-            q, k, v = head_columns(mine, h, half)
-            gh = g[:, h * HEAD_DIM : (h + 1) * HEAD_DIM]
+            q, k, v = head_rows(mine, h, half)
+            gh = g[h * HEAD_DIM : (h + 1) * HEAD_DIM, :]
             weights = attention_weights(q, k, may)
             found = attention_grads(q, k, v, gh, weights, weights.astype(BF16))
             for part, value in zip(grads, found):
                 part.append(value)
-        both.append(jnp.concatenate(grads[0] + grads[1] + grads[2], axis=1))
-    acc[...] += dot(jnp.concatenate(both, axis=0), normed[...], 0, 0)
+        both.append(jnp.concatenate(grads[0] + grads[1] + grads[2], axis=0))
+    acc[...] += dot(jnp.concatenate(both, axis=1), normed[...])
 
     @pl.when(i == pl.num_programs(0) - 1)
     def _():
@@ -239,7 +247,7 @@
     return total
 
 
-def reduce_part(value, scale):
+def sum_pair(value):
     groups = lax.axis_size("seq")
     pairs = groups // 2
     value = value.reshape(pairs, 2, value.shape[0] // groups, value.shape[1])
@@ -247,7 +255,11 @@
     sent = jnp.where(odd, value[:, 0], value[:, 1])
     kept = jnp.where(odd, value[:, 1], value[:, 0])
     got = lax.ppermute(sent, "seq", [(i, i ^ 1) for i in range(groups)])
-    both = (kept.astype(F32) + got.astype(F32)).astype(BF16)
+    return (kept.astype(F32) + got.astype(F32)).astype(BF16)
+
+
+def reduce_pairs(both, scale):
+    groups = lax.axis_size("seq")
     sides = [list(range(side, groups, 2)) for side in range(2)]
     terms = lax.all_to_all(both, "seq", split_axis=0, concat_axis=0, axis_index_groups=sides)
     total = sum_shares(terms).astype(BF16)
@@ -278,7 +290,8 @@
     onehot = (
         jnp.arange(length)[:, None] // (length // blocks) == jnp.arange(blocks)[None, :]
     ).astype(F32)
-    allowed = jnp.dot(jnp.dot(onehot, temporal_mask.astype(F32)), onehot.T)
+    allowed = jnp.dot(jnp.dot(onehot, temporal_mask.astype(F32)), onehot.T).T
+    w_rows = w_qkv.T
 
     owned_half = owned // 2
     share = owned_half * local
@@ -322,7 +335,7 @@
         grid=(local,),
         in_specs=[
             full((count, width)), full((count, half)), full((count, width)),
-            full((width, 3 * half)), full((electrodes, 1)), full((1, electrodes)),
+            full((3 * half, width)), full((electrodes, 1)), full((1, electrodes)),
         ],
         out_specs=[full((count, half)), full((3 * half, width)), full((width, half))],
         out_shape=[shape(count, half), shape(3 * half, width), shape(width, half)],
@@ -332,13 +345,13 @@
             pltpu.VMEM((width // LANES, count, LANES), F32),
             pltpu.VMEM((half // LANES, count, LANES), F32),
             pltpu.VMEM((3 * half, width), F32),
-            pltpu.VMEM((width, half), F32),
+            pltpu.VMEM((half, width), F32),
         ],
         compiler_params=params(),
         cost_estimate=pl.CostEstimate(
             flops=32 * count * width * width, bytes_accessed=8 * count * width, transcendentals=0
         ),
-    )(normed, grad_space, cot, w_qkv, ids.reshape(electrodes, 1), ids.reshape(1, electrodes))
+    )(normed, grad_space, cot, w_rows, ids.reshape(electrodes, 1), ids.reshape(1, electrodes))
 
     recv_first, send_second, space_out = lax.optimization_barrier(
         (recv_first, send_second, space_out)
@@ -351,15 +364,15 @@
             grid=(1,),
             in_specs=[
                 full((some, width + half)),
-                pl.BlockSpec((width, 3 * half), lambda i: (0, 1)),
+                pl.BlockSpec((3 * half, width), lambda i: (1, 0)),
                 full((length, length)),
             ],
             out_specs=[
-                full((some, half)), full((some, width)), full((some, half)),
-                full((some, 3 * half)),
+                full((some, half)), full((some, width)), full((half, some)),
+                full((3 * half, some)),
             ],
             out_shape=[
-                shape(some, half), shape(some, width), shape(some, half), shape(some, 3 * half),
+                shape(some, half), shape(some, width), shape(half, some), shape(3 * half, some),
             ],
             scratch_shapes=[
                 pltpu.VMEM((owned_half, length, width + half), F32),
@@ -370,7 +383,7 @@
                 flops=16 * some * width * width, bytes_accessed=8 * some * width,
                 transcendentals=0,
             ),
-        )(recv, w_qkv, allowed)
+        )(recv, w_rows, allowed)
 
     pair = 2 * length if owned_half % 2 == 0 else length
 
@@ -379,7 +392,7 @@
             functools.partial(time_backward_kernel, length),
             grid=(some // pair,),
             in_specs=[
-                rows_of(pair, width), rows_of(pair, half), rows_of(pair, 3 * half),
+                rows_of(pair, width), columns_of(half, pair), columns_of(3 * half, pair),
                 full((length, length)),
             ],
             out_specs=full((3 * half, width)),
@@ -410,9 +423,9 @@
     grad_qkv_second = time_backward(*kept_second)
     grad_qkv_time = (grad_qkv_first.astype(F32) + grad_qkv_second.astype(F32)).astype(BF16)
     grad_qkv = jnp.concatenate([grad_qkv_space, grad_qkv_time], axis=0)
-    time_back, grad_qkv = lax.optimization_barrier((time_back, grad_qkv))
+    time_back, pair_qkv = lax.optimization_barrier((time_back, sum_pair(grad_qkv)))
     scale = 1.0 / math.sqrt(record_count * lax.axis_size("dp") * electrodes * length)
-    total_qkv, share_qkv = reduce_part(grad_qkv, scale)
+    total_qkv, share_qkv = reduce_pairs(pair_qkv, scale)
 
     layer_out, grad_out_time = pl.pallas_call(
         finish_kernel,
@@ -431,8 +444,8 @@
     )(tokens_flat, mask, mask_token, space_out, time_back, w_out, cot)
 
     grad_out = jnp.concatenate([grad_out_space, grad_out_time], axis=1)
-    total_qkv, grad_out = lax.optimization_barrier((total_qkv, grad_out))
-    _, share_out = reduce_part(grad_out, scale)
+    total_qkv, pair_out = lax.optimization_barrier((total_qkv, sum_pair(grad_out)))
+    _, share_out = reduce_pairs(pair_out, scale)
     return layer_out.reshape(tokens.shape), share_qkv, share_out
 
 

time: 198 us -> 190 us (0.960)
  Pallas kernels: 96.8 us -> 87.5 us
  waiting for transfers between devices: 32.1 us -> 36.3 us
  other arithmetic: 11.3 us -> 8.37 us
    pallas_call x2, Pallas kernels: 28.2 us -> 18.1 us  [time_backward(): pl.pallas_call(functools.partial(time_backward_kernel, length), grid=(som...]
    pallas_call x2, Pallas kernels: 20.7 us -> 24 us  [time_forward(): pl.pallas_call(functools.partial(time_forward_kernel, owned_half, local,...]
    all_to_all x1, waiting for transfers between devices: 4.68 us -> 7.65 us  [shards(): lax.all_to_all(back, 'seq', split_axis=0, concat_axis=0)]
    all_to_all x2, waiting for transfers between devices: 5.75 us -> 8.65 us  [to_electrodes(): lax.all_to_all(send.reshape(groups, owned_half, local, width + half), 'se...]
    pallas_call x1, Pallas kernels: 33.2 us -> 30.4 us  [shards(): pl.pallas_call(functools.partial(space_kernel, local), grid=(local,), in_...]
    unnamed x54 -> x53, local copies, waits for them, and re-layouts: 17.8 us -> 17.7 us
  transfers between devices with their start and end apart: 9 -> 9, of which waited for: 7 -> 7; matrix products, arithmetic and copies ran while one was open for 2% -> 4% of each run, Pallas kernels for 40% -> 36%
where the time goes in v3:
time: 190 us; the launch traced here: 188 us
  Pallas kernels  87.5 us (46%)
  starting transfers between devices  36.8 us (19%)
  waiting for transfers between devices  36.3 us (19%)
  local copies, waits for them, and re-layouts  18.3 us (10%)
  other arithmetic  8.37 us (4%)
    pallas_call x1, Pallas kernels, shards(): pl.pallas_call(functools.partial(space_kernel, local), grid=(local,), in_...  30.4 us
    pallas_call x2, Pallas kernels, time_forward(): pl.pallas_call(functools.partial(time_forward_kernel, owned_half, local,...  24 us
    pallas_call x2, Pallas kernels, time_backward(): pl.pallas_call(functools.partial(time_backward_kernel, length), grid=(som...  18.1 us
    unnamed x53, local copies, waits for them, and re-layouts  17.7 us
    all_to_all x2, waiting for transfers between devices, reduce_pairs(): lax.all_to_all(both, 'seq', split_axis=0, concat_axis=0, axis_index_group...  16.1 us
    all_to_all x2, starting transfers between devices, to_electrodes(): lax.all_to_all(send.reshape(groups, owned_half, local, width + half), 'se...  13.5 us
    all_to_all x2, starting transfers between devices, reduce_pairs(): lax.all_to_all(both, 'seq', split_axis=0, concat_axis=0, axis_index_group...  10.4 us
    all_to_all x1, starting transfers between devices, shards(): lax.all_to_all(back, 'seq', split_axis=0, concat_axis=0)  9.3 us
  transfers between devices with their start and end apart: 9, of which 7 were waited for; matrix products, arithmetic and copies ran while one was open for 4% of the time, Pallas kernels for 36%

profile of v3, /device:TPU:0, one launch (start us, length us, event | category | flops | bytes accessed | tf_op | source)
XLA Modules:
  0.0 188.5 jit_solution(4865246202137771308)
XLA Ops:
  3.2 7.5 %shard_map.112 = (bf16[2048,512]{1,0:T(8,128)(2,1)}, bf16[2048,256]{1,0:T(8,128)(2,1)S(1)}, bf16[1024,768]{1,0:T(8,128)(2,1)}, bf16[1024,768]{1,0:T(8,128)(2,1)S(1)}) custom-call(bf16[2048,512]{1,0:T(8,128)(2,1)} %bitcast.59, f32[2048,1]{1,0:T(8,128)S(1)} %convert_element_type.200.mask, f32[1,512]{1,0:T(1,128)S(1)} %bitcast.71, f32[1,512]{1,0:T(1,128)S(1)} %bitcast.70, ...), custom_call_target="tpu_custom_call" | custom-call | flops 1073741824 | bytes 9437184 | tf_op jit(solution)/shard_map/pallas_call | solution.py:299
  10.8 1.2 copy-done.2
  12.9 7.4 %all-to-all-start = ((bf16[16,8,8,768]{3,2,1,0:T(8,128)(2,1)}), bf16[16,8,8,768]{3,2,1,0:T(8,128)(2,1)}, u32[]{:S(2)}, u32[]{:S(2)}) async-start(bf16[16,8,8,768]{3,2,1,0:T(8,128)(2,1)} %bitcast.4), calls=%async_computation | async-start | bytes 3145728 | tf_op jit(solution)/shard_map/all_to_all | solution.py:323
  20.3 1.7 copy.20
  22.2 1.6 copy-done.15
  23.9 30.4 %shard_map.113 = (bf16[2048,256]{1,0:T(8,128)(2,1)S(1)}, bf16[768,512]{1,0:T(8,128)(2,1)S(1)}, bf16[512,256]{1,0:T(8,128)(2,1)S(1)}) custom-call(bf16[2048,512]{1,0:T(8,128)(2,1)} %get-tuple-element.31.normed, bf16[2048,256]{1,0:T(8,128)(2,1)S(1)} %copy-done.15, bf16[2048,512]{1,0:T(8,128)(2,1)} %bitcast.78, bf16[1536,512]{1,0:T(8,128)(2,1)S(1)} %bitcast.61, ...), custom_call_target="tpu_custom_call" | custom-call | flops 17179869184 | bytes 8388608 | tf_op jit(solution)/shard_map/pallas_call | solution.py:333
  56.0 6.1 %all-to-all-start.1 = ((bf16[16,8,8,768]{3,2,1,0:T(8,128)(2,1)}), bf16[16,8,8,768]{3,2,1,0:T(8,128)(2,1)S(1)}, u32[]{:S(2)}, u32[]{:S(2)}) async-start(bf16[16,8,8,768]{3,2,1,0:T(8,128)(2,1)} %bitcast.64), calls=%async_computation.1 | async-start | bytes 3145728 | tf_op jit(solution)/shard_map/all_to_all | solution.py:323
  62.5 12.2 %shard_map.114 = (bf16[1024,256]{1,0:T(8,128)(2,1)S(1)}, bf16[1024,512]{1,0:T(8,128)(2,1)S(1)}, bf16[256,1024]{1,0:T(8,128)(2,1)S(1)}, bf16[768,1024]{1,0:T(8,128)(2,1)S(1)}) custom-call(bf16[1024,768]{1,0:T(8,128)(2,1)} %bitcast.5.recv, bf16[1536,512]{1,0:T(8,128)(2,1)} %bitcast.62, f32[128,128]{1,0:T(8,128)S(1)} %fusion.1.allowed), custom_call_target="tpu_custom_call" | custom-call | flops 4294967296 | bytes 4194304 | tf_op jit(solution)/shard_map/pallas_call | solution.py:362
  75.5 9.0 %shard_map.115 = bf16[768,512]{1,0:T(8,128)(2,1)S(1)} custom-call(bf16[1024,512]{1,0:T(8,128)(2,1)S(1)} %get-tuple-element.38.normed, bf16[256,1024]{1,0:T(8,128)(2,1)S(1)} %get-tuple-element.39.grad, bf16[768,1024]{1,0:T(8,128)(2,1)S(1)} %get-tuple-element.40.qkv, f32[128,128]{1,0:T(8,128)S(1)} %fusion.1.allowed), custom_call_target="tpu_custom_call" | custom-call | flops 6442450944 | bytes 4194304 | tf_op jit(solution)/shard_map/pallas_call | solution.py:391
  85.4 8.6 %all-to-all-done.1 = bf16[16,8,8,768]{3,2,1,0:T(8,128)(2,1)S(1)} async-done(((bf16[16,8,8,768]{3,2,1,0:T(8,128)(2,1)}), bf16[16,8,8,768]{3,2,1,0:T(8,128)(2,1)S(1)}, u32[]{:S(2)}, u32[]{:S(2)}) %all-to-all-start.1) | async-done | bytes 1572896 | tf_op jit(solution)/shard_map/all_to_all | solution.py:323
  94.1 11.8 %shard_map.116 = (bf16[1024,256]{1,0:T(8,128)(2,1)S(1)}, bf16[1024,512]{1,0:T(8,128)(2,1)S(1)}, bf16[256,1024]{1,0:T(8,128)(2,1)S(1)}, bf16[768,1024]{1,0:T(8,128)(2,1)S(1)}) custom-call(bf16[1024,768]{1,0:T(8,128)(2,1)S(1)} %bitcast.65, bf16[1536,512]{1,0:T(8,128)(2,1)} %bitcast.63, f32[128,128]{1,0:T(8,128)S(1)} %fusion.1.allowed), custom_call_target="tpu_custom_call" | custom-call | flops 4294967296 | bytes 4194304 | tf_op jit(solution)/shard_map/pallas_call | solution.py:362
  105.9 1.1 copy-done.18
  108.8 1.1 pad_maximum_fusion.1
  109.9 9.3 %all-to-all-start.2 = ((bf16[16,128,256]{2,1,0:T(8,128)(2,1)}), bf16[16,128,256]{2,1,0:T(8,128)(2,1)}, u32[]{:S(2)}, u32[]{:S(2)}) async-start(bf16[16,128,256]{2,1,0:T(8,128)(2,1)} %pad_maximum_fusion.1), calls=%async_computation.2 | async-start | bytes 2097152 | tf_op jit(solution)/shard_map/all_to_all | solution.py:422
  119.3 1.2 copy-done.21
  120.5 1.0 copy-done.23
  121.5 9.0 %shard_map.117 = bf16[768,512]{1,0:T(8,128)(2,1)S(1)} custom-call(bf16[1024,512]{1,0:T(8,128)(2,1)S(1)} %copy-done.21, bf16[256,1024]{1,0:T(8,128)(2,1)S(1)} %copy-done.23, bf16[768,1024]{1,0:T(8,128)(2,1)S(1)} %copy-done.19, f32[128,128]{1,0:T(8,128)S(1)} %fusion.1.allowed), custom_call_target="tpu_custom_call" | custom-call | flops 6442450944 | bytes 4194304 | tf_op jit(solution)/shard_map/pallas_call | solution.py:391
  131.4 1.9 %collective-permute-done = bf16[8,96,512]{2,1,0:T(8,128)(2,1)S(1)} collective-permute-done((bf16[8,96,512]{2,1,0:T(8,128)(2,1)S(1)}, bf16[8,96,512]{2,1,0:T(8,128)(2,1)S(1)}, u32[]{:S(2)}, u32[]{:S(2)}) %collective-permute-start) | collective-permute-done | bytes 786464 | tf_op jit(solution)/shard_map/ppermute | solution.py:257
  133.3 1.2 fusion
  134.6 7.7 %all-to-all-done.2 = bf16[16,128,256]{2,1,0:T(8,128)(2,1)} async-done(((bf16[16,128,256]{2,1,0:T(8,128)(2,1)}), bf16[16,128,256]{2,1,0:T(8,128)(2,1)}, u32[]{:S(2)}, u32[]{:S(2)}) %all-to-all-start.2) | async-done | bytes 1048608 | tf_op jit(solution)/shard_map/all_to_all | solution.py:422
  142.2 6.8 %all-to-all-start.3 = ((bf16[8,96,512]{2,1,0:T(8,128)(2,1)}), bf16[8,96,512]{2,1,0:T(8,128)(2,1)}, u32[]{:S(2)}, u32[]{:S(2)}) async-start(bf16[8,96,512]{2,1,0:T(8,128)(2,1)} %fusion), calls=%async_computation.3 | async-start | bytes 1572864 | tf_op jit(solution)/shard_map/all_to_all | solution.py:264
  149.0 1.0 copy-done.6
  150.0 1.2 copy-done.17
  151.3 7.4 %shard_map.118 = (bf16[2048,512]{1,0:T(8,128)(2,1)}, bf16[512,256]{1,0:T(8,128)(2,1)S(1)}) custom-call(bf16[2048,512]{1,0:T(8,128)(2,1)S(1)} %bitcast.60, f32[2048,1]{1,0:T(8,128)S(1)} %convert_element_type.200.mask, f32[1,512]{1,0:T(1,128)S(1)} %bitcast.72, bf16[2048,256]{1,0:T(8,128)(2,1)S(1)} %copy-done.17, bf16[2048,256]{1,0:T(8,128)(2,1)} %bitcast.13.time, ...), custom_call_target="tpu_custom_call" | custom-call | flops 2147483648 | bytes 8388608 | tf_op jit(solution)/shard_map/pallas_call | solution.py:430
  158.8 1.5 collective-permute-done.2
  161.2 8.5 %all-to-all-done.3 = bf16[8,96,512]{2,1,0:T(8,128)(2,1)} async-done(((bf16[8,96,512]{2,1,0:T(8,128)(2,1)}), bf16[8,96,512]{2,1,0:T(8,128)(2,1)}, u32[]{:S(2)}, u32[]{:S(2)}) %all-to-all-start.3) | async-done | bytes 786464 | tf_op jit(solution)/shard_map/all_to_all | solution.py:264
  169.7 1.3 fusion.5
  171.0 3.6 %all-to-all-start.4 = ((bf16[8,32,512]{2,1,0:T(8,128)(2,1)}), bf16[8,32,512]{2,1,0:T(8,128)(2,1)S(1)}, u32[]{:S(2)}, u32[]{:S(2)}) async-start(bf16[8,32,512]{2,1,0:T(8,128)(2,1)} %fusion.4), calls=%async_computation.4 | async-start | bytes 524288 | tf_op jit(solution)/shard_map/all_to_all | solution.py:264
  174.7 1.5 collective-permute-start.1
  176.2 7.6 %all-to-all-done.4 = bf16[8,32,512]{2,1,0:T(8,128)(2,1)S(1)} async-done(((bf16[8,32,512]{2,1,0:T(8,128)(2,1)}), bf16[8,32,512]{2,1,0:T(8,128)(2,1)S(1)}, u32[]{:S(2)}, u32[]{:S(2)}) %all-to-all-start.4) | async-done | bytes 262176 | tf_op jit(solution)/shard_map/all_to_all | solution.py:264
  183.8 1.6 collective-permute-start.3
  185.4 2.0 %add_multiply_fusion = f32[96,512]{1,0:T(8,128)} fusion(bf16[96,512]{1,0:T(8,128)(2,1)S(1)} %collective-permute-done.1, bf16[8,96,512]{2,1,0:T(8,128)(2,1)} %all-to-all-done.3), kind=kLoop, calls=%fused_computation.17 | loop fusion | flops 983040 | bytes 1081344 | tf_op jit(solution)/shard_map/mul | solution.py:271
  (65 shorter events, 12.1 us)
Async XLA Ops:
  0.6 1.2 copy-start.5
  10.8 1.2 copy-start.2
  11.9 1.0 copy-start.14
  12.9 43.1 %all-to-all-start = ((bf16[16,8,8,768]{3,2,1,0:T(8,128)(2,1)}), bf16[16,8,8,768]{3,2,1,0:T(8,128)(2,1)}, u32[]{:S(2)}, u32[]{:S(2)}) async-start(bf16[16,8,8,768]{3,2,1,0:T(8,128)(2,1)} %bitcast.4), calls=%async_computation | async-start | bytes 3145728 | tf_op jit(solution)/shard_map/all_to_all | solution.py:323
  20.3 1.7 copy-start.24
  22.1 32.2 %copy-start.1 = (bf16[512,1536]{0,1:T(8,128)(2,1)}, bf16[512,1536]{0,1:T(8,128)(2,1)S(1)}, u32[]{:S(2)}) copy-start(bf16[512,1536]{0,1:T(8,128)(2,1)S(1)} %copy.20) | copy-start | bytes 4718596
  22.2 1.6 copy-start.15
  55.0 1.0 copy-start.16
  56.0 6.1 %copy-start.25 = (s32[8,8]{1,0:T(8,128)S(1)}, s32[8,8]{1,0:T(8,128)}, u32[]{:S(2)}) copy-start(s32[8,8]{1,0:T(8,128)} %param.16) | copy-start | bytes 772
  56.0 38.1 %all-to-all-start.1 = ((bf16[16,8,8,768]{3,2,1,0:T(8,128)(2,1)}), bf16[16,8,8,768]{3,2,1,0:T(8,128)(2,1)S(1)}, u32[]{:S(2)}, u32[]{:S(2)}) async-start(bf16[16,8,8,768]{3,2,1,0:T(8,128)(2,1)} %bitcast.64), calls=%async_computation.1 | async-start | bytes 3145728 | tf_op jit(solution)/shard_map/all_to_all | solution.py:323
  74.7 0.8 copy-start.7
  84.6 0.9 copy-start.3
  94.1 14.7 %copy-start.8 = (bf16[1024,256]{1,0:T(8,128)(2,1)S(1)}, bf16[1024,256]{1,0:T(8,128)(2,1)}, u32[]{:S(2)}) copy-start(bf16[1024,256]{1,0:T(8,128)(2,1)} %copy-done.7) | copy-start | bytes 1572868
  105.9 1.1 copy-start.18
  107.1 1.0 copy-start.20
  108.0 0.8 copy-start.22
  109.9 9.3 %copy-start.19 = (bf16[768,1024]{1,0:T(8,128)(2,1)S(1)}, bf16[768,1024]{1,0:T(8,128)(2,1)}, u32[]{:S(2)}) copy-start(bf16[768,1024]{1,0:T(8,128)(2,1)} %copy-done.18) | copy-start | bytes 4718596
  109.9 32.3 %all-to-all-start.2 = ((bf16[16,128,256]{2,1,0:T(8,128)(2,1)}), bf16[16,128,256]{2,1,0:T(8,128)(2,1)}, u32[]{:S(2)}, u32[]{:S(2)}) async-start(bf16[16,128,256]{2,1,0:T(8,128)(2,1)} %pad_maximum_fusion.1), calls=%async_computation.2 | async-start | bytes 2097152 | tf_op jit(solution)/shard_map/all_to_all | solution.py:422
  119.2 1.2 copy-start.21
  120.5 1.0 copy-start.23
  121.5 9.0 %copy-start.4 = (bf16[768,512]{1,0:T(8,128)(2,1)S(1)}, bf16[768,512]{1,0:T(8,128)(2,1)}, u32[]{:S(2)}) copy-start(bf16[768,512]{1,0:T(8,128)(2,1)} %copy-done.3) | copy-start | bytes 2359300
  131.0 2.4 %collective-permute-start = (bf16[8,96,512]{2,1,0:T(8,128)(2,1)S(1)}, bf16[8,96,512]{2,1,0:T(8,128)(2,1)S(1)}, u32[]{:S(2)}, u32[]{:S(2)}) collective-permute-start(bf16[8,96,512]{2,1,0:T(8,128)(2,1)S(1)} %select_bitcast_fusion), channel_id=1, source_target_pairs={{0,1},{1,0},{2,3},{3,2},{4,5},{5,4},{6,7},{7,6},{8,9},{9,8},{10,11... | collective-permute-start | bytes 2359304 | tf_op jit(solution)/shard_map/ppermute | solution.py:257
  133.3 15.6 %copy-start = (bf16[1,256,8,512]{3,2,1,0:T(8,128)(2,1)S(1)}, bf16[1,256,8,512]{3,2,1,0:T(8,128)(2,1)}, u32[]{:S(2)}) copy-start(bf16[1,256,8,512]{3,2,1,0:T(8,128)(2,1)} %param.9) | copy-start | bytes 6291460
  134.6 14.4 %copy-start.13 = (f32[512]{0:T(512)S(1)}, f32[512]{0:T(512)}, u32[]{:S(2)}) copy-start(f32[512]{0:T(512)} %param.11) | copy-start | bytes 6148
  142.2 27.5 %all-to-all-start.3 = ((bf16[8,96,512]{2,1,0:T(8,128)(2,1)}), bf16[8,96,512]{2,1,0:T(8,128)(2,1)}, u32[]{:S(2)}, u32[]{:S(2)}) async-start(bf16[8,96,512]{2,1,0:T(8,128)(2,1)} %fusion), calls=%async_computation.3 | async-start | bytes 1572864 | tf_op jit(solution)/shard_map/all_to_all | solution.py:264
  149.0 1.0 copy-start.6
  150.0 1.2 copy-start.17
  151.3 7.4 %copy-start.10 = (bf16[512,256]{1,0:T(8,128)(2,1)S(1)}, bf16[512,256]{1,0:T(8,128)(2,1)}, u32[]{:S(2)}) copy-start(bf16[512,256]{1,0:T(8,128)(2,1)} %copy-done.9) | copy-start | bytes 786436
  158.8 1.6 collective-permute-start.2
  171.0 12.8 %all-to-all-start.4 = ((bf16[8,32,512]{2,1,0:T(8,128)(2,1)}), bf16[8,32,512]{2,1,0:T(8,128)(2,1)S(1)}, u32[]{:S(2)}, u32[]{:S(2)}) async-start(bf16[8,32,512]{2,1,0:T(8,128)(2,1)} %fusion.4), calls=%async_computation.4 | async-start | bytes 524288 | tf_op jit(solution)/shard_map/all_to_all | solution.py:264
  174.7 10.7 %collective-permute-start.1 = (bf16[96,512]{1,0:T(8,128)(2,1)S(1)}, bf16[96,512]{1,0:T(8,128)(2,1)S(1)}, u32[]{:S(2)}, u32[]{:S(2)}) collective-permute-start(bf16[96,512]{1,0:T(8,128)(2,1)S(1)} %fusion.5), channel_id=1, source_target_pairs={{0,16},{16,0},{1,17},{17,1},{2,18},{18,2},{3,19},{19,3},{4,20},{20... | collective-permute-start | bytes 294920 | tf_op jit(solution)/shard_map/ppermute | solution.py:267
  183.8 4.0 %collective-permute-start.3 = (bf16[32,512]{1,0:T(8,128)(2,1)S(1)}, bf16[32,512]{1,0:T(8,128)(2,1)S(1)}, u32[]{:S(2)}, u32[]{:S(2)}) collective-permute-start(bf16[32,512]{1,0:T(8,128)(2,1)S(1)} %fusion.6), channel_id=1, source_target_pairs={{0,16},{16,0},{1,17},{17,1},{2,18},{18,2},{3,19},{19,3},{4,20},{20... | collective-permute-start | bytes 98312 | tf_op jit(solution)/shard_map/ppermute | solution.py:267
  (3 other events, 2.1 us)

commit v4 on v3

--- a/solution.py
+++ b/solution.py
@@ -89,12 +89,15 @@
     normed[...] = n
     grad = dot(cot[...], w_out[...], 1, 1).astype(BF16)
     grad_space[...] = grad[:, :half]
-    for s in range(tokens.shape[0] // share // 2):
-        for which, send in enumerate((first, second)):
-            to = slice(s * share, (s + 1) * share)
-            at = slice((2 * s + which) * share, (2 * s + which + 1) * share)
+    both = sum(share)
+    for s in range(tokens.shape[0] // both):
+        start = s * both
+        for size, send in zip(share, (first, second)):
+            to = slice(s * size, (s + 1) * size)
+            at = slice(start, start + size)
             send[to, :width] = n[at, :]
             send[to, width:] = grad[at, half:]
+            start += size
 
 
 def space_kernel(
@@ -293,9 +296,10 @@
     allowed = jnp.dot(jnp.dot(onehot, temporal_mask.astype(F32)), onehot.T).T
     w_rows = w_qkv.T
 
-    owned_half = owned // 2
-    share = owned_half * local
-    some = count // 2
+    step = max(1, 16 // local)
+    owned_first = owned * 5 // 8 // step * step
+    portions = (owned_first, owned - owned_first)
+    share = tuple(portion * local for portion in portions)
     normed, grad_space, send_first, send_second = pl.pallas_call(
         functools.partial(prepare_kernel, share),
         grid=(steps,),
@@ -305,11 +309,12 @@
         ],
         out_specs=[
             rows_of(tile, width), rows_of(tile, half),
-            rows_of(tile // 2, width + half), rows_of(tile // 2, width + half),
+            rows_of(tile // (owned * local) * share[0], width + half),
+            rows_of(tile // (owned * local) * share[1], width + half),
         ],
         out_shape=[
             shape(count, width), shape(count, half),
-            shape(some, width + half), shape(some, width + half),
+            shape(groups * share[0], width + half), shape(groups * share[1], width + half),
         ],
         compiler_params=params(),
         cost_estimate=pl.CostEstimate(
@@ -319,16 +324,16 @@
 
     direct = local % 8 == 0
 
-    def to_electrodes(send):
+    def to_electrodes(send, portion):
         recv = lax.all_to_all(
-            send.reshape(groups, owned_half, local, width + half), "seq",
+            send.reshape(groups, portion, local, width + half), "seq",
             split_axis=0, concat_axis=0,
         )
         if not direct:
             recv = jnp.swapaxes(recv, 0, 1)
-        return recv.reshape(some, width + half)
-
-    recv_first = to_electrodes(send_first)
+        return recv.reshape(portion * length, width + half)
+
+    recv_first = to_electrodes(send_first, portions[0])
 
     space_out, grad_qkv_space, grad_out_space = pl.pallas_call(
         functools.partial(space_kernel, local),
@@ -356,11 +361,12 @@
     recv_first, send_second, space_out = lax.optimization_barrier(
         (recv_first, send_second, space_out)
     )
-    recv_second = to_electrodes(send_second)
-
-    def time_forward(recv):
+    recv_second = to_electrodes(send_second, portions[1])
+
+    def time_forward(recv, portion):
+        some = portion * length
         return pl.pallas_call(
-            functools.partial(time_forward_kernel, owned_half, local, direct),
+            functools.partial(time_forward_kernel, portion, local, direct),
             grid=(1,),
             in_specs=[
                 full((some, width + half)),
@@ -375,8 +381,8 @@
                 shape(some, half), shape(some, width), shape(half, some), shape(3 * half, some),
             ],
             scratch_shapes=[
-                pltpu.VMEM((owned_half, length, width + half), F32),
-                pltpu.VMEM((owned_half, length, half), F32),
+                pltpu.VMEM((portion, length, width + half), F32),
+                pltpu.VMEM((portion, length, half), F32),
             ],
             compiler_params=params(),
             cost_estimate=pl.CostEstimate(
@@ -385,9 +391,9 @@
             ),
         )(recv, w_rows, allowed)
 
-    pair = 2 * length if owned_half % 2 == 0 else length
-
     def time_backward(normed_time, grad_time, qkv_time):
+        some = normed_time.shape[0]
+        pair = 2 * length if some % (2 * length) == 0 else length
         return pl.pallas_call(
             functools.partial(time_backward_kernel, length),
             grid=(some // pair,),
@@ -405,20 +411,20 @@
             ),
         )(normed_time, grad_time, qkv_time, allowed)
 
-    time_first, *kept_first = time_forward(recv_first)
+    time_first, *kept_first = time_forward(recv_first, portions[0])
+    recv_second, time_first = lax.optimization_barrier((recv_second, time_first))
+    time_second, *kept_second = time_forward(recv_second, portions[1])
+    time_second, kept_first = lax.optimization_barrier((time_second, kept_first))
     grad_qkv_first = time_backward(*kept_first)
-    recv_second, time_first, grad_qkv_first = lax.optimization_barrier(
-        (recv_second, time_first, grad_qkv_first)
+
+    def by_group(out, portion):
+        if not direct:
+            out = jnp.swapaxes(out.reshape(portion, groups, local, half), 0, 1)
+        return out.reshape(groups, portion * local, half)
+
+    back = jnp.concatenate(
+        [by_group(time_first, portions[0]), by_group(time_second, portions[1])], axis=1
     )
-    time_second, *kept_second = time_forward(recv_second)
-
-    def by_group(out):
-        if direct:
-            return out.reshape(groups, share, half)
-        back = jnp.swapaxes(out.reshape(owned_half, groups, local, half), 0, 1)
-        return back.reshape(groups, share, half)
-
-    back = jnp.concatenate([by_group(time_first), by_group(time_second)], axis=1)
     time_back = lax.all_to_all(back, "seq", split_axis=0, concat_axis=0).reshape(count, half)
     grad_qkv_second = time_backward(*kept_second)
     grad_qkv_time = (grad_qkv_first.astype(F32) + grad_qkv_second.astype(F32)).astype(BF16)

time: 190 us -> 187 us (0.984)
  waiting for transfers between devices: 36.3 us -> 29.3 us
  local copies, waits for them, and re-layouts: 18.3 us -> 20.3 us
  starting transfers between devices: 36.8 us -> 38.8 us
    all_to_all x1, waiting for transfers between devices: 7.65 us -> 0.01 us  [shards(): lax.all_to_all(back, 'seq', split_axis=0, concat_axis=0)]
    all_to_all x2, starting transfers between devices: 13.5 us -> 18.1 us  [to_electrodes(): lax.all_to_all(send.reshape(groups, portion, local, width + half), 'seq',...]
    unnamed x53 -> x59, local copies, waits for them, and re-layouts: 17.7 us -> 19.8 us
  transfers between devices with their start and end apart: 9 -> 9, of which waited for: 7 -> 7; matrix products, arithmetic and copies ran while one was open for 4% -> 4% of each run, Pallas kernels for 36% -> 38%
where the time goes in v4:
time: 187 us; the launch traced here: 186 us
  Pallas kernels  87.4 us (47%)
  starting transfers between devices  38.8 us (21%)
  waiting for transfers between devices  29.3 us (16%)
  local copies, waits for them, and re-layouts  20.3 us (11%)
  other arithmetic  8.39 us (4%)
    pallas_call x1, Pallas kernels, shards(): pl.pallas_call(functools.partial(space_kernel, local), grid=(local,), in_...  30.4 us
    pallas_call x2, Pallas kernels, time_forward(): pl.pallas_call(functools.partial(time_forward_kernel, portion, local, dir...  24.1 us
    unnamed x59, local copies, waits for them, and re-layouts  19.8 us
    all_to_all x2, starting transfers between devices, to_electrodes(): lax.all_to_all(send.reshape(groups, portion, local, width + half), 'seq',...  18.1 us
    pallas_call x2, Pallas kernels, time_backward(): pl.pallas_call(functools.partial(time_backward_kernel, length), grid=(som...  17.8 us
    all_to_all x2, waiting for transfers between devices, reduce_pairs(): lax.all_to_all(both, 'seq', split_axis=0, concat_axis=0, axis_index_group...  15.9 us
    all_to_all x2, starting transfers between devices, reduce_pairs(): lax.all_to_all(both, 'seq', split_axis=0, concat_axis=0, axis_index_group...  9.57 us
    all_to_all x2, waiting for transfers between devices, to_electrodes(): lax.all_to_all(send.reshape(groups, portion, local, width + half), 'seq',...  9.53 us
  transfers between devices with their start and end apart: 9, of which 7 were waited for; matrix products, arithmetic and copies ran while one was open for 4% of the time, Pallas kernels for 38%

profile of v4, /device:TPU:0, one launch (start us, length us, event | category | flops | bytes accessed | tf_op | source)
XLA Modules:
  0.0 185.6 jit_solution(1554780777814951665)
XLA Ops:
  3.2 7.6 %shard_map.112 = (bf16[2048,512]{1,0:T(8,128)(2,1)}, bf16[2048,256]{1,0:T(8,128)(2,1)S(1)}, bf16[1280,768]{1,0:T(8,128)(2,1)}, bf16[768,768]{1,0:T(8,128)(2,1)S(1)}) custom-call(bf16[2048,512]{1,0:T(8,128)(2,1)} %bitcast.59, f32[2048,1]{1,0:T(8,128)S(1)} %convert_element_type.200.mask, f32[1,512]{1,0:T(1,128)S(1)} %bitcast.70, f32[1,512]{1,0:T(1,128)S(1)} %bitcast.69, ...), custom_call_target="tpu_custom_call" | custom-call | flops 1073741824 | bytes 9437184 | tf_op jit(solution)/shard_map/pallas_call | solution.py:303
  12.9 7.4 %all-to-all-start = ((bf16[16,10,8,768]{3,2,1,0:T(8,128)(2,1)}), bf16[16,10,8,768]{3,2,1,0:T(8,128)(2,1)}, u32[]{:S(2)}, u32[]{:S(2)}) async-start(bf16[16,10,8,768]{3,2,1,0:T(8,128)(2,1)} %bitcast.4), calls=%async_computation | async-start | bytes 3932160 | tf_op jit(solution)/shard_map/all_to_all | solution.py:328
  20.3 1.7 copy.20
  22.2 1.2 copy-done.12
  23.4 30.4 %shard_map.113 = (bf16[2048,256]{1,0:T(8,128)(2,1)S(1)}, bf16[768,512]{1,0:T(8,128)(2,1)S(1)}, bf16[512,256]{1,0:T(8,128)(2,1)S(1)}) custom-call(bf16[2048,512]{1,0:T(8,128)(2,1)} %get-tuple-element.34.normed, bf16[2048,256]{1,0:T(8,128)(2,1)S(1)} %copy-done.12, bf16[2048,512]{1,0:T(8,128)(2,1)} %bitcast.77, bf16[1536,512]{1,0:T(8,128)(2,1)S(1)} %bitcast.61, ...), custom_call_target="tpu_custom_call" | custom-call | flops 17179869184 | bytes 8388608 | tf_op jit(solution)/shard_map/pallas_call | solution.py:338
  55.6 3.6 %all-to-all-done = bf16[16,10,8,768]{3,2,1,0:T(8,128)(2,1)} async-done(((bf16[16,10,8,768]{3,2,1,0:T(8,128)(2,1)}), bf16[16,10,8,768]{3,2,1,0:T(8,128)(2,1)}, u32[]{:S(2)}, u32[]{:S(2)}) %all-to-all-start) | async-done | bytes 1966112 | tf_op jit(solution)/shard_map/all_to_all | solution.py:328
  59.2 10.7 %all-to-all-start.1 = ((bf16[16,6,8,768]{3,2,1,0:T(8,128)(2,1)}), bf16[16,6,8,768]{3,2,1,0:T(8,128)(2,1)}, u32[]{:S(2)}, u32[]{:S(2)}) async-start(bf16[16,6,8,768]{3,2,1,0:T(8,128)(2,1)} %bitcast.64), calls=%async_computation.1 | async-start | bytes 2359296 | tf_op jit(solution)/shard_map/all_to_all | solution.py:328
  70.3 14.8 %shard_map.114 = (bf16[1280,256]{1,0:T(8,128)(2,1)S(1)}, bf16[1280,512]{1,0:T(8,128)(2,1)S(1)}, bf16[256,1280]{1,0:T(8,128)(2,1)S(1)}, bf16[768,1280]{1,0:T(8,128)(2,1)S(1)}) custom-call(bf16[1280,768]{1,0:T(8,128)(2,1)} %bitcast.5.recv, bf16[1536,512]{1,0:T(8,128)(2,1)S(1)} %bitcast.62, f32[128,128]{1,0:T(8,128)S(1)} %fusion.1.allowed), custom_call_target="tpu_custom_call" | custom-call | flops 5368709120 | bytes 5242880 | tf_op jit(solution)/shard_map/pallas_call | solution.py:368
  86.0 1.3 copy-done.19
  87.2 1.1 copy-done.21
  89.2 6.0 %all-to-all-done.1 = bf16[16,6,8,768]{3,2,1,0:T(8,128)(2,1)} async-done(((bf16[16,6,8,768]{3,2,1,0:T(8,128)(2,1)}), bf16[16,6,8,768]{3,2,1,0:T(8,128)(2,1)}, u32[]{:S(2)}, u32[]{:S(2)}) %all-to-all-start.1) | async-done | bytes 1179680 | tf_op jit(solution)/shard_map/all_to_all | solution.py:328
  95.1 9.3 %shard_map.115 = (bf16[768,256]{1,0:T(8,128)(2,1)S(1)}, bf16[768,512]{1,0:T(8,128)(2,1)S(1)}, bf16[256,768]{1,0:T(8,128)(2,1)S(1)}, bf16[768,768]{1,0:T(8,128)(2,1)S(1)}) custom-call(bf16[768,768]{1,0:T(8,128)(2,1)} %bitcast.10.recv, bf16[1536,512]{1,0:T(8,128)(2,1)S(1)} %bitcast.63, f32[128,128]{1,0:T(8,128)S(1)} %fusion.1.allowed), custom_call_target="tpu_custom_call" | custom-call | flops 3221225472 | bytes 3145728 | tf_op jit(solution)/shard_map/pallas_call | solution.py:368
  104.4 1.0 copy-done.15
  107.2 1.1 pad_maximum_fusion.1
  108.3 7.5 %all-to-all-start.2 = ((bf16[16,128,256]{2,1,0:T(8,128)(2,1)}), bf16[16,128,256]{2,1,0:T(8,128)(2,1)}, u32[]{:S(2)}, u32[]{:S(2)}) async-start(bf16[16,128,256]{2,1,0:T(8,128)(2,1)} %pad_maximum_fusion.1), calls=%async_computation.2 | async-start | bytes 2097152 | tf_op jit(solution)/shard_map/all_to_all | solution.py:428
  115.8 1.5 copy-done.20
  117.4 1.1 copy-done.26
  118.5 11.1 %shard_map.116 = bf16[768,512]{1,0:T(8,128)(2,1)S(1)} custom-call(bf16[1280,512]{1,0:T(8,128)(2,1)S(1)} %copy-done.22, bf16[256,1280]{1,0:T(8,128)(2,1)S(1)} %copy-done.26, bf16[768,1280]{1,0:T(8,128)(2,1)S(1)} %copy-done.20, f32[128,128]{1,0:T(8,128)S(1)} %fusion.1.allowed), custom_call_target="tpu_custom_call" | custom-call | flops 8053063680 | bytes 5242880 | tf_op jit(solution)/shard_map/pallas_call | solution.py:397
  129.6 6.7 %shard_map.117 = bf16[768,512]{1,0:T(8,128)(2,1)S(1)} custom-call(bf16[768,512]{1,0:T(8,128)(2,1)S(1)} %copy-done.18, bf16[256,768]{1,0:T(8,128)(2,1)S(1)} %copy-done.24, bf16[768,768]{1,0:T(8,128)(2,1)S(1)} %copy-done.16, f32[128,128]{1,0:T(8,128)S(1)} %fusion.1.allowed), custom_call_target="tpu_custom_call" | custom-call | flops 4831838208 | bytes 3145728 | tf_op jit(solution)/shard_map/pallas_call | solution.py:397
  137.2 1.9 %collective-permute-done = bf16[8,96,512]{2,1,0:T(8,128)(2,1)S(1)} collective-permute-done((bf16[8,96,512]{2,1,0:T(8,128)(2,1)S(1)}, bf16[8,96,512]{2,1,0:T(8,128)(2,1)S(1)}, u32[]{:S(2)}, u32[]{:S(2)}) %collective-permute-start) | collective-permute-done | bytes 786464 | tf_op jit(solution)/shard_map/ppermute | solution.py:260
  139.1 1.2 fusion
  140.3 6.0 %all-to-all-start.3 = ((bf16[8,96,512]{2,1,0:T(8,128)(2,1)}), bf16[8,96,512]{2,1,0:T(8,128)(2,1)}, u32[]{:S(2)}, u32[]{:S(2)}) async-start(bf16[8,96,512]{2,1,0:T(8,128)(2,1)} %fusion), calls=%async_computation.3 | async-start | bytes 1572864 | tf_op jit(solution)/shard_map/all_to_all | solution.py:267
  147.3 1.2 copy-done.14
  148.6 7.4 %shard_map.118 = (bf16[2048,512]{1,0:T(8,128)(2,1)}, bf16[512,256]{1,0:T(8,128)(2,1)S(1)}) custom-call(bf16[2048,512]{1,0:T(8,128)(2,1)S(1)} %bitcast.60, f32[2048,1]{1,0:T(8,128)S(1)} %convert_element_type.200.mask, f32[1,512]{1,0:T(1,128)S(1)} %bitcast.71, bf16[2048,256]{1,0:T(8,128)(2,1)S(1)} %copy-done.14, bf16[2048,256]{1,0:T(8,128)(2,1)} %bitcast.13.time, ...), custom_call_target="tpu_custom_call" | custom-call | flops 2147483648 | bytes 8388608 | tf_op jit(solution)/shard_map/pallas_call | solution.py:436
  156.1 1.5 collective-permute-done.2
  158.5 8.4 %all-to-all-done.3 = bf16[8,96,512]{2,1,0:T(8,128)(2,1)} async-done(((bf16[8,96,512]{2,1,0:T(8,128)(2,1)}), bf16[8,96,512]{2,1,0:T(8,128)(2,1)}, u32[]{:S(2)}, u32[]{:S(2)}) %all-to-all-start.3) | async-done | bytes 786464 | tf_op jit(solution)/shard_map/all_to_all | solution.py:267
  166.8 1.3 fusion.5
  168.2 3.6 %all-to-all-start.4 = ((bf16[8,32,512]{2,1,0:T(8,128)(2,1)}), bf16[8,32,512]{2,1,0:T(8,128)(2,1)S(1)}, u32[]{:S(2)}, u32[]{:S(2)}) async-start(bf16[8,32,512]{2,1,0:T(8,128)(2,1)} %fusion.4), calls=%async_computation.4 | async-start | bytes 524288 | tf_op jit(solution)/shard_map/all_to_all | solution.py:267
  171.8 1.5 collective-permute-start.1
  173.3 7.6 %all-to-all-done.4 = bf16[8,32,512]{2,1,0:T(8,128)(2,1)S(1)} async-done(((bf16[8,32,512]{2,1,0:T(8,128)(2,1)}), bf16[8,32,512]{2,1,0:T(8,128)(2,1)S(1)}, u32[]{:S(2)}, u32[]{:S(2)}) %all-to-all-start.4) | async-done | bytes 262176 | tf_op jit(solution)/shard_map/all_to_all | solution.py:267
  180.9 1.6 collective-permute-start.3
  182.5 2.0 %add_multiply_fusion = f32[96,512]{1,0:T(8,128)} fusion(bf16[96,512]{1,0:T(8,128)(2,1)S(1)} %collective-permute-done.1, bf16[8,96,512]{2,1,0:T(8,128)(2,1)} %all-to-all-done.3), kind=kLoop, calls=%fused_computation.17 | loop fusion | flops 983040 | bytes 1081344 | tf_op jit(solution)/shard_map/mul | solution.py:274
  (71 shorter events, 14.1 us)
Async XLA Ops:
  0.6 1.2 copy-start.4
  10.8 1.0 copy-start.1
  11.9 1.0 copy-start.11
  12.9 46.3 %all-to-all-start = ((bf16[16,10,8,768]{3,2,1,0:T(8,128)(2,1)}), bf16[16,10,8,768]{3,2,1,0:T(8,128)(2,1)}, u32[]{:S(2)}, u32[]{:S(2)}) async-start(bf16[16,10,8,768]{3,2,1,0:T(8,128)(2,1)} %bitcast.4), calls=%async_computation | async-start | bytes 3932160 | tf_op jit(solution)/shard_map/all_to_all | solution.py:328
  20.3 1.7 copy-start.27
  22.2 1.2 copy-start.12
  54.6 1.0 copy-start.13
  55.6 14.3 %copy-start.28 = (s32[8,8]{1,0:T(8,128)S(1)}, s32[8,8]{1,0:T(8,128)}, u32[]{:S(2)}) copy-start(s32[8,8]{1,0:T(8,128)} %param.16) | copy-start | bytes 772
  59.2 35.9 %all-to-all-start.1 = ((bf16[16,6,8,768]{3,2,1,0:T(8,128)(2,1)}), bf16[16,6,8,768]{3,2,1,0:T(8,128)(2,1)}, u32[]{:S(2)}, u32[]{:S(2)}) async-start(bf16[16,6,8,768]{3,2,1,0:T(8,128)(2,1)} %bitcast.64), calls=%async_computation.1 | async-start | bytes 2359296 | tf_op jit(solution)/shard_map/all_to_all | solution.py:328
  86.0 1.3 copy-start.19
  87.2 1.1 copy-start.21
  95.1 12.0 %copy-start.3 = (bf16[1280,256]{1,0:T(8,128)(2,1)S(1)}, bf16[1280,256]{1,0:T(8,128)(2,1)}, u32[]{:S(2)}) copy-start(bf16[1280,256]{1,0:T(8,128)(2,1)} %copy-done.2) | copy-start | bytes 1966084
  104.4 1.1 copy-start.15
  105.5 0.9 copy-start.17
  107.1 8.7 %copy-start.22 = (bf16[1280,512]{1,0:T(8,128)(2,1)S(1)}, bf16[1280,512]{1,0:T(8,128)(2,1)}, u32[]{:S(2)}) copy-start(bf16[1280,512]{1,0:T(8,128)(2,1)} %copy-done.21) | copy-start | bytes 3932164
  108.3 32.1 %all-to-all-start.2 = ((bf16[16,128,256]{2,1,0:T(8,128)(2,1)}), bf16[16,128,256]{2,1,0:T(8,128)(2,1)}, u32[]{:S(2)}, u32[]{:S(2)}) async-start(bf16[16,128,256]{2,1,0:T(8,128)(2,1)} %pad_maximum_fusion.1), calls=%async_computation.2 | async-start | bytes 2097152 | tf_op jit(solution)/shard_map/all_to_all | solution.py:428
  115.8 1.5 copy-start.20
  117.4 1.1 copy-start.26
  118.5 11.1 %copy-start.16 = (bf16[768,768]{1,0:T(8,128)(2,1)S(1)}, bf16[768,768]{1,0:T(8,128)(2,1)}, u32[]{:S(2)}) copy-start(bf16[768,768]{1,0:T(8,128)(2,1)} %copy-done.15) | copy-start | bytes 3538948
  118.5 11.1 %copy-start.18 = (bf16[768,512]{1,0:T(8,128)(2,1)S(1)}, bf16[768,512]{1,0:T(8,128)(2,1)}, u32[]{:S(2)}) copy-start(bf16[768,512]{1,0:T(8,128)(2,1)} %copy-done.17) | copy-start | bytes 2359300
  118.5 11.1 %copy-start.24 = (bf16[256,768]{1,0:T(8,128)(2,1)S(1)}, bf16[256,768]{1,0:T(8,128)(2,1)}, u32[]{:S(2)}) copy-start(bf16[256,768]{1,0:T(8,128)(2,1)} %copy-done.23) | copy-start | bytes 1179652
  136.7 2.4 %collective-permute-start = (bf16[8,96,512]{2,1,0:T(8,128)(2,1)S(1)}, bf16[8,96,512]{2,1,0:T(8,128)(2,1)S(1)}, u32[]{:S(2)}, u32[]{:S(2)}) collective-permute-start(bf16[8,96,512]{2,1,0:T(8,128)(2,1)S(1)} %select_bitcast_fusion), channel_id=1, source_target_pairs={{0,1},{1,0},{2,3},{3,2},{4,5},{5,4},{6,7},{7,6},{8,9},{9,8},{10,11... | collective-permute-start | bytes 2359304 | tf_op jit(solution)/shard_map/ppermute | solution.py:260
  139.1 7.2 %copy-start = (bf16[1,256,8,512]{3,2,1,0:T(8,128)(2,1)S(1)}, bf16[1,256,8,512]{3,2,1,0:T(8,128)(2,1)}, u32[]{:S(2)}) copy-start(bf16[1,256,8,512]{3,2,1,0:T(8,128)(2,1)} %param.9) | copy-start | bytes 6291460
  140.3 6.0 %copy-start.10 = (f32[512]{0:T(512)S(1)}, f32[512]{0:T(512)}, u32[]{:S(2)}) copy-start(f32[512]{0:T(512)} %param.11) | copy-start | bytes 6148
  140.3 26.5 %all-to-all-start.3 = ((bf16[8,96,512]{2,1,0:T(8,128)(2,1)}), bf16[8,96,512]{2,1,0:T(8,128)(2,1)}, u32[]{:S(2)}, u32[]{:S(2)}) async-start(bf16[8,96,512]{2,1,0:T(8,128)(2,1)} %fusion), calls=%async_computation.3 | async-start | bytes 1572864 | tf_op jit(solution)/shard_map/all_to_all | solution.py:267
  146.3 1.0 copy-start.5
  147.3 1.2 copy-start.14
  148.6 7.4 %copy-start.7 = (bf16[512,256]{1,0:T(8,128)(2,1)S(1)}, bf16[512,256]{1,0:T(8,128)(2,1)}, u32[]{:S(2)}) copy-start(bf16[512,256]{1,0:T(8,128)(2,1)} %copy-done.6) | copy-start | bytes 786436
  156.1 1.6 collective-permute-start.2
  168.2 12.7 %all-to-all-start.4 = ((bf16[8,32,512]{2,1,0:T(8,128)(2,1)}), bf16[8,32,512]{2,1,0:T(8,128)(2,1)S(1)}, u32[]{:S(2)}, u32[]{:S(2)}) async-start(bf16[8,32,512]{2,1,0:T(8,128)(2,1)} %fusion.4), calls=%async_computation.4 | async-start | bytes 524288 | tf_op jit(solution)/shard_map/all_to_all | solution.py:267
  171.8 10.7 %collective-permute-start.1 = (bf16[96,512]{1,0:T(8,128)(2,1)S(1)}, bf16[96,512]{1,0:T(8,128)(2,1)S(1)}, u32[]{:S(2)}, u32[]{:S(2)}) collective-permute-start(bf16[96,512]{1,0:T(8,128)(2,1)S(1)} %fusion.5), channel_id=1, source_target_pairs={{0,16},{16,0},{1,17},{17,1},{2,18},{18,2},{3,19},{19,3},{4,20},{20... | collective-permute-start | bytes 294920 | tf_op jit(solution)/shard_map/ppermute | solution.py:270
  180.9 4.0 %collective-permute-start.3 = (bf16[32,512]{1,0:T(8,128)(2,1)S(1)}, bf16[32,512]{1,0:T(8,128)(2,1)S(1)}, u32[]{:S(2)}, u32[]{:S(2)}) collective-permute-start(bf16[32,512]{1,0:T(8,128)(2,1)S(1)} %fusion.6), channel_id=1, source_target_pairs={{0,16},{16,0},{1,17},{17,1},{2,18},{18,2},{3,19},{19,3},{4,20},{20... | collective-permute-start | bytes 98312 | tf_op jit(solution)/shard_map/ppermute | solution.py:270
  (6 other events, 4.6 us)

commit v5 on v4

--- a/solution.py
+++ b/solution.py
@@ -71,10 +71,6 @@
     at = h * HEAD_DIM
     q, k, v = [qkv[part * half + at : part * half + at + HEAD_DIM, :] for part in range(3)]
     return (q.astype(F32) * (HEAD_DIM**-0.5)).astype(BF16), k, v
-
-
-def transposed(value):
-    return value.astype(F32).T.astype(BF16)
 
 
 def prepare_kernel(
@@ -160,12 +156,12 @@
     def one(e):
         at = pl.ds(pl.multiple_of(e * length, length), length)
         if direct:
-            block = scr[e].astype(BF16)
+            block = scr[e]
         else:
-            block = recv[at, :]
-        n = block[:, :width]
+            block = recv[at, :].astype(F32)
+        n = block[:, :width].astype(BF16)
         normed[at, :] = n
-        grad[:, at] = transposed(block[:, width:])
+        grad[:, at] = block[:, width:].T.astype(BF16)
         mine = dot(w[...], n, 1, 1).astype(BF16)
         qkv[:, at] = mine
         outs = []
@@ -179,7 +175,7 @@
         else:
             out[at, :] = o.astype(BF16)
 
-    together = 2 if owned % 2 == 0 else 1
+    together = next(n for n in (5, 3, 2, 1) if owned % n == 0)
 
     @pl.loop(0, owned // together)
     def _(i):

time: 187 us -> 185 us (0.989)
  Pallas kernels: 87.4 us -> 83.1 us
  waiting for transfers between devices: 29.3 us -> 32.1 us
    pallas_call x2, Pallas kernels: 24.1 us -> 19.9 us  [time_forward(): pl.pallas_call(functools.partial(time_forward_kernel, portion, local, dir...]
    all_to_all x2, waiting for transfers between devices: 9.53 us -> 12.3 us  [to_electrodes(): lax.all_to_all(send.reshape(groups, portion, local, width + half), 'seq',...]
  transfers between devices with their start and end apart: 9 -> 9, of which waited for: 7 -> 7; matrix products, arithmetic and copies ran while one was open for 4% -> 4% of each run, Pallas kernels for 38% -> 37%
where the time goes in v5:
time: 185 us; the launch traced here: 184 us
  Pallas kernels  83.1 us (45%)
  starting transfers between devices  38.8 us (21%)
  waiting for transfers between devices  32.1 us (17%)
  local copies, waits for them, and re-layouts  20.3 us (11%)
  other arithmetic  8.39 us (5%)
    pallas_call x1, Pallas kernels, shards(): pl.pallas_call(functools.partial(space_kernel, local), grid=(local,), in_...  30.4 us
    pallas_call x2, Pallas kernels, time_forward(): pl.pallas_call(functools.partial(time_forward_kernel, portion, local, dir...  19.9 us
    unnamed x59, local copies, waits for them, and re-layouts  19.8 us
    all_to_all x2, starting transfers between devices, to_electrodes(): lax.all_to_all(send.reshape(groups, portion, local, width + half), 'seq',...  18.1 us
    pallas_call x2, Pallas kernels, time_backward(): pl.pallas_call(functools.partial(time_backward_kernel, length), grid=(som...  17.8 us
    all_to_all x2, waiting for transfers between devices, reduce_pairs(): lax.all_to_all(both, 'seq', split_axis=0, concat_axis=0, axis_index_group...  15.9 us
    all_to_all x2, waiting for transfers between devices, to_electrodes(): lax.all_to_all(send.reshape(groups, portion, local, width + half), 'seq',...  12.3 us
    all_to_all x2, starting transfers between devices, reduce_pairs(): lax.all_to_all(both, 'seq', split_axis=0, concat_axis=0, axis_index_group...  9.57 us
  transfers between devices with their start and end apart: 9, of which 7 were waited for; matrix products, arithmetic and copies ran while one was open for 4% of the time, Pallas kernels for 37%

profile of v5, /device:TPU:0, one launch (start us, length us, event | category | flops | bytes accessed | tf_op | source)
XLA Modules:
  0.0 184.1 jit_solution(5647416696055413993)
XLA Ops:
  3.2 7.6 %shard_map.112 = (bf16[2048,512]{1,0:T(8,128)(2,1)}, bf16[2048,256]{1,0:T(8,128)(2,1)S(1)}, bf16[1280,768]{1,0:T(8,128)(2,1)}, bf16[768,768]{1,0:T(8,128)(2,1)S(1)}) custom-call(bf16[2048,512]{1,0:T(8,128)(2,1)} %bitcast.59, f32[2048,1]{1,0:T(8,128)S(1)} %convert_element_type.200.mask, f32[1,512]{1,0:T(1,128)S(1)} %bitcast.70, f32[1,512]{1,0:T(1,128)S(1)} %bitcast.69, ...), custom_call_target="tpu_custom_call" | custom-call | flops 1073741824 | bytes 9437184 | tf_op jit(solution)/shard_map/pallas_call | solution.py:299
  12.9 7.4 %all-to-all-start = ((bf16[16,10,8,768]{3,2,1,0:T(8,128)(2,1)}), bf16[16,10,8,768]{3,2,1,0:T(8,128)(2,1)}, u32[]{:S(2)}, u32[]{:S(2)}) async-start(bf16[16,10,8,768]{3,2,1,0:T(8,128)(2,1)} %bitcast.4), calls=%async_computation | async-start | bytes 3932160 | tf_op jit(solution)/shard_map/all_to_all | solution.py:324
  20.3 1.7 copy.20
  22.2 1.2 copy-done.12
  23.4 30.4 %shard_map.113 = (bf16[2048,256]{1,0:T(8,128)(2,1)S(1)}, bf16[768,512]{1,0:T(8,128)(2,1)S(1)}, bf16[512,256]{1,0:T(8,128)(2,1)S(1)}) custom-call(bf16[2048,512]{1,0:T(8,128)(2,1)} %get-tuple-element.34.normed, bf16[2048,256]{1,0:T(8,128)(2,1)S(1)} %copy-done.12, bf16[2048,512]{1,0:T(8,128)(2,1)} %bitcast.77, bf16[1536,512]{1,0:T(8,128)(2,1)S(1)} %bitcast.61, ...), custom_call_target="tpu_custom_call" | custom-call | flops 17179869184 | bytes 8388608 | tf_op jit(solution)/shard_map/pallas_call | solution.py:334
  55.6 3.6 %all-to-all-done = bf16[16,10,8,768]{3,2,1,0:T(8,128)(2,1)} async-done(((bf16[16,10,8,768]{3,2,1,0:T(8,128)(2,1)}), bf16[16,10,8,768]{3,2,1,0:T(8,128)(2,1)}, u32[]{:S(2)}, u32[]{:S(2)}) %all-to-all-start) | async-done | bytes 1966112 | tf_op jit(solution)/shard_map/all_to_all | solution.py:324
  59.2 10.7 %all-to-all-start.1 = ((bf16[16,6,8,768]{3,2,1,0:T(8,128)(2,1)}), bf16[16,6,8,768]{3,2,1,0:T(8,128)(2,1)}, u32[]{:S(2)}, u32[]{:S(2)}) async-start(bf16[16,6,8,768]{3,2,1,0:T(8,128)(2,1)} %bitcast.64), calls=%async_computation.1 | async-start | bytes 2359296 | tf_op jit(solution)/shard_map/all_to_all | solution.py:324
  70.3 12.0 %shard_map.114 = (bf16[1280,256]{1,0:T(8,128)(2,1)S(1)}, bf16[1280,512]{1,0:T(8,128)(2,1)S(1)}, bf16[256,1280]{1,0:T(8,128)(2,1)S(1)}, bf16[768,1280]{1,0:T(8,128)(2,1)S(1)}) custom-call(bf16[1280,768]{1,0:T(8,128)(2,1)} %bitcast.5.recv, bf16[1536,512]{1,0:T(8,128)(2,1)S(1)} %bitcast.62, f32[128,128]{1,0:T(8,128)S(1)} %fusion.1.allowed), custom_call_target="tpu_custom_call" | custom-call | flops 5368709120 | bytes 5242880 | tf_op jit(solution)/shard_map/pallas_call | solution.py:364
  83.2 1.3 copy-done.19
  84.4 1.1 copy-done.21
  86.4 8.8 %all-to-all-done.1 = bf16[16,6,8,768]{3,2,1,0:T(8,128)(2,1)} async-done(((bf16[16,6,8,768]{3,2,1,0:T(8,128)(2,1)}), bf16[16,6,8,768]{3,2,1,0:T(8,128)(2,1)}, u32[]{:S(2)}, u32[]{:S(2)}) %all-to-all-start.1) | async-done | bytes 1179680 | tf_op jit(solution)/shard_map/all_to_all | solution.py:324
  95.1 7.9 %shard_map.115 = (bf16[768,256]{1,0:T(8,128)(2,1)S(1)}, bf16[768,512]{1,0:T(8,128)(2,1)S(1)}, bf16[256,768]{1,0:T(8,128)(2,1)S(1)}, bf16[768,768]{1,0:T(8,128)(2,1)S(1)}) custom-call(bf16[768,768]{1,0:T(8,128)(2,1)} %bitcast.10.recv, bf16[1536,512]{1,0:T(8,128)(2,1)S(1)} %bitcast.63, f32[128,128]{1,0:T(8,128)S(1)} %fusion.1.allowed), custom_call_target="tpu_custom_call" | custom-call | flops 3221225472 | bytes 3145728 | tf_op jit(solution)/shard_map/pallas_call | solution.py:364
  103.0 1.0 copy-done.15
  105.7 1.1 pad_maximum_fusion.1
  106.8 7.5 %all-to-all-start.2 = ((bf16[16,128,256]{2,1,0:T(8,128)(2,1)}), bf16[16,128,256]{2,1,0:T(8,128)(2,1)}, u32[]{:S(2)}, u32[]{:S(2)}) async-start(bf16[16,128,256]{2,1,0:T(8,128)(2,1)} %pad_maximum_fusion.1), calls=%async_computation.2 | async-start | bytes 2097152 | tf_op jit(solution)/shard_map/all_to_all | solution.py:424
  114.4 1.5 copy-done.20
  115.9 1.1 copy-done.26
  117.0 11.1 %shard_map.116 = bf16[768,512]{1,0:T(8,128)(2,1)S(1)} custom-call(bf16[1280,512]{1,0:T(8,128)(2,1)S(1)} %copy-done.22, bf16[256,1280]{1,0:T(8,128)(2,1)S(1)} %copy-done.26, bf16[768,1280]{1,0:T(8,128)(2,1)S(1)} %copy-done.20, f32[128,128]{1,0:T(8,128)S(1)} %fusion.1.allowed), custom_call_target="tpu_custom_call" | custom-call | flops 8053063680 | bytes 5242880 | tf_op jit(solution)/shard_map/pallas_call | solution.py:393
  128.1 6.7 %shard_map.117 = bf16[768,512]{1,0:T(8,128)(2,1)S(1)} custom-call(bf16[768,512]{1,0:T(8,128)(2,1)S(1)} %copy-done.18, bf16[256,768]{1,0:T(8,128)(2,1)S(1)} %copy-done.24, bf16[768,768]{1,0:T(8,128)(2,1)S(1)} %copy-done.16, f32[128,128]{1,0:T(8,128)S(1)} %fusion.1.allowed), custom_call_target="tpu_custom_call" | custom-call | flops 4831838208 | bytes 3145728 | tf_op jit(solution)/shard_map/pallas_call | solution.py:393
  135.7 1.9 %collective-permute-done = bf16[8,96,512]{2,1,0:T(8,128)(2,1)S(1)} collective-permute-done((bf16[8,96,512]{2,1,0:T(8,128)(2,1)S(1)}, bf16[8,96,512]{2,1,0:T(8,128)(2,1)S(1)}, u32[]{:S(2)}, u32[]{:S(2)}) %collective-permute-start) | collective-permute-done | bytes 786464 | tf_op jit(solution)/shard_map/ppermute | solution.py:256
  137.7 1.2 fusion
  138.9 6.0 %all-to-all-start.3 = ((bf16[8,96,512]{2,1,0:T(8,128)(2,1)}), bf16[8,96,512]{2,1,0:T(8,128)(2,1)}, u32[]{:S(2)}, u32[]{:S(2)}) async-start(bf16[8,96,512]{2,1,0:T(8,128)(2,1)} %fusion), calls=%async_computation.3 | async-start | bytes 1572864 | tf_op jit(solution)/shard_map/all_to_all | solution.py:263
  145.9 1.2 copy-done.14
  147.1 7.4 %shard_map.118 = (bf16[2048,512]{1,0:T(8,128)(2,1)}, bf16[512,256]{1,0:T(8,128)(2,1)S(1)}) custom-call(bf16[2048,512]{1,0:T(8,128)(2,1)S(1)} %bitcast.60, f32[2048,1]{1,0:T(8,128)S(1)} %convert_element_type.200.mask, f32[1,512]{1,0:T(1,128)S(1)} %bitcast.71, bf16[2048,256]{1,0:T(8,128)(2,1)S(1)} %copy-done.14, bf16[2048,256]{1,0:T(8,128)(2,1)} %bitcast.13.time, ...), custom_call_target="tpu_custom_call" | custom-call | flops 2147483648 | bytes 8388608 | tf_op jit(solution)/shard_map/pallas_call | solution.py:432
  154.7 1.5 collective-permute-done.2
  157.0 8.4 %all-to-all-done.3 = bf16[8,96,512]{2,1,0:T(8,128)(2,1)} async-done(((bf16[8,96,512]{2,1,0:T(8,128)(2,1)}), bf16[8,96,512]{2,1,0:T(8,128)(2,1)}, u32[]{:S(2)}, u32[]{:S(2)}) %all-to-all-start.3) | async-done | bytes 786464 | tf_op jit(solution)/shard_map/all_to_all | solution.py:263
  165.4 1.3 fusion.5
  166.7 3.6 %all-to-all-start.4 = ((bf16[8,32,512]{2,1,0:T(8,128)(2,1)}), bf16[8,32,512]{2,1,0:T(8,128)(2,1)S(1)}, u32[]{:S(2)}, u32[]{:S(2)}) async-start(bf16[8,32,512]{2,1,0:T(8,128)(2,1)} %fusion.4), calls=%async_computation.4 | async-start | bytes 524288 | tf_op jit(solution)/shard_map/all_to_all | solution.py:263
  170.3 1.5 collective-permute-start.1
  171.9 7.6 %all-to-all-done.4 = bf16[8,32,512]{2,1,0:T(8,128)(2,1)S(1)} async-done(((bf16[8,32,512]{2,1,0:T(8,128)(2,1)}), bf16[8,32,512]{2,1,0:T(8,128)(2,1)S(1)}, u32[]{:S(2)}, u32[]{:S(2)}) %all-to-all-start.4) | async-done | bytes 262176 | tf_op jit(solution)/shard_map/all_to_all | solution.py:263
  179.5 1.6 collective-permute-start.3
  181.1 2.0 %add_multiply_fusion = f32[96,512]{1,0:T(8,128)} fusion(bf16[96,512]{1,0:T(8,128)(2,1)S(1)} %collective-permute-done.1, bf16[8,96,512]{2,1,0:T(8,128)(2,1)} %all-to-all-done.3), kind=kLoop, calls=%fused_computation.17 | loop fusion | flops 983040 | bytes 1081344 | tf_op jit(solution)/shard_map/mul | solution.py:270
  (71 shorter events, 14.1 us)
Async XLA Ops:
  0.6 1.2 copy-start.4
  10.8 1.0 copy-start.1
  11.9 1.0 copy-start.11
  12.9 46.3 %all-to-all-start = ((bf16[16,10,8,768]{3,2,1,0:T(8,128)(2,1)}), bf16[16,10,8,768]{3,2,1,0:T(8,128)(2,1)}, u32[]{:S(2)}, u32[]{:S(2)}) async-start(bf16[16,10,8,768]{3,2,1,0:T(8,128)(2,1)} %bitcast.4), calls=%async_computation | async-start | bytes 3932160 | tf_op jit(solution)/shard_map/all_to_all | solution.py:324
  20.3 1.7 copy-start.27
  22.2 1.2 copy-start.12
  54.6 1.0 copy-start.13
  55.6 14.3 %copy-start.28 = (s32[8,8]{1,0:T(8,128)S(1)}, s32[8,8]{1,0:T(8,128)}, u32[]{:S(2)}) copy-start(s32[8,8]{1,0:T(8,128)} %param.16) | copy-start | bytes 772
  59.2 35.9 %all-to-all-start.1 = ((bf16[16,6,8,768]{3,2,1,0:T(8,128)(2,1)}), bf16[16,6,8,768]{3,2,1,0:T(8,128)(2,1)}, u32[]{:S(2)}, u32[]{:S(2)}) async-start(bf16[16,6,8,768]{3,2,1,0:T(8,128)(2,1)} %bitcast.64), calls=%async_computation.1 | async-start | bytes 2359296 | tf_op jit(solution)/shard_map/all_to_all | solution.py:324
  83.2 1.3 copy-start.19
  84.4 1.1 copy-start.21
  95.1 10.6 %copy-start.3 = (bf16[1280,256]{1,0:T(8,128)(2,1)S(1)}, bf16[1280,256]{1,0:T(8,128)(2,1)}, u32[]{:S(2)}) copy-start(bf16[1280,256]{1,0:T(8,128)(2,1)} %copy-done.2) | copy-start | bytes 1966084
  103.0 1.1 copy-start.15
  104.0 0.9 copy-start.17
  105.7 8.7 %copy-start.22 = (bf16[1280,512]{1,0:T(8,128)(2,1)S(1)}, bf16[1280,512]{1,0:T(8,128)(2,1)}, u32[]{:S(2)}) copy-start(bf16[1280,512]{1,0:T(8,128)(2,1)} %copy-done.21) | copy-start | bytes 3932164
  106.8 32.1 %all-to-all-start.2 = ((bf16[16,128,256]{2,1,0:T(8,128)(2,1)}), bf16[16,128,256]{2,1,0:T(8,128)(2,1)}, u32[]{:S(2)}, u32[]{:S(2)}) async-start(bf16[16,128,256]{2,1,0:T(8,128)(2,1)} %pad_maximum_fusion.1), calls=%async_computation.2 | async-start | bytes 2097152 | tf_op jit(solution)/shard_map/all_to_all | solution.py:424
  114.4 1.5 copy-start.20
  115.9 1.1 copy-start.26
  117.0 11.1 %copy-start.16 = (bf16[768,768]{1,0:T(8,128)(2,1)S(1)}, bf16[768,768]{1,0:T(8,128)(2,1)}, u32[]{:S(2)}) copy-start(bf16[768,768]{1,0:T(8,128)(2,1)} %copy-done.15) | copy-start | bytes 3538948
  117.0 11.1 %copy-start.18 = (bf16[768,512]{1,0:T(8,128)(2,1)S(1)}, bf16[768,512]{1,0:T(8,128)(2,1)}, u32[]{:S(2)}) copy-start(bf16[768,512]{1,0:T(8,128)(2,1)} %copy-done.17) | copy-start | bytes 2359300
  117.0 11.1 %copy-start.24 = (bf16[256,768]{1,0:T(8,128)(2,1)S(1)}, bf16[256,768]{1,0:T(8,128)(2,1)}, u32[]{:S(2)}) copy-start(bf16[256,768]{1,0:T(8,128)(2,1)} %copy-done.23) | copy-start | bytes 1179652
  135.3 2.4 %collective-permute-start = (bf16[8,96,512]{2,1,0:T(8,128)(2,1)S(1)}, bf16[8,96,512]{2,1,0:T(8,128)(2,1)S(1)}, u32[]{:S(2)}, u32[]{:S(2)}) collective-permute-start(bf16[8,96,512]{2,1,0:T(8,128)(2,1)S(1)} %select_bitcast_fusion), channel_id=1, source_target_pairs={{0,1},{1,0},{2,3},{3,2},{4,5},{5,4},{6,7},{7,6},{8,9},{9,8},{10,11... | collective-permute-start | bytes 2359304 | tf_op jit(solution)/shard_map/ppermute | solution.py:256
  137.7 7.2 %copy-start = (bf16[1,256,8,512]{3,2,1,0:T(8,128)(2,1)S(1)}, bf16[1,256,8,512]{3,2,1,0:T(8,128)(2,1)}, u32[]{:S(2)}) copy-start(bf16[1,256,8,512]{3,2,1,0:T(8,128)(2,1)} %param.9) | copy-start | bytes 6291460
  138.9 6.0 %copy-start.10 = (f32[512]{0:T(512)S(1)}, f32[512]{0:T(512)}, u32[]{:S(2)}) copy-start(f32[512]{0:T(512)} %param.11) | copy-start | bytes 6148
  138.9 26.5 %all-to-all-start.3 = ((bf16[8,96,512]{2,1,0:T(8,128)(2,1)}), bf16[8,96,512]{2,1,0:T(8,128)(2,1)}, u32[]{:S(2)}, u32[]{:S(2)}) async-start(bf16[8,96,512]{2,1,0:T(8,128)(2,1)} %fusion), calls=%async_computation.3 | async-start | bytes 1572864 | tf_op jit(solution)/shard_map/all_to_all | solution.py:263
  144.9 1.0 copy-start.5
  145.9 1.2 copy-start.14
  147.1 7.4 %copy-start.7 = (bf16[512,256]{1,0:T(8,128)(2,1)S(1)}, bf16[512,256]{1,0:T(8,128)(2,1)}, u32[]{:S(2)}) copy-start(bf16[512,256]{1,0:T(8,128)(2,1)} %copy-done.6) | copy-start | bytes 786436
  154.6 1.6 collective-permute-start.2
  166.7 12.7 %all-to-all-start.4 = ((bf16[8,32,512]{2,1,0:T(8,128)(2,1)}), bf16[8,32,512]{2,1,0:T(8,128)(2,1)S(1)}, u32[]{:S(2)}, u32[]{:S(2)}) async-start(bf16[8,32,512]{2,1,0:T(8,128)(2,1)} %fusion.4), calls=%async_computation.4 | async-start | bytes 524288 | tf_op jit(solution)/shard_map/all_to_all | solution.py:263
  170.3 10.7 %collective-permute-start.1 = (bf16[96,512]{1,0:T(8,128)(2,1)S(1)}, bf16[96,512]{1,0:T(8,128)(2,1)S(1)}, u32[]{:S(2)}, u32[]{:S(2)}) collective-permute-start(bf16[96,512]{1,0:T(8,128)(2,1)S(1)} %fusion.5), channel_id=1, source_target_pairs={{0,16},{16,0},{1,17},{17,1},{2,18},{18,2},{3,19},{19,3},{4,20},{20... | collective-permute-start | bytes 294920 | tf_op jit(solution)/shard_map/ppermute | solution.py:266
  179.5 4.0 %collective-permute-start.3 = (bf16[32,512]{1,0:T(8,128)(2,1)S(1)}, bf16[32,512]{1,0:T(8,128)(2,1)S(1)}, u32[]{:S(2)}, u32[]{:S(2)}) collective-permute-start(bf16[32,512]{1,0:T(8,128)(2,1)S(1)} %fusion.6), channel_id=1, source_target_pairs={{0,16},{16,0},{1,17},{17,1},{2,18},{18,2},{3,19},{19,3},{4,20},{20... | collective-permute-start | bytes 98312 | tf_op jit(solution)/shard_map/ppermute | solution.py:266
  (6 other events, 4.6 us)

commit v6 on v5

--- a/solution.py
+++ b/solution.py
@@ -293,7 +293,7 @@
     w_rows = w_qkv.T
 
     step = max(1, 16 // local)
-    owned_first = owned * 5 // 8 // step * step
+    owned_first = owned * 3 // 4 // step * step
     portions = (owned_first, owned - owned_first)
     share = tuple(portion * local for portion in portions)
     normed, grad_space, send_first, send_second = pl.pallas_call(

time: 185 us -> 184 us (level)
  waiting for transfers between devices: 32.1 us -> 29.7 us
    all_to_all x2, waiting for transfers between devices: 12.3 us -> 9.94 us  [to_electrodes(): lax.all_to_all(send.reshape(groups, portion, local, width + half), 'seq',...]
    unnamed x59 -> x61, local copies, waits for them, and re-layouts: 19.8 us -> 21 us
  transfers between devices with their start and end apart: 9 -> 9, of which waited for: 7 -> 7; matrix products, arithmetic and copies ran while one was open for 4% -> 4% of each run, Pallas kernels for 37% -> 39%
where the time goes in v6:
time: 184 us; the launch traced here: 183 us
  Pallas kernels  83.4 us (45%)
  starting transfers between devices  38.6 us (21%)
  waiting for transfers between devices  29.7 us (16%)
  local copies, waits for them, and re-layouts  21.5 us (12%)
  other arithmetic  8.34 us (5%)
    pallas_call x1, Pallas kernels, shards(): pl.pallas_call(functools.partial(space_kernel, local), grid=(local,), in_...  30.4 us
    unnamed x61, local copies, waits for them, and re-layouts  21 us
    pallas_call x2, Pallas kernels, time_forward(): pl.pallas_call(functools.partial(time_forward_kernel, portion, local, dir...  20.3 us
    all_to_all x2, starting transfers between devices, to_electrodes(): lax.all_to_all(send.reshape(groups, portion, local, width + half), 'seq',...  19.7 us
    pallas_call x2, Pallas kernels, time_backward(): pl.pallas_call(functools.partial(time_backward_kernel, length), grid=(som...  17.8 us
    all_to_all x2, waiting for transfers between devices, reduce_pairs(): lax.all_to_all(both, 'seq', split_axis=0, concat_axis=0, axis_index_group...  16 us
    all_to_all x2, waiting for transfers between devices, to_electrodes(): lax.all_to_all(send.reshape(groups, portion, local, width + half), 'seq',...  9.94 us
    all_to_all x2, starting transfers between devices, reduce_pairs(): lax.all_to_all(both, 'seq', split_axis=0, concat_axis=0, axis_index_group...  9.58 us
  transfers between devices with their start and end apart: 9, of which 7 were waited for; matrix products, arithmetic and copies ran while one was open for 4% of the time, Pallas kernels for 39%

profile of v6, /device:TPU:0, one launch (start us, length us, event | category | flops | bytes accessed | tf_op | source)
XLA Modules:
  0.0 183.0 jit_solution(13079860262518257426)
XLA Ops:
  3.2 7.5 %shard_map.112 = (bf16[2048,512]{1,0:T(8,128)(2,1)S(1)}, bf16[2048,256]{1,0:T(8,128)(2,1)S(1)}, bf16[1536,768]{1,0:T(8,128)(2,1)}, bf16[512,768]{1,0:T(8,128)(2,1)}) custom-call(bf16[2048,512]{1,0:T(8,128)(2,1)} %bitcast.59, f32[2048,1]{1,0:T(8,128)S(1)} %convert_element_type.200.mask, f32[1,512]{1,0:T(1,128)S(1)} %bitcast.70, f32[1,512]{1,0:T(1,128)S(1)} %bitcast.69, ...), custom_call_target="tpu_custom_call" | custom-call | flops 1073741824 | bytes 9437184 | tf_op jit(solution)/shard_map/pallas_call | solution.py:299
  10.7 1.3 copy-done.12
  12.1 1.0 copy-done.13
  13.1 7.4 %all-to-all-start = ((bf16[16,12,8,768]{3,2,1,0:T(8,128)(2,1)}), bf16[16,12,8,768]{3,2,1,0:T(8,128)(2,1)}, u32[]{:S(2)}, u32[]{:S(2)}) async-start(bf16[16,12,8,768]{3,2,1,0:T(8,128)(2,1)} %bitcast.76), calls=%async_computation | async-start | bytes 4718592 | tf_op jit(solution)/shard_map/all_to_all | solution.py:324
  20.5 1.7 copy.20
  22.4 1.2 copy-done.14
  23.6 30.4 %shard_map.113 = (bf16[2048,256]{1,0:T(8,128)(2,1)S(1)}, bf16[768,512]{1,0:T(8,128)(2,1)S(1)}, bf16[512,256]{1,0:T(8,128)(2,1)S(1)}) custom-call(bf16[2048,512]{1,0:T(8,128)(2,1)} %copy-done.12, bf16[2048,256]{1,0:T(8,128)(2,1)S(1)} %copy-done.14, bf16[2048,512]{1,0:T(8,128)(2,1)} %bitcast.78, bf16[1536,512]{1,0:T(8,128)(2,1)S(1)} %bitcast.61, ...), custom_call_target="tpu_custom_call" | custom-call | flops 17179869184 | bytes 8388608 | tf_op jit(solution)/shard_map/pallas_call | solution.py:334
  56.7 9.5 %all-to-all-done = bf16[16,12,8,768]{3,2,1,0:T(8,128)(2,1)} async-done(((bf16[16,12,8,768]{3,2,1,0:T(8,128)(2,1)}), bf16[16,12,8,768]{3,2,1,0:T(8,128)(2,1)}, u32[]{:S(2)}, u32[]{:S(2)}) %all-to-all-start) | async-done | bytes 2359328 | tf_op jit(solution)/shard_map/all_to_all | solution.py:324
  66.2 12.3 %all-to-all-start.1 = ((bf16[16,4,8,768]{3,2,1,0:T(8,128)(2,1)}), bf16[16,4,8,768]{3,2,1,0:T(8,128)(2,1)S(1)}, u32[]{:S(2)}, u32[]{:S(2)}) async-start(bf16[16,4,8,768]{3,2,1,0:T(8,128)(2,1)} %bitcast.9), calls=%async_computation.1 | async-start | bytes 1572864 | tf_op jit(solution)/shard_map/all_to_all | solution.py:324
  78.9 15.0 %shard_map.114 = (bf16[1536,256]{1,0:T(8,128)(2,1)S(1)}, bf16[1536,512]{1,0:T(8,128)(2,1)S(1)}, bf16[256,1536]{1,0:T(8,128)(2,1)S(1)}, bf16[768,1536]{1,0:T(8,128)(2,1)}) custom-call(bf16[1536,768]{1,0:T(8,128)(2,1)} %bitcast.5.recv, bf16[1536,512]{1,0:T(8,128)(2,1)S(1)} %bitcast.62, f32[128,128]{1,0:T(8,128)S(1)} %fusion.1.allowed), custom_call_target="tpu_custom_call" | custom-call | flops 6442450944 | bytes 6291456 | tf_op jit(solution)/shard_map/pallas_call | solution.py:364
  94.7 1.1 copy-done.24
  97.2 5.3 %shard_map.115 = (bf16[512,256]{1,0:T(8,128)(2,1)S(1)}, bf16[512,512]{1,0:T(8,128)(2,1)S(1)}, bf16[256,512]{1,0:T(8,128)(2,1)S(1)}, bf16[768,512]{1,0:T(8,128)(2,1)S(1)}) custom-call(bf16[512,768]{1,0:T(8,128)(2,1)S(1)} %bitcast.64, bf16[1536,512]{1,0:T(8,128)(2,1)S(1)} %bitcast.63, f32[128,128]{1,0:T(8,128)S(1)} %fusion.1.allowed), custom_call_target="tpu_custom_call" | custom-call | flops 2147483648 | bytes 2097152 | tf_op jit(solution)/shard_map/pallas_call | solution.py:364
  105.0 1.0 pad_maximum_fusion.1
  106.0 5.8 %all-to-all-start.2 = ((bf16[16,128,256]{2,1,0:T(8,128)(2,1)}), bf16[16,128,256]{2,1,0:T(8,128)(2,1)}, u32[]{:S(2)}, u32[]{:S(2)}) async-start(bf16[16,128,256]{2,1,0:T(8,128)(2,1)} %pad_maximum_fusion.1), calls=%async_computation.2 | async-start | bytes 2097152 | tf_op jit(solution)/shard_map/all_to_all | solution.py:424
  111.9 1.7 copy-done.23
  113.5 1.4 copy-done.25
  114.9 13.3 %shard_map.116 = bf16[768,512]{1,0:T(8,128)(2,1)S(1)} custom-call(bf16[1536,512]{1,0:T(8,128)(2,1)S(1)} %copy-done.25, bf16[256,1536]{1,0:T(8,128)(2,1)S(1)} %copy-done.27, bf16[768,1536]{1,0:T(8,128)(2,1)S(1)} %copy-done.23, f32[128,128]{1,0:T(8,128)S(1)} %fusion.1.allowed), custom_call_target="tpu_custom_call" | custom-call | flops 9663676416 | bytes 6291456 | tf_op jit(solution)/shard_map/pallas_call | solution.py:393
  128.2 4.6 %shard_map.117 = bf16[768,512]{1,0:T(8,128)(2,1)S(1)} custom-call(bf16[512,512]{1,0:T(8,128)(2,1)S(1)} %copy-done.20, bf16[256,512]{1,0:T(8,128)(2,1)S(1)} %copy-done.22, bf16[768,512]{1,0:T(8,128)(2,1)S(1)} %copy-done.18, f32[128,128]{1,0:T(8,128)S(1)} %fusion.1.allowed), custom_call_target="tpu_custom_call" | custom-call | flops 3221225472 | bytes 2097152 | tf_op jit(solution)/shard_map/pallas_call | solution.py:393
  134.5 1.9 %collective-permute-done = bf16[8,96,512]{2,1,0:T(8,128)(2,1)S(1)} collective-permute-done((bf16[8,96,512]{2,1,0:T(8,128)(2,1)S(1)}, bf16[8,96,512]{2,1,0:T(8,128)(2,1)S(1)}, u32[]{:S(2)}, u32[]{:S(2)}) %collective-permute-start) | collective-permute-done | bytes 786464 | tf_op jit(solution)/shard_map/ppermute | solution.py:256
  136.5 1.2 fusion
  137.7 6.0 %all-to-all-start.3 = ((bf16[8,96,512]{2,1,0:T(8,128)(2,1)}), bf16[8,96,512]{2,1,0:T(8,128)(2,1)}, u32[]{:S(2)}, u32[]{:S(2)}) async-start(bf16[8,96,512]{2,1,0:T(8,128)(2,1)} %fusion), calls=%async_computation.3 | async-start | bytes 1572864 | tf_op jit(solution)/shard_map/all_to_all | solution.py:263
  143.7 1.0 copy-done.6
  144.8 1.2 copy-done.16
  146.0 7.4 %shard_map.118 = (bf16[2048,512]{1,0:T(8,128)(2,1)}, bf16[512,256]{1,0:T(8,128)(2,1)S(1)}) custom-call(bf16[2048,512]{1,0:T(8,128)(2,1)S(1)} %bitcast.60, f32[2048,1]{1,0:T(8,128)S(1)} %convert_element_type.200.mask, f32[1,512]{1,0:T(1,128)S(1)} %bitcast.71, bf16[2048,256]{1,0:T(8,128)(2,1)S(1)} %copy-done.16, bf16[2048,256]{1,0:T(8,128)(2,1)} %bitcast.13.time, ...), custom_call_target="tpu_custom_call" | custom-call | flops 2147483648 | bytes 8388608 | tf_op jit(solution)/shard_map/pallas_call | solution.py:432
  153.6 1.5 collective-permute-done.2
  155.9 8.4 %all-to-all-done.3 = bf16[8,96,512]{2,1,0:T(8,128)(2,1)} async-done(((bf16[8,96,512]{2,1,0:T(8,128)(2,1)}), bf16[8,96,512]{2,1,0:T(8,128)(2,1)}, u32[]{:S(2)}, u32[]{:S(2)}) %all-to-all-start.3) | async-done | bytes 786464 | tf_op jit(solution)/shard_map/all_to_all | solution.py:263
  164.3 1.3 fusion.5
  165.6 3.6 %all-to-all-start.4 = ((bf16[8,32,512]{2,1,0:T(8,128)(2,1)}), bf16[8,32,512]{2,1,0:T(8,128)(2,1)S(1)}, u32[]{:S(2)}, u32[]{:S(2)}) async-start(bf16[8,32,512]{2,1,0:T(8,128)(2,1)} %fusion.4), calls=%async_computation.4 | async-start | bytes 524288 | tf_op jit(solution)/shard_map/all_to_all | solution.py:263
  169.2 1.5 collective-permute-start.1
  170.7 7.6 %all-to-all-done.4 = bf16[8,32,512]{2,1,0:T(8,128)(2,1)S(1)} async-done(((bf16[8,32,512]{2,1,0:T(8,128)(2,1)}), bf16[8,32,512]{2,1,0:T(8,128)(2,1)S(1)}, u32[]{:S(2)}, u32[]{:S(2)}) %all-to-all-start.4) | async-done | bytes 262176 | tf_op jit(solution)/shard_map/all_to_all | solution.py:263
  178.3 1.6 collective-permute-start.3
  179.9 2.0 %add_multiply_fusion = f32[96,512]{1,0:T(8,128)} fusion(bf16[96,512]{1,0:T(8,128)(2,1)S(1)} %collective-permute-done.1, bf16[8,96,512]{2,1,0:T(8,128)(2,1)} %all-to-all-done.3), kind=kLoop, calls=%fused_computation.17 | loop fusion | flops 983040 | bytes 1081344 | tf_op jit(solution)/shard_map/mul | solution.py:270
  (73 shorter events, 14.1 us)
Async XLA Ops:
  0.6 1.2 copy-start.5
  10.7 1.3 copy-start.12
  12.1 1.0 copy-start.13
  13.1 53.1 %all-to-all-start = ((bf16[16,12,8,768]{3,2,1,0:T(8,128)(2,1)}), bf16[16,12,8,768]{3,2,1,0:T(8,128)(2,1)}, u32[]{:S(2)}, u32[]{:S(2)}) async-start(bf16[16,12,8,768]{3,2,1,0:T(8,128)(2,1)} %bitcast.76), calls=%async_computation | async-start | bytes 4718592 | tf_op jit(solution)/shard_map/all_to_all | solution.py:324
  20.5 1.7 copy-start.28
  22.4 1.2 copy-start.14
  54.0 0.9 copy-start.1
  55.7 1.0 copy-start.15
  56.7 21.8 %copy-start.29 = (s32[8,8]{1,0:T(8,128)S(1)}, s32[8,8]{1,0:T(8,128)}, u32[]{:S(2)}) copy-start(s32[8,8]{1,0:T(8,128)} %param.16) | copy-start | bytes 772
  66.2 31.0 %all-to-all-start.1 = ((bf16[16,4,8,768]{3,2,1,0:T(8,128)(2,1)}), bf16[16,4,8,768]{3,2,1,0:T(8,128)(2,1)S(1)}, u32[]{:S(2)}, u32[]{:S(2)}) async-start(bf16[16,4,8,768]{3,2,1,0:T(8,128)(2,1)} %bitcast.9), calls=%async_computation.1 | async-start | bytes 1572864 | tf_op jit(solution)/shard_map/all_to_all | solution.py:324
  94.7 1.1 copy-start.24
  95.9 0.9 copy-start.26
  97.2 7.8 %copy-start.4 = (bf16[1536,256]{1,0:T(8,128)(2,1)S(1)}, bf16[1536,256]{1,0:T(8,128)(2,1)}, u32[]{:S(2)}) copy-start(bf16[1536,256]{1,0:T(8,128)(2,1)} %copy-done.3) | copy-start | bytes 2359300
  106.0 5.8 %copy-start.27 = (bf16[256,1536]{1,0:T(8,128)(2,1)S(1)}, bf16[256,1536]{1,0:T(8,128)(2,1)}, u32[]{:S(2)}) copy-start(bf16[256,1536]{1,0:T(8,128)(2,1)} %copy-done.26) | copy-start | bytes 2359300
  106.0 31.7 %all-to-all-start.2 = ((bf16[16,128,256]{2,1,0:T(8,128)(2,1)}), bf16[16,128,256]{2,1,0:T(8,128)(2,1)}, u32[]{:S(2)}, u32[]{:S(2)}) async-start(bf16[16,128,256]{2,1,0:T(8,128)(2,1)} %pad_maximum_fusion.1), calls=%async_computation.2 | async-start | bytes 2097152 | tf_op jit(solution)/shard_map/all_to_all | solution.py:424
  111.9 1.7 copy-start.23
  113.5 1.4 copy-start.25
  114.9 13.3 %copy-start.18 = (bf16[768,512]{1,0:T(8,128)(2,1)S(1)}, bf16[768,512]{1,0:T(8,128)(2,1)}, u32[]{:S(2)}) copy-start(bf16[768,512]{1,0:T(8,128)(2,1)} %copy-done.17) | copy-start | bytes 2359300
  114.9 13.3 %copy-start.20 = (bf16[512,512]{1,0:T(8,128)(2,1)S(1)}, bf16[512,512]{1,0:T(8,128)(2,1)}, u32[]{:S(2)}) copy-start(bf16[512,512]{1,0:T(8,128)(2,1)} %copy-done.19) | copy-start | bytes 1572868
  114.9 13.3 %copy-start.22 = (bf16[256,512]{1,0:T(8,128)(2,1)S(1)}, bf16[256,512]{1,0:T(8,128)(2,1)}, u32[]{:S(2)}) copy-start(bf16[256,512]{1,0:T(8,128)(2,1)} %copy-done.21) | copy-start | bytes 786436
  132.8 1.1 copy-start.2
  134.1 2.4 %collective-permute-start = (bf16[8,96,512]{2,1,0:T(8,128)(2,1)S(1)}, bf16[8,96,512]{2,1,0:T(8,128)(2,1)S(1)}, u32[]{:S(2)}, u32[]{:S(2)}) collective-permute-start(bf16[8,96,512]{2,1,0:T(8,128)(2,1)S(1)} %select_bitcast_fusion), channel_id=1, source_target_pairs={{0,1},{1,0},{2,3},{3,2},{4,5},{5,4},{6,7},{7,6},{8,9},{9,8},{10,11... | collective-permute-start | bytes 2359304 | tf_op jit(solution)/shard_map/ppermute | solution.py:256
  136.5 7.2 %copy-start = (bf16[1,256,8,512]{3,2,1,0:T(8,128)(2,1)S(1)}, bf16[1,256,8,512]{3,2,1,0:T(8,128)(2,1)}, u32[]{:S(2)}) copy-start(bf16[1,256,8,512]{3,2,1,0:T(8,128)(2,1)} %param.9) | copy-start | bytes 6291460
  137.7 6.0 %copy-start.11 = (f32[512]{0:T(512)S(1)}, f32[512]{0:T(512)}, u32[]{:S(2)}) copy-start(f32[512]{0:T(512)} %param.11) | copy-start | bytes 6148
  137.7 26.5 %all-to-all-start.3 = ((bf16[8,96,512]{2,1,0:T(8,128)(2,1)}), bf16[8,96,512]{2,1,0:T(8,128)(2,1)}, u32[]{:S(2)}, u32[]{:S(2)}) async-start(bf16[8,96,512]{2,1,0:T(8,128)(2,1)} %fusion), calls=%async_computation.3 | async-start | bytes 1572864 | tf_op jit(solution)/shard_map/all_to_all | solution.py:263
  143.7 1.0 copy-start.6
  144.8 1.2 copy-start.16
  146.0 7.4 %copy-start.8 = (bf16[512,256]{1,0:T(8,128)(2,1)S(1)}, bf16[512,256]{1,0:T(8,128)(2,1)}, u32[]{:S(2)}) copy-start(bf16[512,256]{1,0:T(8,128)(2,1)} %copy-done.7) | copy-start | bytes 786436
  153.5 1.6 collective-permute-start.2
  165.6 12.7 %all-to-all-start.4 = ((bf16[8,32,512]{2,1,0:T(8,128)(2,1)}), bf16[8,32,512]{2,1,0:T(8,128)(2,1)S(1)}, u32[]{:S(2)}, u32[]{:S(2)}) async-start(bf16[8,32,512]{2,1,0:T(8,128)(2,1)} %fusion.4), calls=%async_computation.4 | async-start | bytes 524288 | tf_op jit(solution)/shard_map/all_to_all | solution.py:263
  169.2 10.7 %collective-permute-start.1 = (bf16[96,512]{1,0:T(8,128)(2,1)S(1)}, bf16[96,512]{1,0:T(8,128)(2,1)S(1)}, u32[]{:S(2)}, u32[]{:S(2)}) collective-permute-start(bf16[96,512]{1,0:T(8,128)(2,1)S(1)} %fusion.5), channel_id=1, source_target_pairs={{0,16},{16,0},{1,17},{17,1},{2,18},{18,2},{3,19},{19,3},{4,20},{20... | collective-permute-start | bytes 294920 | tf_op jit(solution)/shard_map/ppermute | solution.py:266
  178.3 4.0 %collective-permute-start.3 = (bf16[32,512]{1,0:T(8,128)(2,1)S(1)}, bf16[32,512]{1,0:T(8,128)(2,1)S(1)}, u32[]{:S(2)}, u32[]{:S(2)}) collective-permute-start(bf16[32,512]{1,0:T(8,128)(2,1)S(1)} %fusion.6), channel_id=1, source_target_pairs={{0,16},{16,0},{1,17},{17,1},{2,18},{18,2},{3,19},{19,3},{4,20},{20... | collective-permute-start | bytes 98312 | tf_op jit(solution)/shard_map/ppermute | solution.py:266
  (7 other events, 5.4 us)
